TPU v7x, 32 devices: a whole 2x2x4 slice. The times are simulated.
32 devices in a mesh: dp: 16 (over z, y, x), tensor: 2 (over core).
Axes of the slice: x: 2, y: 2, z: 4, core: 2. Of those that a mesh axis runs over, the one named last changes fastest.
Arguments:
- latents: bfloat16 [4160, 1536], P(('dp', 'tensor')), may hold values from -6 to 6
- context: bfloat16 [8192, 1536], P('dp'), may hold values from -6 to 6
- cotangent: bfloat16 [4160, 1536], P(('dp', 'tensor')), may hold values from -6 to 6
- positions: int32 [3, 4160], P(None, 'dp'), may hold values from 0 to 63
- step_ids: int32 [16], P('dp'), may hold values from 0 to 15
- owners: int32 [118], replicated, may hold values from 0 to 15, as said below
- time_table: float32 [16, 6, 1536], replicated, may hold values from -3 to 3
- master: float32 [2, 144, 1536, 128], P('tensor', 'dp'), may hold values from -6 to 6
- first_moment: float32 [2, 144, 1536, 128], P('tensor', 'dp'), as said below
- second_moment: float32 [2, 144, 1536, 128], P('tensor', 'dp'), as said below
- head_params: float32 [2, 12160], P('tensor'), as said below
- head_first: float32 [2, 12160], P('tensor'), may hold values from -20 to 20
- head_second: float32 [2, 12160], P('tensor'), may hold values from 0.52 to 8.32
- shared_params: float32 [11, 1536], replicated, as said below
- shared_first: float32 [11, 1536], replicated, may hold values from -20 to 20
- shared_second: float32 [11, 1536], replicated, may hold values from 0.52 to 8.32
Outputs:
- block_out: bfloat16 [4160, 1536], P(('dp', 'tensor'))
- grad_latents: float32 [4160, 1536], P(('dp', 'tensor'))
- new_master: float32 [2, 144, 1536, 128], P('tensor', 'dp')
- new_first: float32 [2, 144, 1536, 128], P('tensor', 'dp')
- new_second: float32 [2, 144, 1536, 128], P('tensor', 'dp')
- new_head: float32 [2, 12160], P('tensor')
- new_head_first: float32 [2, 12160], P('tensor')
- new_head_second: float32 [2, 12160], P('tensor')
- new_shared: float32 [11, 1536], replicated
- new_shared_first: float32 [11, 1536], replicated
- new_shared_second: float32 [11, 1536], replicated
Inputs may be any that keep to these rules, and one draw needn't show every extreme that they name: `owners`: no owner holds more than 9 blocks, and some owner holds exactly 9. `first_moment`: entries are finite, of both signs. `second_moment`: entries are positive. `head_params`: the gains among them are positive. `shared_params`: the norm gain row is positive.
All inputs are finite; a program needn't handle non-finite values.
Results may differ from a plain program's by a relative error of at most 0.014.
Values may be sent and summed in bfloat16 or wider, within the bound.
A program may use at most 512 MiB of HBM per device.

v0:
```python
import functools

import jax
import jax.numpy as jnp
from jax import lax
from jax.experimental import pallas as pl
from jax.experimental.pallas import tpu as pltpu
from jax.sharding import PartitionSpec as P

D = 1536
HEADS = 12
HEAD = 128
FF = 8960
TSTEPS = 16
STEPC = 10


NORM_EPS = 1e-06
BETA_ONE = 0.9
BETA_TWO = 0.999
ADAM_EPS = 1e-08
TILE_RATE = 1.0
TILE_DECAY = 0.1
VECTOR_RATE = 0.5
GELU_COEF = 0.7978845608028654


def rope_tables(token_places, head_size):
    sixths = head_size // 6
    frame_pairs = (head_size - 4 * sixths) // 2
    frame_freq = 10000.0 ** (-jnp.arange(frame_pairs, dtype=jnp.float32) / frame_pairs)
    side_freq = 10000.0 ** (-jnp.arange(sixths, dtype=jnp.float32) / sixths)
    spots = token_places.astype(jnp.float32)
    angles = jnp.concatenate(
        [
            spots[0][..., None] * frame_freq,
            spots[1][..., None] * side_freq,
            spots[2][..., None] * side_freq,
        ],
        -1,
    )
    angles = jnp.repeat(angles, 2, axis=-1)
    return (jnp.cos(angles), jnp.sin(angles))


def owner_layout(owners, slot_count, devices):
    indices = jnp.arange(owners.shape[0], dtype=jnp.int32)
    same_owner = (owners[:, None] == owners[None, :]) & (indices[None, :] < indices[:, None])
    slot_of = jnp.sum(same_owner.astype(jnp.int32), axis=1)
    places = owners * slot_count + slot_of
    spots = jnp.arange(slot_count * devices, dtype=jnp.int32)
    holder = (
        jnp.sum(jnp.where(places[None, :] == spots[:, None], indices[None, :] + 1, 0), axis=1) - 1
    )
    return (places, holder)


def tile_scales(tile_count, heads_here, blocks_here):
    indices = jnp.arange(tile_count)
    scale_in = D ** (-0.5)
    scale_out = HEADS ** (-0.5)
    scale_down = FF ** (-0.5)
    scales = jnp.where(
        indices < 3 * heads_here,
        scale_in,
        jnp.where(
            indices < 4 * heads_here,
            scale_out,
            jnp.where(
                indices < 7 * heads_here,
                scale_in,
                jnp.where(
                    indices < 8 * heads_here,
                    scale_out,
                    jnp.where(indices < 8 * heads_here + blocks_here, scale_in, scale_down),
                ),
            ),
        ),
    )
    return scales.astype(jnp.float32)


def adam_step(weight, gradient, moment_one, moment_two, step_rate, decay_rate):
    first_new = BETA_ONE * moment_one + (1.0 - BETA_ONE) * gradient
    second_new = BETA_TWO * moment_two + (1.0 - BETA_TWO) * gradient * gradient
    first_hat = first_new / (1.0 - BETA_ONE**STEPC)
    second_hat = second_new / (1.0 - BETA_TWO**STEPC)
    weight_new = weight - step_rate * (
        first_hat / (jnp.sqrt(second_hat) + ADAM_EPS) + decay_rate * weight
    )
    return (weight_new, first_new, second_new)


MESH = pl.DeviceIdType.MESH
ANY = pl.BlockSpec(memory_space=pl.ANY)
MIB = 1 << 20


def chip_pairs():
    return lax.axis_size("dp") == 16 and lax.axis_size("tensor") == 2


def pair_rank():
    if chip_pairs():
        return (lax.axis_index("dp") // 4) % 2
    return lax.axis_index("tensor")


def pair_swap(value):
    if chip_pairs():
        return lax.ppermute(value, "dp", [(i, i ^ 4) for i in range(16)])
    return lax.ppermute(value, "tensor", [(0, 1), (1, 0)])


def pair_sums(*values):
    stacked = jnp.concatenate([v.reshape(-1) for v in values])
    total = stacked + pair_swap(stacked)
    out, at = [], 0
    for v in values:
        out.append(total[at : at + v.size].reshape(v.shape))
        at += v.size
    return tuple(out)


def place_of():
    chip, core = lax.axis_index("dp"), lax.axis_index("tensor")
    z, y, x = chip // 4, (chip // 2) % 2, chip % 2
    return chip, core, z, y, x


def column_of(z, y, x, k):
    high, low_bit = z // 2, z % 2
    if k & 2:
        high = 1 - high
    if k & 1:
        low_bit = 1 - low_bit
    return (2 * high + low_bit) * 4 + 2 * y + x


def greet(chip, core, z, y, x):
    barrier = pltpu.get_barrier_semaphore()
    friends = []
    for k in range(4):
        for flip in (0, 1):
            if k or flip:
                friends.append((column_of(z, y, x, k), core if flip == 0 else 1 - core))
    friends.append((column_of(z, y, 1 - x, 0), core))
    friends.append((column_of(z, 1 - y, x, 0), core))
    for friend in friends:
        pl.semaphore_signal(barrier, inc=1, device_id=friend, device_id_type=MESH)
    pl.semaphore_wait(barrier, len(friends))


def gather_kernel(
    own, lat, cot, text, small, out, lats, cots, texts, smalls, clip_s, clip_r,
    near_s, col_r, x_s, x_r, y_s, y_r, sib_s, sib_r,
):
    chip, core, z, y, x = place_of()
    rank = z % 2
    half = own.shape[1] // 2
    part = half // 2
    at_x = column_of(z, y, 1 - x, 0)
    at_y = column_of(z, 1 - y, x, 0)
    greet(chip, core, z, y, x)

    batch = max(n for n in (1, 2, 3) if own.shape[0] % n == 0)
    batches = own.shape[0] // batch
    turns = 4 * batches

    def case(s):
        late = jnp.maximum(s - batches, 0)
        k = jnp.where(s < batches, 0, 1 + late % 3)
        return k, jnp.where(s < batches, s, late // 3)

    def remote(unit, g, first, count, send, recv, device):
        piece = out.at[
            unit, pl.ds(g * batch, batch), pl.ds(pl.multiple_of(first, 16), count), :
        ]
        return pltpu.make_async_remote_copy(
            src_ref=piece, dst_ref=piece, send_sem=send, recv_sem=recv,
            device_id=device, device_id_type=MESH,
        )

    def own_copy(g, j, h):
        target = (toggled(z, y, x, 0, 0, 2 * j) // 8 * 8) + core * 4 + 2 * y + x
        part_of = (pl.ds(g * batch, batch), pl.ds(h * half, half))
        src = own.at[part_of[0], part_of[1], :]
        dst = out.at[chip, part_of[0], part_of[1], :]
        recv = col_r.at[z * batches + g]
        go = pltpu.make_async_remote_copy(
            src_ref=src, dst_ref=dst, send_sem=near_s.at[(2 * j + h) * batches + g],
            recv_sem=recv, device_id=(target, h), device_id_type=MESH,
        )
        return go, pltpu.make_async_copy(src, dst, recv)

    for g in range(batches):
        for j in range(2):
            for h in range(2):
                go, here = own_copy(g, j, h)
                if j == 1:
                    go.start()
                    continue
                stays = jnp.logical_and(rank == core, core == h)

                @pl.when(stays)
                def _():
                    here.start()

                @pl.when(jnp.logical_not(stays))
                def _():
                    go.start()

    pair_chip = column_of(z, y, x, 1)
    rows_of_text = text.shape[0] // 2

    def clip_pieces(h):
        share = pl.ds(h * rows_of_text, rows_of_text)
        return ((lat, lats.at[h]), (cot, cots.at[h]), (text.at[share], texts.at[share]))

    home = rank == core
    trade = pltpu.make_async_remote_copy(
        src_ref=small, dst_ref=smalls, send_sem=clip_s.at[6], recv_sem=clip_r.at[6],
        device_id=(pair_chip, 1 - core), device_id_type=MESH,
    )
    keep = pltpu.make_async_copy(small, smalls, clip_r.at[6])

    @pl.when(home)
    def _():
        keep.start()

    @pl.when(jnp.logical_not(home))
    def _():
        trade.start()

    def hand_out(h, n, wait):
        src, dst = clip_pieces(h)[n]
        far = pltpu.make_async_remote_copy(
            src_ref=src, dst_ref=dst, send_sem=clip_s.at[n], recv_sem=clip_r.at[3 * h + n],
            device_id=(pair_chip, rank), device_id_type=MESH,
        )
        near = pltpu.make_async_remote_copy(
            src_ref=src, dst_ref=dst, send_sem=clip_s.at[3 + n], recv_sem=clip_r.at[3 * h + n],
            device_id=(chip, 1 - core), device_id_type=MESH,
        )
        here = pltpu.make_async_copy(src, dst, clip_r.at[3 * h + n])

        @pl.when(core == h)
        def _():
            if wait:
                far.wait_send()
            else:
                far.start()

            @pl.when(home)
            def _():
                if not wait:
                    here.start()

            @pl.when(jnp.logical_not(home))
            def _():
                if wait:
                    near.wait_send()
                else:
                    near.start()

    for n in range(3):
        for h in range(2):
            hand_out(h, n, False)

    mine, other = core * half, (1 - core) * half
    sibling = (chip, 1 - core)

    def to_x(s, n):
        k, g = case(s)
        i = turns * n + s
        unit = toggled(z, y, x, n, 0, k)
        return remote(unit, g, mine, part if n else half, x_s.at[i], x_r.at[i], (at_x, core))

    def from_x(s, n):
        k, g = case(s)
        i = turns * n + s
        unit = toggled(z, y, x, n, 1, k)
        return remote(unit, g, mine, part if n else half, x_s.at[i], x_r.at[i], (at_x, core))

    def to_y(s, n):
        k, g = case(s)
        i = turns * n + s
        unit = toggled(z, y, x, 0, n, k)
        first, count = (mine + part, part) if n else (mine, half)
        return remote(unit, g, first, count, y_s.at[i], y_r.at[i], (at_y, core))

    def from_y(s, n):
        k, g = case(s)
        i = turns * n + s
        unit = toggled(z, y, x, 1, n, k)
        first, count = (mine + part, part) if n else (mine, half)
        return remote(unit, g, first, count, y_s.at[i], y_r.at[i], (at_y, core))

    def to_sib(s, n, away=False):
        k, g = case(s)
        i = turns * n + s
        unit = toggled(z, y, x, int(n in (2, 3, 4)), int(n in (1, 3, 4)), k)
        first = (other if away else mine) + (part if n == 4 else 0)
        return remote(
            unit, g, first, part if n >= 3 else half, sib_s.at[i], sib_r.at[i], sibling
        )

    def column_in(s):
        k, g = case(s)
        unit = toggled(z, y, x, 0, 0, k)
        piece = out.at[
            unit, pl.ds(g * batch, batch), pl.ds(pl.multiple_of(mine, 16), half), :
        ]
        pltpu.make_async_copy(piece, piece, col_r.at[unit // 4 * batches + g]).wait()
        to_x(s, 0).start()
        to_y(s, 0).start()
        to_sib(s, 0).start()

    def side_in(s):
        from_x(s, 0).wait_recv()
        to_y(s, 1).start()
        to_sib(s, 1).start()
        from_y(s, 0).wait_recv()
        to_x(s, 1).start()
        to_sib(s, 2).start()

    def corner_in(s):
        from_x(s, 1).wait_recv()
        to_sib(s, 3).start()
        from_y(s, 1).wait_recv()
        to_sib(s, 4).start()

    def turn(step, carry):
        @pl.when(step < turns)
        def _():
            column_in(step)

        @pl.when(jnp.logical_and(step >= 1, step < turns + 1))
        def _():
            side_in(step - 1)

        @pl.when(step >= 2)
        def _():
            corner_in(step - 2)

        return carry

    lax.fori_loop(0, turns + 2, turn, 0)

    def settle(s, carry):
        for n in range(2):
            to_x(s, n).wait_send()
            to_y(s, n).wait_send()
        for n in range(5):
            to_sib(s, n).wait_send()
            to_sib(s, n, True).wait_recv()
        return carry

    lax.fori_loop(0, turns, settle, 0)
    for g in range(batches):
        for j in range(2):
            for h in range(2):
                go, _ = own_copy(g, j, h)
                if j == 1:
                    go.wait_send()
                    continue

                @pl.when(jnp.logical_not(jnp.logical_and(rank == core, core == h)))
                def _():
                    go.wait_send()

    for n in range(3):
        for h in range(2):
            hand_out(h, n, True)
            dst = clip_pieces(h)[n][1]
            pltpu.make_async_copy(dst, dst, clip_r.at[3 * h + n]).wait()

    @pl.when(jnp.logical_not(home))
    def _():
        trade.wait_send()

    pltpu.make_async_copy(smalls, smalls, clip_r.at[6]).wait()


def gather_slots(scaled, lat, cot, text, small):
    if not chip_pairs():
        everyone = lax.all_gather(scaled, "dp", axis=0, tiled=True)
        lats, cots = (lax.all_gather(v, "tensor") for v in (lat, cot))
        return everyone, lats, cots, text, small
    dma = pltpu.SemaphoreType.DMA
    turns = 4 * scaled.shape[0] // max(n for n in (1, 2, 3) if scaled.shape[0] % n == 0)
    counts = (7, 7, turns, turns) + (2 * turns,) * 4 + (5 * turns,) * 2
    everyone, *rest = pl.pallas_call(
        gather_kernel,
        out_shape=[
            jax.ShapeDtypeStruct((16,) + scaled.shape, scaled.dtype),
            jax.ShapeDtypeStruct((2,) + lat.shape, lat.dtype),
            jax.ShapeDtypeStruct((2,) + cot.shape, cot.dtype),
            jax.ShapeDtypeStruct(text.shape, text.dtype),
            jax.ShapeDtypeStruct(small.shape, small.dtype),
        ],
        in_specs=[ANY] * 5,
        out_specs=[ANY] * 5,
        scratch_shapes=[dma((n,)) for n in counts],
        compiler_params=pltpu.CompilerParams(
            collective_id=0, has_side_effects=True, vmem_limit_bytes=4 * MIB
        ),
    )(scaled, lat, cot, text, small)
    return everyone.reshape((-1,) + scaled.shape[1:]), *rest


def toggled(z, y, x, flip_y, flip_x, k):
    high = (z // 2 + k // 2) % 2
    low_bit = (z % 2 + k % 2) % 2
    return (2 * high + low_bit) * 4 + 2 * ((y + flip_y) % 2) + (x + flip_x) % 2


def reduce_kernel(
    kind, block, *refs,
):
    (
        *pieces, rows_in, after_in, dx_in, y_in, da_in, gains, vec_in,
        final, vec_out, result, result_grad, y_other, da_other, from_sib, from_x, from_y, corner_a, corner_b,
        left, right, ring, corners, side_x, side_y, middle, stage, vec_box,
        load_s, stage_s, sib_s, sib_r, x_s, x_r, y_s, y_r, ca_s, ca_r, cb_s, cb_r, f_s, f_r, v_s, v_r,
        end_s, end_r,
    ) = refs
    chip, core, z, y, x = place_of()
    rank = z % 2
    slots, width, lanes = final.shape[1:]
    half = width // 2
    part = half // 2
    at_x = toggled(z, y, x, 0, 1, 0)
    at_y = toggled(z, y, x, 1, 0, 0)
    sibling = (chip, 1 - core)
    mates = (
        sibling,
        (at_x, core),
        (at_y, core),
        (toggled(z, y, x, 0, 0, 1), core),
        (toggled(z, y, x, 0, 0, 2), core),
    )

    kinds = left.shape[0]
    depth = right.shape[1]
    loads = [
        pltpu.make_async_copy(pieces[i], left.at[i], load_s.at[i]) for i in range(kinds)
    ]
    first = 0
    blank = []
    for i, piece in enumerate(pieces[kinds:]):
        number, rows = piece.shape[:2]
        loads.append(
            pltpu.make_async_copy(
                piece, right.at[pl.ds(first, number), pl.ds(0, rows), :], load_s.at[kinds + i]
            )
        )
        if rows < depth:
            blank.append((first, number, rows))
        first += number
    for load in loads:
        load.start()
    for start, number, rows in blank:

        def clear(i, carry):
            right[start + i, pl.ds(rows, depth - rows), :] = jnp.zeros(
                (depth - rows, lanes), right.dtype
            )
            return carry

        lax.fori_loop(0, number, clear, 0)
    right[first] = jnp.zeros((depth, lanes), right.dtype)
    vec_out[...] = vec_in[...]
    greet(chip, core, z, y, x)
    for load in loads:
        load.wait()

    def remote(src, dst, send, recv, device):
        return pltpu.make_async_remote_copy(
            src_ref=src, dst_ref=dst, send_sem=send, recv_sem=recv,
            device_id=device, device_id_type=MESH,
        )

    batch = ring.shape[1]
    batches = slots // batch
    turns = 4 * batches
    deep = corners.shape[0]

    def flips(s):
        return 3 - s // batches

    def sums(q, s, first, terms, total):
        unit = toggled(z, y, x, 1 - q % 2, 1 - q // 2, flips(s))
        base = unit * slots + (s % batches) * batch
        count = total.shape[1]

        def one(i, carry):
            slot = base + i
            rows = pl.ds(pl.multiple_of(first, 128), count)
            acc = jnp.dot(
                left[kind[slot], rows, :], right[block[slot]], preferred_element_type=jnp.float32
            )
            for term in terms:
                acc = acc + term[i].astype(jnp.float32)
            total[i] = acc.astype(total.dtype)
            return carry

        lax.fori_loop(0, batch, one, 0)

    mine, other = core * half, (1 - core) * half

    def sub(ref, first):
        return ref.at[:, pl.ds(first, part), :]

    def sib_copy(q, s):
        i = turns * q + s
        return remote(ring.at[q], from_sib.at[i], sib_s.at[i], sib_r.at[i], sibling)

    def a_copy(s):
        return remote(
            sub(corners.at[s % deep], 0), corner_a.at[s], ca_s.at[s], ca_r.at[s], (at_x, core)
        )

    def b_copy(s):
        return remote(
            sub(corners.at[s % deep], part), corner_b.at[s], cb_s.at[s], cb_r.at[s], (at_y, core)
        )

    def x_copy(s, n):
        rows = pl.ds(n * part, part)
        i = turns * n + s
        return remote(
            side_x.at[s % deep, :, rows, :], from_x.at[s, :, rows, :], x_s.at[i], x_r.at[i],
            (at_x, core),
        )

    def y_copy(s, n):
        rows = pl.ds((1 - n) * part, part)
        i = turns * n + s
        return remote(
            side_y.at[s % deep, :, rows, :], from_y.at[s, :, rows, :], y_s.at[i], y_r.at[i],
            (at_y, core),
        )

    def f_copy(s):
        src = middle.at[s % deep]
        g = s % batches
        dst = final.at[
            z // 2, pl.ds(g * batch, batch), pl.ds(pl.multiple_of(mine, 128), half), :
        ]
        recv = f_r.at[(2 * (z // 2) + core) * batches + g]
        target = (toggled(z, y, x, 0, 0, flips(s)), rank)
        return remote(src, dst, f_s.at[s], recv, target), pltpu.make_async_copy(src, dst, recv)

    def stays(s):
        return jnp.logical_and(s >= turns - batches, rank == core)

    def staged(source, place, i):
        copy = pltpu.make_async_copy(source, place, stage_s.at[i])
        copy.start()
        return copy

    def for_sibling(s):
        def one(q, carry):
            @pl.when(s >= 1)
            def _():
                sib_copy(q, s - 1).wait_send()

            sums(q, s, other, (), ring.at[q])
            sib_copy(q, s).start()
            return carry

        lax.fori_loop(0, 4, one, 0)

    def corner(s):
        sib_copy(0, s).wait_recv()
        in_sib = staged(from_sib.at[s], stage.at[0], 0)

        @pl.when(s >= deep)
        def _():
            a_copy(s - deep).wait_send()
            b_copy(s - deep).wait_send()

        in_sib.wait()
        sums(0, s, mine, (stage.at[0],), corners.at[s % deep])
        a_copy(s).start()
        b_copy(s).start()

    def direct_sides(s):
        sib_copy(1, s).wait_recv()
        in_x = staged(from_sib.at[turns + s], stage.at[0], 0)
        sib_copy(2, s).wait_recv()
        in_y = staged(from_sib.at[2 * turns + s], stage.at[1], 1)

        @pl.when(s >= deep)
        def _():
            for n in range(2):
                x_copy(s - deep, n).wait_send()
                y_copy(s - deep, n).wait_send()

        in_x.wait()
        sums(1, s, mine, (sub(stage.at[0], 0),), sub(side_x.at[s % deep], 0))
        x_copy(s, 0).start()
        in_y.wait()
        sums(2, s, mine + part, (sub(stage.at[1], part),), sub(side_y.at[s % deep], part))
        y_copy(s, 0).start()

    def relayed_sides(s):
        b_copy(s).wait_recv()
        in_b = staged(corner_b.at[s], sub(stage.at[2], 0), 2)
        a_copy(s).wait_recv()
        in_a = staged(corner_a.at[s], sub(stage.at[2], part), 3)
        in_b.wait()
        sums(
            1, s, mine + part, (sub(stage.at[0], part), sub(stage.at[2], 0)),
            sub(side_x.at[s % deep], part),
        )
        x_copy(s, 1).start()
        in_a.wait()
        sums(
            2, s, mine, (sub(stage.at[1], 0), sub(stage.at[2], part)), sub(side_y.at[s % deep], 0)
        )
        y_copy(s, 1).start()

    def centre(s):
        sib_copy(3, s).wait_recv()
        in_sib = staged(from_sib.at[3 * turns + s], stage.at[3], 4)
        x_copy(s, 0).wait_recv()
        x_copy(s, 1).wait_recv()
        in_x = staged(from_x.at[s], stage.at[4], 5)
        y_copy(s, 0).wait_recv()
        y_copy(s, 1).wait_recv()
        in_y = staged(from_y.at[s], stage.at[5], 6)

        @pl.when(s >= deep)
        def _():
            f_copy(s - deep)[0].wait_send()

        in_sib.wait()
        in_x.wait()
        in_y.wait()
        sums(3, s, mine, (stage.at[3], stage.at[4], stage.at[5]), middle.at[s % deep])
        go, here = f_copy(s)

        @pl.when(stays(s))
        def _():
            here.start()

        @pl.when(jnp.logical_not(stays(s)))
        def _():
            go.start()

    home = rank == core
    pair_device = (toggled(z, y, x, 0, 0, 1), core)
    ends = [
        remote(y_in, y_other, end_s.at[0], end_r.at[0], pair_device),
        remote(da_in, da_other, end_s.at[1], end_r.at[1], pair_device),
        remote(result, result, end_s.at[2], end_r.at[2], sibling),
        remote(result_grad, result_grad, end_s.at[3], end_r.at[3], sibling),
    ]

    def finish_rows():
        ends[0].wait_recv()
        ends[1].wait_recv()
        tall = 16
        spec = pl.BlockSpec((tall, width), lambda i: (i, 0))

        def one(x_ref, x2_ref, dx_ref, y_ref, yo_ref, da_ref, dao_ref, out_ref, grad_ref):
            y_all = y_ref[...].astype(F32) + yo_ref[...].astype(F32) + gains[2:3]
            out_ref[...] = (x2_ref[...] + gains[0:1] * y_all).astype(out_ref.dtype)
            da = da_ref[...].astype(F32) + dao_ref[...].astype(F32)
            back, _ = normed_back(x_ref[...], da * (1.0 + gains[1:2]))
            grad_ref[...] = dx_ref[...] + back

        pltpu.emit_pipeline(
            one, grid=(rows_in.shape[0] // tall,), in_specs=[spec] * 7, out_specs=[spec] * 2
        )(rows_in, after_in, dx_in, y_in, y_other, da_in, da_other, result, result_grad)
        ends[2].start()
        ends[3].start()

    @pl.when(jnp.logical_not(home))
    def _():
        ends[0].start()
        ends[1].start()

    def vec_copy(i):
        return remote(vec_out, vec_box.at[i], v_s.at[i], v_r.at[i], mates[i])

    def turn(step, carry):
        for i in range(5):

            @pl.when(step == i)
            def _():
                vec_copy(i).start()

        @pl.when(step < turns)
        def _():
            corner(step)
            direct_sides(step)

        @pl.when(step + 1 < turns)
        def _():
            for_sibling(step + 1)

        @pl.when(step >= 1)
        def _():
            centre(step - 1)

        @pl.when(step < turns)
        def _():
            relayed_sides(step)

        @pl.when(jnp.logical_and(step == turns - batches, home))
        def _():
            finish_rows()

        for i in range(5):

            @pl.when(step == i)
            def _():
                vec_copy(i).wait()
                vec_out[...] = vec_out[...] + vec_box[i]

        return carry

    for_sibling(0)
    lax.fori_loop(0, turns + 1, turn, 0)
    for q in range(4):
        sib_copy(q, turns - 1).wait_send()

    def settle(i, carry):
        s = turns - deep + i
        a_copy(s).wait_send()
        b_copy(s).wait_send()
        for n in range(2):
            x_copy(s, n).wait_send()
            y_copy(s, n).wait_send()

        @pl.when(jnp.logical_not(stays(s)))
        def _():
            f_copy(s)[0].wait_send()

        return carry

    lax.fori_loop(0, deep, settle, 0)

    @pl.when(home)
    def _():
        ends[2].wait_send()
        ends[3].wait_send()

    @pl.when(jnp.logical_not(home))
    def _():
        ends[0].wait_send()
        ends[1].wait_send()
        ends[2].wait_recv()
        ends[3].wait_recv()

    for plane in range(2):
        for h in range(2):
            for g in range(batches):
                piece = final.at[plane, pl.ds(g * batch, batch), pl.ds(h * half, half), :]
                recv = f_r.at[(2 * plane + h) * batches + g]
                pltpu.make_async_copy(piece, piece, recv).wait()


def reduce_slots(holder, kinds, rows, columns, vector, ends, gains, slot_count):
    if not chip_pairs():
        grads = slot_grads(holder, kinds, [r.T for r in rows], columns)
        total = lax.psum_scatter(grads, "dp", scatter_dimension=0, tiled=True)
        x, after, dx, y_part, da_part = ends
        y_all, da_all = (
            v.astype(F32) + pair_swap(v).astype(F32) for v in (y_part, da_part)
        )
        result = (after + gains[0] * (y_all + gains[2])).astype(BF16)
        back, _ = normed_back(x, da_all * (1.0 + gains[1]))
        return total[None], lax.psum(vector, ("dp", "tensor")), result, dx + back
    left = rows
    width, depth = left[0].shape
    lanes = columns[0].shape[2]
    tiles = sum(c.shape[0] for c in columns)
    block = jnp.where(holder >= 0, holder, tiles)
    kind = kinds[jnp.maximum(holder, 0)]
    half = width // 2
    dma = pltpu.SemaphoreType.DMA
    scalars = pl.BlockSpec(memory_space=pltpu.SMEM)
    inside = pl.BlockSpec(memory_space=pltpu.VMEM)
    low = jnp.bfloat16

    batch = max(n for n in (1, 2, 3) if slot_count % n == 0)
    turns = 4 * slot_count // batch
    deep = 3

    def room(count, tall):
        return jax.ShapeDtypeStruct((count, batch, tall, lanes), low)

    def slab(count):
        return pltpu.VMEM((count, batch, half, lanes), low)

    outs = pl.pallas_call(
        reduce_kernel,
        out_shape=[
            jax.ShapeDtypeStruct((2, slot_count, width, lanes), low),
            jax.ShapeDtypeStruct(vector.shape, vector.dtype),
            jax.ShapeDtypeStruct(ends[0].shape, low), jax.ShapeDtypeStruct(ends[0].shape, F32),
            jax.ShapeDtypeStruct(ends[0].shape, low), jax.ShapeDtypeStruct(ends[0].shape, low),
            room(4 * turns, half), room(turns, half), room(turns, half),
            room(turns, half // 2), room(turns, half // 2),
        ],
        in_specs=[scalars, scalars] + [ANY] * (len(left) + len(columns) + 5) + [inside] * 2,
        out_specs=[ANY, inside] + [ANY] * 9,
        scratch_shapes=[
            pltpu.VMEM((len(left), width, depth), low),
            pltpu.VMEM((tiles + 1, depth, lanes), low),
            slab(4), slab(deep), slab(deep), slab(deep), slab(deep), slab(6),
            pltpu.VMEM((5,) + vector.shape, vector.dtype),
        ]
        + [
            dma((n,))
            for n in (len(left) + len(columns), 7)
            + (4 * turns,) * 2
            + (2 * turns,) * 4
            + (turns,) * 6
            + (5, 5, 4, 4)
        ],
        compiler_params=pltpu.CompilerParams(
            collective_id=1, has_side_effects=True, vmem_limit_bytes=48 * MIB
        ),
    )(kind, block, *left, *columns, *ends, gains, vector)
    return outs[:4]


def kind_of_blocks(tile_count, heads_here, blocks_here):
    number = jnp.arange(tile_count)
    kind = number // heads_here
    table = jnp.array([0, 0, 0, 1, 2, 3, 3, 4], jnp.int32)
    late = jnp.where(number < 8 * heads_here + blocks_here, 5, 6)
    return jnp.where(number < 8 * heads_here, table[jnp.minimum(kind, 7)], late).astype(jnp.int32)


def slot_grads(holder, kinds, rows, columns):
    depth = max(r.shape[0] for r in rows)

    def deep(value, axis):
        room = [(0, 0)] * value.ndim
        room[axis] = (0, depth - value.shape[axis])
        return jnp.pad(value, room)

    left = jnp.stack([deep(r, 0) for r in rows])
    right = jnp.concatenate([deep(c, 1) for c in columns], 0)
    slots = holder.shape[0]
    used = (holder >= 0).astype(jnp.int32)
    block = jnp.maximum(holder, 0)
    kind = kinds[block]
    width = rows[0].shape[1]
    lanes = right.shape[2]

    def multiply(kind_ref, block_ref, used_ref, left_ref, right_ref, out_ref):
        slot = pl.program_id(0)

        @pl.when(used_ref[slot] == 1)
        def _():
            out_ref[0] = lax.dot_general(
                left_ref[kind_ref[slot]],
                right_ref[0],
                (((0,), (0,)), ((), ())),
                preferred_element_type=jnp.float32,
            ).astype(out_ref.dtype)

        @pl.when(used_ref[slot] == 0)
        def _():
            out_ref[...] = jnp.zeros_like(out_ref)

    return pl.pallas_call(
        multiply,
        grid_spec=pltpu.PrefetchScalarGridSpec(
            num_scalar_prefetch=3,
            grid=(slots,),
            in_specs=[
                pl.BlockSpec(left.shape, lambda s, kd, b, u: (0, 0, 0)),
                pl.BlockSpec((1, depth, lanes), lambda s, kd, b, u: (b[s], 0, 0)),
            ],
            out_specs=pl.BlockSpec((1, width, lanes), lambda s, kd, b, u: (s, 0, 0)),
        ),
        out_shape=jax.ShapeDtypeStruct((slots, width, lanes), jnp.bfloat16),
        compiler_params=pltpu.CompilerParams(vmem_limit_bytes=48 * MIB),
    )(kind, block, used, left, right)


def adam_slots(planes, master, moment_one, moment_two, slot_scale, filled):
    count, slot_count, width, lanes = planes.shape

    def step(scale_ref, fill_ref, grads, weight, one, two, new_weight, new_one, new_two):
        slot = pl.program_id(0)

        @pl.when(fill_ref[slot] == 1)
        def _():
            total = grads[0, 0].astype(jnp.float32)
            for n in range(1, count):
                total = total + grads[n, 0].astype(jnp.float32)
            results = adam_step(
                weight[0, 0], total * scale_ref[slot], one[0, 0], two[0, 0], TILE_RATE, TILE_DECAY
            )
            for ref, value in zip((new_weight, new_one, new_two), results):
                ref[0, 0] = value

        @pl.when(fill_ref[slot] == 0)
        def _():
            new_weight[...] = weight[...]
            new_one[...] = one[...]
            new_two[...] = two[...]

    deep = pl.BlockSpec((1, 1, width, lanes), lambda s: (0, s, 0, 0))
    scalars = pl.BlockSpec(memory_space=pltpu.SMEM)
    return pl.pallas_call(
        step,
        grid=(slot_count,),
        in_specs=[scalars, scalars, pl.BlockSpec((count, 1, width, lanes), lambda s: (0, s, 0, 0))]
        + [deep] * 3,
        out_specs=[deep] * 3,
        out_shape=[jax.ShapeDtypeStruct(master.shape, jnp.float32)] * 3,
        compiler_params=pltpu.CompilerParams(vmem_limit_bytes=32 * MIB),
    )(
        slot_scale,
        filled.astype(jnp.int32),
        *[
            pltpu.with_memory_space_constraint(v, pltpu.HBM)
            for v in (planes, master, moment_one, moment_two)
        ],
    )


SCALING = HEAD ** (-0.5)
BF16 = jnp.bfloat16
F32 = jnp.float32


def nn(left, right):
    return jnp.dot(left, right, preferred_element_type=F32)


def nt(left, right):
    return lax.dot_general(left, right, (((1,), (1,)), ((), ())), preferred_element_type=F32)


def tn(left, right):
    return lax.dot_general(left, right, (((0,), (0,)), ((), ())), preferred_element_type=F32)


def normed(rows):
    centre = rows - jnp.mean(rows, -1, keepdims=True)
    inverse = lax.rsqrt(jnp.mean(centre * centre, -1, keepdims=True) + NORM_EPS)
    return centre * inverse, inverse


def normed_back(rows, grad):
    unit, inverse = normed(rows)
    mean = jnp.mean(grad, -1, keepdims=True)
    return (grad - mean - unit * jnp.mean(grad * unit, -1, keepdims=True)) * inverse, unit


def total_of(rows):
    return jnp.sum(rows, 0, keepdims=True)


def turned(rows, cos_tab, sin_tab):
    even = lax.broadcasted_iota(jnp.int32, rows.shape, 1) % 2 == 0
    partner = jnp.where(even, pltpu.roll(rows, HEAD - 1, 1), pltpu.roll(rows, 1, 1))
    return rows * cos_tab + partner * sin_tab


def wide(column):
    return jnp.broadcast_to(column, (column.shape[0], HEAD))


def pack_sums(for_rows, for_text=None):
    out = wide(for_rows)
    if for_text is None:
        return out
    lane = lax.broadcasted_iota(jnp.int32, out.shape, 1)
    count = for_text.shape[0] // 2
    rest = jnp.zeros((out.shape[0] - count, HEAD), F32)
    first = jnp.concatenate([wide(for_text[:count]), rest], 0)
    second = jnp.concatenate([wide(for_text[count:]), rest], 0)
    return jnp.where(lane < 32, out, jnp.where(lane < 64, first, second))


def unpack_text(sums, count):
    return jnp.concatenate([sums[: count // 2, 32:33], sums[: count // 2, 64:65]], 0)


def softmax(scores):
    expo = jnp.exp(scores - jnp.max(scores, -1, keepdims=True))
    return expo / jnp.sum(expo, -1, keepdims=True)


def self_scores(query_low, key_low, tokens):
    scores = nt(query_low, key_low) * SCALING
    lane = lax.broadcasted_iota(jnp.int32, scores.shape, 1)
    return jnp.where(lane < tokens, scores, -1e30)


def whole(array):
    zeros = (0,) * len(array.shape)
    return pl.BlockSpec(array.shape, lambda *_: zeros)


def block_at(first, stride=1):
    return pl.BlockSpec((1, D, HEAD), lambda i, where: (where[first + stride * i], 0, 0))


def call(body, places, grid, ins, outs, scratch=(), vmem=24):
    specs = [spec if spec is not None else whole(array) for array, spec in ins]
    shapes = [pltpu.HBM(shape, kind) for shape, kind, _ in outs]
    out_specs = [
        spec if spec is not None else whole(shape) for (_, _, spec), shape in zip(outs, shapes)
    ]
    return pl.pallas_call(
        body,
        grid_spec=pltpu.PrefetchScalarGridSpec(
            num_scalar_prefetch=1,
            grid=(grid,),
            in_specs=specs,
            out_specs=out_specs,
            scratch_shapes=list(scratch),
        ),
        out_shape=shapes,
        compiler_params=pltpu.CompilerParams(vmem_limit_bytes=vmem * MIB),
    )(places, *[pltpu.with_memory_space_constraint(array, pltpu.HBM) for array, _ in ins])


def head_lanes(rows, per=1):
    return pl.BlockSpec((rows, per * HEAD), lambda h, *_: (0, h))


def heads_per_step(heads, most):
    return max(n for n in (1, 2, 3, 6) if heads % n == 0 and n <= most)


def lane_group(ref, j):
    return ref[:, j * HEAD : (j + 1) * HEAD]


def joined(refs):
    return jnp.concatenate([ref[0] for ref in refs], 1)


def project_self(places, everyone, rows, mod, vecs, heads):
    count = rows.shape[0]
    span = heads * HEAD

    def body(_, rows_ref, mod_ref, vec_ref, *refs):
        weights, (low, pre, value, sums, acc) = refs[:heads], refs[heads:]
        i = pl.program_id(0)

        @pl.when(i == 0)
        def _():
            unit, _ = normed(rows_ref[...])
            low[...] = (unit * (1.0 + mod_ref[1:2]) + mod_ref[0:1]).astype(BF16)

        made = nn(low[...], joined(weights))

        @pl.when(i == 0)
        def _():
            q = made + vec_ref[0:1]
            pre[0] = q
            acc[...] = wide(jnp.sum(q * q, -1, keepdims=True))

        @pl.when(i == 1)
        def _():
            k = made + vec_ref[1:2]
            pre[0] = k
            lane = lax.broadcasted_iota(jnp.int32, acc.shape, 1)
            sums[...] = jnp.where(lane < 64, acc[...], wide(jnp.sum(k * k, -1, keepdims=True)))

        @pl.when(i == 2)
        def _():
            value[...] = (made + vec_ref[2:3]).astype(BF16)

    return call(
        body, places, 3,
        [(rows, None), (mod, None), (vecs, None)]
        + [(everyone, block_at(h, heads)) for h in range(heads)],
        [
            ((count, D), BF16, None),
            ((2, count, span), F32, pl.BlockSpec((1, count, span), lambda i, _: (jnp.minimum(i, 1), 0, 0))),
            ((count, span), BF16, None),
            ((count, HEAD), F32, None),
        ],
        [pltpu.VMEM((count, HEAD), F32)],
    )


def attend_self(places, everyone, pre, value, sums, other, vecs, cos_tab, sin_tab, heads, tokens):
    count = value.shape[0]
    per = heads_per_step(heads, 2)
    steps = heads // per

    def body(_, pre_ref, value_ref, sum_ref, other_ref, vec_ref, cos_ref, sin_ref, *refs):
        weights, (q_ref, k_ref, o_ref, y_ref, acc) = refs[:per], refs[per:]
        h = pl.program_id(0)
        total = sum_ref[...] + other_ref[...]
        q_inv = lax.rsqrt(total[:, 0:1] / D + NORM_EPS)
        k_inv = lax.rsqrt(total[:, 64:65] / D + NORM_EPS)
        cos, sin = cos_ref[...], sin_ref[...]
        outs = []
        for j in range(per):
            lanes = slice(j * HEAD, (j + 1) * HEAD)
            q = turned(pre_ref[0, :, lanes] * q_inv * vec_ref[3:4, lanes], cos, sin).astype(BF16)
            k = turned(pre_ref[1, :, lanes] * k_inv * vec_ref[4:5, lanes], cos, sin).astype(BF16)
            q_ref[:, lanes] = q
            k_ref[:, lanes] = k
            chance = softmax(self_scores(q, k, tokens))
            out = nn(chance.astype(BF16), value_ref[:, lanes]).astype(BF16)
            o_ref[j] = out
            outs.append(out)
        part = nt(jnp.concatenate(outs, 1), joined(weights))

        @pl.when(h == 0)
        def _():
            acc[...] = part

        @pl.when(h > 0)
        def _():
            acc[...] = acc[...] + part

        @pl.when(h == steps - 1)
        def _():
            y_ref[...] = acc[...].astype(BF16)

    lanes = head_lanes(count, per)
    return call(
        body, places, steps,
        [
            (pre, pl.BlockSpec((2, count, per * HEAD), lambda h, _: (0, 0, h))),
            (value, lanes), (sums, None), (other, None),
            (vecs, head_lanes(vecs.shape[0], per)), (cos_tab, None), (sin_tab, None),
        ]
        + [(everyone, block_at(3 * heads + j, per)) for j in range(per)],
        [
            (value.shape, BF16, lanes),
            (value.shape, BF16, lanes),
            ((heads, count, HEAD), BF16, pl.BlockSpec((per, count, HEAD), lambda h, _: (h, 0, 0))),
            ((count, D), BF16, None),
        ],
        [pltpu.VMEM((count, D), F32)],
    )


def project_text(places, everyone, context, vecs, heads):
    count = context.shape[0]
    span = heads * HEAD

    def body(_, text_ref, vec_ref, *refs):
        weights, (key, value, sums) = refs[:heads], refs[heads:]
        i = pl.program_id(0)
        made = nn(text_ref[...], joined(weights))

        @pl.when(i == 0)
        def _():
            k = made + vec_ref[6:7]
            key[...] = k
            sums[...] = wide(jnp.sum(k * k, -1, keepdims=True))

        @pl.when(i == 1)
        def _():
            value[...] = (made + vec_ref[7:8]).astype(BF16)

    return call(
        body, places, 2,
        [(context, None), (vecs, None)]
        + [(everyone, block_at(5 * heads + h, heads)) for h in range(heads)],
        [((count, span), F32, None), ((count, span), BF16, None), ((count, HEAD), F32, None)],
    )


def project_cross(places, everyone, rows, part, other, mod, shared, vecs, text_sums, heads):
    count = rows.shape[0]
    span = heads * HEAD
    text = text_sums.shape[0]

    def body(_, rows_ref, part_ref, other_ref, mod_ref, shared_ref, vec_ref, text_ref, *refs):
        weights, (branch, after, low, pre, sums) = refs[:heads], refs[heads:]
        y = part_ref[...].astype(F32) + other_ref[...].astype(F32) + shared_ref[0:1]
        branch[...] = y
        x = rows_ref[...] + mod_ref[2:3] * y
        after[...] = x
        unit, _ = normed(x)
        a = (unit * shared_ref[3:4] + shared_ref[4:5]).astype(BF16)
        low[...] = a
        q = nn(a, joined(weights)) + vec_ref[5:6]
        pre[...] = q
        sums[...] = pack_sums(jnp.sum(q * q, -1, keepdims=True), text_ref[:, 0:1])

    return call(
        body, places, 1,
        [(v, None) for v in (rows, part, other, mod, shared, vecs, text_sums)]
        + [(everyone, block_at(4 * heads + h)) for h in range(heads)],
        [
            ((count, D), F32, None),
            ((count, D), F32, None),
            ((count, D), BF16, None),
            ((count, span), F32, None),
            ((count, HEAD), F32, None),
        ],
    )


def attend_cross(places, everyone, pre, key_pre, value, sums, other, vecs, heads):
    count, text = pre.shape[0], value.shape[0]
    per = heads_per_step(heads, 6)
    steps = heads // per

    def body(_, pre_ref, key_ref, value_ref, sum_ref, other_ref, vec_ref, *refs):
        weights, (q_ref, k_ref, o_ref, y_ref, acc) = refs[:per], refs[per:]
        h = pl.program_id(0)
        total = sum_ref[...] + other_ref[...]
        q_inv = lax.rsqrt(total[:, 0:1] / D + NORM_EPS)
        k_inv = lax.rsqrt(unpack_text(total, text) / D + NORM_EPS)
        outs = []
        for j in range(per):
            lanes = slice(j * HEAD, (j + 1) * HEAD)
            q = (pre_ref[:, lanes] * q_inv * vec_ref[8:9, lanes]).astype(BF16)
            k = (key_ref[:, lanes] * k_inv * vec_ref[9:10, lanes]).astype(BF16)
            q_ref[:, lanes] = q
            k_ref[:, lanes] = k
            chance = softmax(nt(q, k) * SCALING)
            out = nn(chance.astype(BF16), value_ref[:, lanes]).astype(BF16)
            o_ref[j] = out
            outs.append(out)
        part = nt(jnp.concatenate(outs, 1), joined(weights))

        @pl.when(h == 0)
        def _():
            acc[...] = part

        @pl.when(h > 0)
        def _():
            acc[...] = acc[...] + part

        @pl.when(h == steps - 1)
        def _():
            y_ref[...] = acc[...].astype(BF16)

    return call(
        body, places, steps,
        [
            (pre, head_lanes(count, per)), (key_pre, head_lanes(text, per)),
            (value, head_lanes(text, per)), (sums, None), (other, None),
            (vecs, head_lanes(vecs.shape[0], per)),
        ]
        + [(everyone, block_at(7 * heads + j, per)) for j in range(per)],
        [
            (pre.shape, BF16, head_lanes(count, per)),
            (value.shape, BF16, head_lanes(text, per)),
            ((heads, count, HEAD), BF16, pl.BlockSpec((per, count, HEAD), lambda h, _: (h, 0, 0))),
            ((count, D), BF16, None),
        ],
        [pltpu.VMEM((count, D), F32)],
        vmem=40,
    )


def hidden_group(blocks):
    return max(g for g in (7, 5, 4, 3, 2, 1) if blocks % g == 0)


def block_lanes(where, everyone, held, sems, first, group, steps):
    i = pl.program_id(0)

    def fetch(step, act):
        slot = step % 2
        for j in range(group):
            copy = pltpu.make_async_copy(
                everyone.at[where[first + step * group + j]],
                held.at[slot, :, pl.ds(j * HEAD, HEAD)],
                sems.at[slot, j],
            )
            copy.start() if act else copy.wait()

    @pl.when(i == 0)
    def _():
        fetch(0, True)

    @pl.when(i + 1 < steps)
    def _():
        fetch(i + 1, True)

    fetch(i, False)
    return held[i % 2]


def lanes_scratch(group):
    return [pltpu.VMEM((2, D, group * HEAD), BF16), pltpu.SemaphoreType.DMA((2, group))]


def hidden_back(places, everyone, mod, cot, heads, blocks):
    count = cot.shape[0]
    group = hidden_group(blocks)
    steps = blocks // group

    def body(where, weights, mod_ref, cot_ref, grad, out, held, sems):
        @pl.when(pl.program_id(0) == 0)
        def _():
            grad[...] = (mod_ref[5:6] * cot_ref[...]).astype(BF16)

        down = block_lanes(where, weights, held, sems, 8 * heads + blocks, group, steps)
        out[...] = nn(grad[...], down).astype(BF16)

    return call(
        body, places, steps,
        [(everyone, ANY), (mod, None), (cot, None)],
        [
            ((count, D), BF16, None),
            ((count, blocks * HEAD), BF16, pl.BlockSpec((count, group * HEAD), lambda i, _: (0, i))),
        ],
        lanes_scratch(group),
        vmem=40,
    )


def hidden_both(places, everyone, after_one, part, other, mod, shared, d_act, up_bias, heads, blocks):
    count = after_one.shape[0]
    group = hidden_group(blocks)
    steps = blocks // group
    span = group * HEAD

    def body(where, weights, after_ref, part_ref, other_ref, mod_ref, shared_ref, d_ref, bias_ref, after, low, hidden, d_hidden, d_bias, da_ref, acc, held, sems):
        i = pl.program_id(0)

        @pl.when(i == 0)
        def _():
            x = after_ref[...] + part_ref[...].astype(F32) + other_ref[...].astype(F32)
            x = x + shared_ref[1:2]
            after[...] = x
            unit, _ = normed(x)
            low[...] = (unit * (1.0 + mod_ref[4:5]) + mod_ref[3:4]).astype(BF16)
            acc[...] = jnp.zeros_like(acc)

        up = block_lanes(where, weights, held, sems, 8 * heads, group, steps)
        pre = nn(low[...], up) + bias_ref[...]
        square = pre * pre
        bent = jnp.tanh(GELU_COEF * (pre + 0.044715 * pre * square))
        act = (0.5 * pre * (1.0 + bent)).astype(BF16)
        slope = 0.5 * (1.0 + bent) + 0.5 * pre * (1.0 - bent * bent) * (
            GELU_COEF * (1.0 + 3.0 * 0.044715 * square)
        )
        dh = (d_ref[...].astype(F32) * slope).astype(BF16)
        d_bias[...] = total_of(dh.astype(F32))
        for j in range(group):
            hidden[j] = act[:, j * HEAD : (j + 1) * HEAD]
            d_hidden[j] = dh[:, j * HEAD : (j + 1) * HEAD]
        acc[...] = acc[...] + nt(dh, up)

        @pl.when(i == steps - 1)
        def _():
            da_ref[...] = acc[...].astype(BF16)

    tall = pl.BlockSpec((group, count, HEAD), lambda i, _: (i, 0, 0))
    flat = pl.BlockSpec((1, span), lambda i, _: (0, i))
    return call(
        body, places, steps,
        [(everyone, ANY)]
        + [(v, None) for v in (after_one, part, other, mod, shared)]
        + [(d_act, pl.BlockSpec((count, span), lambda i, _: (0, i))), (up_bias, flat)],
        [
            ((count, D), F32, None),
            ((count, D), BF16, None),
            ((blocks, count, HEAD), BF16, tall),
            ((blocks, count, HEAD), BF16, tall),
            (up_bias.shape, F32, flat),
            ((count, D), BF16, None),
        ],
        [pltpu.VMEM((count, D), F32)] + lanes_scratch(group),
        vmem=40,
    )


def hidden_out(places, everyone, hidden, heads):
    blocks, count = hidden.shape[:2]
    group = hidden_group(blocks)
    steps = blocks // group

    def body(where, weights, hidden_ref, y_ref, acc, held, sems):
        i = pl.program_id(0)
        down = block_lanes(where, weights, held, sems, 8 * heads + blocks, group, steps)
        part = nt(jnp.concatenate([hidden_ref[j] for j in range(group)], 1), down)

        @pl.when(i == 0)
        def _():
            acc[...] = part

        @pl.when(i > 0)
        def _():
            acc[...] = acc[...] + part

        @pl.when(i == steps - 1)
        def _():
            y_ref[...] = acc[...].astype(BF16)

    return call(
        body, places, steps,
        [(everyone, ANY), (hidden, pl.BlockSpec((group, count, HEAD), lambda i, _: (i, 0, 0)))],
        [((count, D), BF16, None)],
        [pltpu.VMEM((count, D), F32)] + lanes_scratch(group),
        vmem=40,
    )[0]


def cross_back(places, everyone, cot, after_two, part, other, mod, query, key, value, pre, key_pre, vecs, heads):
    count, text = query.shape[0], key.shape[0]
    per = heads_per_step(heads, 6)
    steps = heads // per

    def body(_, cot_ref, after_ref, part_ref, other_ref, mod_ref, q_ref, k_ref, v_ref, pre_ref, key_ref, vec_ref, *refs):
        weights, (dx_ref, low_ref, dq_ref, dk_ref, dv_ref, sums, q_acc, k_acc) = refs[:per], refs[per:]
        h = pl.program_id(0)

        @pl.when(h == 0)
        def _():
            da = part_ref[...].astype(F32) + other_ref[...].astype(F32)
            back, _ = normed_back(after_ref[...], da * (1.0 + mod_ref[4:5]))
            dx = cot_ref[...] + back
            dx_ref[...] = dx
            low_ref[...] = dx.astype(BF16)
            q_acc[...] = jnp.zeros_like(q_acc)
            k_acc[...] = jnp.zeros_like(k_acc)

        do_all = nn(low_ref[...], joined(weights)).astype(BF16)
        q_sums, k_sums = 0.0, 0.0
        for j in range(per):
            lanes = slice(j * HEAD, (j + 1) * HEAD)
            do = do_all[:, lanes]
            q, k = q_ref[:, lanes], k_ref[:, lanes]
            chance = softmax(nt(q, k) * SCALING)
            dp = nt(do, v_ref[:, lanes])
            ds = (chance * (dp - jnp.sum(chance * dp, -1, keepdims=True))).astype(BF16)
            dv_ref[j] = tn(chance.astype(BF16), do).astype(BF16)
            dq = nn(ds, k) * SCALING
            dk = tn(ds, q) * SCALING
            dq_ref[:, lanes] = dq
            dk_ref[:, lanes] = dk
            q_sums += pre_ref[:, lanes] * vec_ref[8:9, lanes] * dq
            k_sums += key_ref[:, lanes] * vec_ref[9:10, lanes] * dk
        q_acc[...] = q_acc[...] + q_sums
        k_acc[...] = k_acc[...] + k_sums

        @pl.when(h == steps - 1)
        def _():
            sums[...] = pack_sums(
                jnp.sum(q_acc[...], -1, keepdims=True), jnp.sum(k_acc[...], -1, keepdims=True)
            )

    return call(
        body, places, steps,
        [(v, None) for v in (cot, after_two, part, other, mod)]
        + [
            (query, head_lanes(count, per)), (key, head_lanes(text, per)),
            (value, head_lanes(text, per)), (pre, head_lanes(count, per)),
            (key_pre, head_lanes(text, per)), (vecs, head_lanes(vecs.shape[0], per)),
        ]
        + [(everyone, block_at(7 * heads + j, per)) for j in range(per)],
        [
            ((count, D), F32, None),
            ((count, D), BF16, None),
            (query.shape, F32, head_lanes(count, per)),
            (key.shape, F32, head_lanes(text, per)),
            ((heads, text, HEAD), BF16, pl.BlockSpec((per, text, HEAD), lambda h, _: (h, 0, 0))),
            ((count, HEAD), F32, None),
        ],
        [pltpu.VMEM((count, HEAD), F32), pltpu.VMEM((text, HEAD), F32)],
        vmem=48,
    )


def norm_grad(pre, inverse, gain, incoming, total):
    grad = inverse * (gain * incoming) - pre * (inverse * inverse * inverse) * (total / D)
    low = grad.astype(BF16)
    return low, total_of(low.astype(F32)), total_of(incoming * pre * inverse)


def cross_back_rows(places, everyone, pre, key_pre, dq, dk, dv, squares, squares_other, sums, sums_other, vecs, heads):
    count, text = pre.shape[0], key_pre.shape[0]
    per = heads_per_step(heads, 6)
    steps = heads // per

    def body(_, pre_ref, key_ref, dq_ref, dk_ref, dv_ref, sq_ref, sqo_ref, sum_ref, sumo_ref, vec_ref, *refs):
        weights, (gq_ref, gk_ref, vec_out, da_ref, acc) = refs[:per], refs[per:]
        h = pl.program_id(0)
        squares_all = sq_ref[...] + sqo_ref[...]
        total = sum_ref[...] + sumo_ref[...]
        q_inv = lax.rsqrt(squares_all[:, 0:1] / D + NORM_EPS)
        k_inv = lax.rsqrt(unpack_text(squares_all, text) / D + NORM_EPS)
        q_total, k_total = total[:, 0:1], unpack_text(total, text)
        lows = []
        for j in range(per):
            lanes = slice(j * HEAD, (j + 1) * HEAD)
            low_q, bias_q, gain_q = norm_grad(
                pre_ref[:, lanes], q_inv, vec_ref[8:9, lanes], dq_ref[:, lanes], q_total
            )
            low_k, bias_k, gain_k = norm_grad(
                key_ref[:, lanes], k_inv, vec_ref[9:10, lanes], dk_ref[:, lanes], k_total
            )
            gq_ref[j] = low_q
            gk_ref[j] = low_k
            lows.append(low_q)
            bias_v = total_of(dv_ref[j].astype(F32))
            vec_out[:, lanes] = jnp.concatenate(
                [bias_q, bias_k, bias_v, gain_q, gain_k, jnp.zeros((3, HEAD), F32)], 0
            )
        part = nt(jnp.concatenate(lows, 1), joined(weights))

        @pl.when(h == 0)
        def _():
            acc[...] = part

        @pl.when(h > 0)
        def _():
            acc[...] = acc[...] + part

        @pl.when(h == steps - 1)
        def _():
            da_ref[...] = acc[...].astype(BF16)

    tall = pl.BlockSpec((per, count, HEAD), lambda h, _: (h, 0, 0))
    tall_text = pl.BlockSpec((per, text, HEAD), lambda h, _: (h, 0, 0))
    return call(
        body, places, steps,
        [
            (pre, head_lanes(count, per)), (key_pre, head_lanes(text, per)),
            (dq, head_lanes(count, per)), (dk, head_lanes(text, per)), (dv, tall_text),
            (squares, None), (squares_other, None), (sums, None), (sums_other, None),
            (vecs, head_lanes(vecs.shape[0], per)),
        ]
        + [(everyone, block_at(4 * heads + j, per)) for j in range(per)],
        [
            ((heads, count, HEAD), BF16, tall),
            ((heads, text, HEAD), BF16, tall_text),
            ((8, heads * HEAD), F32, head_lanes(8, per)),
            ((count, D), BF16, None),
        ],
        [pltpu.VMEM((count, D), F32)],
        vmem=40,
    )


def self_back(places, everyone, dx_two, after_one, part, other, mod, shared, branch, query, key, value, pre, vecs, cos_tab, sin_tab, heads, tokens):
    count = query.shape[0]
    per = heads_per_step(heads, 2)
    steps = heads // per

    def body(_, dx_in, after_ref, part_ref, other_ref, mod_ref, shared_ref, branch_ref, q_ref, k_ref, v_ref, pre_ref, vec_ref, cos_ref, sin_ref, *refs):
        weights, (dx_ref, low_ref, d_ref, dv_ref, sums, vec_out, q_acc, k_acc) = refs[:per], refs[per:]
        h = pl.program_id(0)

        @pl.when(h == 0)
        def _():
            da = part_ref[...].astype(F32) + other_ref[...].astype(F32)
            back, _ = normed_back(after_ref[...], da * shared_ref[3:4])
            dx = dx_in[...] + back
            dx_ref[...] = dx
            low = (mod_ref[2:3] * dx).astype(BF16)
            low_ref[...] = low
            vec_out[0:1] = 0.5 * total_of(low.astype(F32))
            vec_out[1:2] = 0.5 * total_of(dx * branch_ref[...])
            q_acc[...] = jnp.zeros_like(q_acc)
            k_acc[...] = jnp.zeros_like(k_acc)

        do_all = nn(low_ref[...], joined(weights)).astype(BF16)
        cos, sin = cos_ref[...], -sin_ref[...]
        q_sums, k_sums = 0.0, 0.0
        for j in range(per):
            lanes = slice(j * HEAD, (j + 1) * HEAD)
            do = do_all[:, lanes]
            q, k = q_ref[:, lanes], k_ref[:, lanes]
            chance = softmax(self_scores(q, k, tokens))
            dp = nt(do, v_ref[:, lanes])
            ds = (chance * (dp - jnp.sum(chance * dp, -1, keepdims=True))).astype(BF16)
            dv_ref[j] = tn(chance.astype(BF16), do).astype(BF16)
            dq = turned(nn(ds, k) * SCALING, cos, sin)
            dk = turned(tn(ds, q) * SCALING, cos, sin)
            d_ref[0, :, lanes] = dq
            d_ref[1, :, lanes] = dk
            q_sums += pre_ref[0, :, lanes] * vec_ref[3:4, lanes] * dq
            k_sums += pre_ref[1, :, lanes] * vec_ref[4:5, lanes] * dk
        q_acc[...] = q_acc[...] + q_sums
        k_acc[...] = k_acc[...] + k_sums

        @pl.when(h == steps - 1)
        def _():
            lane = lax.broadcasted_iota(jnp.int32, q_acc.shape, 1)
            sums[...] = jnp.where(
                lane < 64,
                wide(jnp.sum(q_acc[...], -1, keepdims=True)),
                wide(jnp.sum(k_acc[...], -1, keepdims=True)),
            )

    lanes = head_lanes(count, per)
    pair = pl.BlockSpec((2, count, per * HEAD), lambda h, _: (0, 0, h))
    return call(
        body, places, steps,
        [(v, None) for v in (dx_two, after_one, part, other, mod, shared, branch)]
        + [
            (query, lanes), (key, lanes), (value, lanes), (pre, pair),
            (vecs, head_lanes(vecs.shape[0], per)), (cos_tab, None), (sin_tab, None),
        ]
        + [(everyone, block_at(3 * heads + j, per)) for j in range(per)],
        [
            ((count, D), F32, None),
            ((count, D), BF16, None),
            (pre.shape, F32, pair),
            ((heads, count, HEAD), BF16, pl.BlockSpec((per, count, HEAD), lambda h, _: (h, 0, 0))),
            ((count, HEAD), F32, None),
            ((2, D), F32, None),
        ],
        [pltpu.VMEM((count, HEAD), F32), pltpu.VMEM((count, HEAD), F32)],
        vmem=32,
    )


def self_back_rows(places, everyone, rows, pre, grads, dv, squares, squares_other, sums, sums_other, vecs, heads):
    count = pre.shape[1]
    per = heads_per_step(heads, 2)
    steps = heads // per

    def body(_, rows_ref, pre_ref, d_ref, dv_ref, sq_ref, sqo_ref, sum_ref, sumo_ref, vec_ref, *refs):
        weights, (gq_ref, gk_ref, vec_out, da_ref, row_out, acc) = refs[: 3 * per], refs[3 * per :]
        h = pl.program_id(0)
        squares_all = sq_ref[...] + sqo_ref[...]
        total = sum_ref[...] + sumo_ref[...]
        inverses = [
            lax.rsqrt(squares_all[:, n : n + 1] / D + NORM_EPS) for n in (0, 64)
        ]
        lows = []
        for j in range(per):
            lanes = slice(j * HEAD, (j + 1) * HEAD)
            biases, gains = [], []
            for n, out in enumerate((gq_ref, gk_ref)):
                low, bias, gain = norm_grad(
                    pre_ref[n, :, lanes], inverses[n], vec_ref[3 + n : 4 + n, lanes],
                    d_ref[n, :, lanes], total[:, 64 * n : 64 * n + 1],
                )
                out[j] = low
                lows.append(low)
                biases.append(bias)
                gains.append(gain)
            dv_low = dv_ref[j]
            lows.append(dv_low)
            vec_out[:, lanes] = jnp.concatenate(
                biases + [total_of(dv_low.astype(F32))] + gains + [jnp.zeros((3, HEAD), F32)], 0
            )
        part = nt(jnp.concatenate(lows, 1), joined(weights))

        @pl.when(h == 0)
        def _():
            acc[...] = part

        @pl.when(h > 0)
        def _():
            acc[...] = acc[...] + part

        @pl.when(h == steps - 1)
        def _():
            da = acc[...]
            da_ref[...] = da.astype(BF16)
            row_out[0:1] = total_of(da)
            row_out[1:2] = total_of(da * normed(rows_ref[...])[0])

    tall = pl.BlockSpec((per, count, HEAD), lambda h, _: (h, 0, 0))
    pair = pl.BlockSpec((2, count, per * HEAD), lambda h, _: (0, 0, h))
    return call(
        body, places, steps,
        [
            (rows, None), (pre, pair), (grads, pair), (dv, tall), (squares, None),
            (squares_other, None), (sums, None), (sums_other, None),
            (vecs, head_lanes(vecs.shape[0], per)),
        ]
        + [(everyone, block_at(n * heads + j, per)) for j in range(per) for n in range(3)],
        [
            ((heads, count, HEAD), BF16, tall),
            ((heads, count, HEAD), BF16, tall),
            ((8, heads * HEAD), F32, head_lanes(8, per)),
            ((count, D), BF16, None),
            ((2, D), F32, None),
        ],
        [pltpu.VMEM((count, D), F32)],
        vmem=40,
    )


def shared_sums(places, after_one, after_two, grad_two, grad_three, cot, da_two, da_three, y_three, shared):
    def body(_, x1_ref, x2_ref, dy2, dy3, cot_ref, da2, da3, y3, shared_ref, out):
        out[...] = jnp.zeros_like(out)
        out[1:2] = 0.5 * total_of(dy2[...].astype(F32))
        out[2:3] = 0.5 * total_of(dy3[...].astype(F32))
        part = da3[...].astype(F32)
        out[3:4] = total_of(part * normed(x1_ref[...])[0])
        out[4:5] = total_of(part)
        part = da2[...].astype(F32)
        out[8:9] = total_of(part)
        out[9:10] = total_of(part * normed(x2_ref[...])[0])
        out[10:11] = total_of(cot_ref[...] * (y3[...].astype(F32) + 0.5 * shared_ref[2:3]))

    return call(
        body, places, 1,
        [(v, None) for v in (after_one, after_two, grad_two, grad_three, cot, da_two, da_three, y_three, shared)],
        [(shared.shape, F32, None)],
    )[0]


def body(
    latents,
    context,
    cotangent,
    positions,
    step_ids,
    owners,
    time_table,
    master,
    first_moment,
    second_moment,
    head_params,
    head_first,
    head_second,
    shared_params,
    shared_first,
    shared_second,
):
    tensors = lax.axis_size("tensor")
    devices = lax.axis_size("dp")
    slot_count = master.shape[1]
    tile_count = owners.shape[0]
    heads_here = HEADS // tensors
    blocks_here = FF // (HEAD * tensors)
    width_here = D // tensors
    places, holder = owner_layout(owners, slot_count, devices)
    scales = tile_scales(tile_count, heads_here, blocks_here)
    my_slots = lax.dynamic_slice_in_dim(holder, lax.axis_index("dp") * slot_count, slot_count)
    rank = pair_rank()
    filled = my_slots >= 0
    slot_scale = jnp.where(filled, scales[jnp.maximum(my_slots, 0)], 0.0)
    scaled = (master[0] * slot_scale[:, None, None]).astype(jnp.bfloat16)
    half = latents.shape[0]
    tokens = 2 * half
    count = -(-tokens // 16) * 16
    taller = ((0, -half % 16), (0, 0))
    small = jnp.concatenate(
        [
            head_params[0],
            positions.reshape(-1).astype(jnp.float32),
            step_ids.astype(jnp.float32),
        ]
    )
    packed = jnp.pad(small, (0, -small.shape[0] % 1024)).reshape(-1, HEAD)
    everyone, lats, cots, context, packed = gather_slots(
        scaled, jnp.pad(latents, taller), jnp.pad(cotangent, taller), context, packed
    )
    small = packed.reshape(-1)
    vectors = small[: head_params.shape[1]]
    small = small[head_params.shape[1] :]
    positions = small[: positions.size].reshape(positions.shape)
    step = small[positions.size]
    vecs = vectors[: 10 * width_here].reshape(10, width_here)
    up_bias = vectors[10 * width_here :].reshape(1, -1)
    chosen = (step == jnp.arange(TSTEPS)).astype(jnp.float32)
    mod = shared_params[5:11] + jnp.einsum(
        "s,skd->kd", chosen, time_table, precision=lax.Precision.HIGHEST
    )
    cos_tab, sin_tab = rope_tables(positions, HEAD)
    sin_tab = jnp.where(jnp.arange(HEAD) % 2 == 0, -sin_tab, sin_tab)
    cos_tab, sin_tab = (jnp.pad(t, ((0, count - tokens), (0, 0))) for t in (cos_tab, sin_tab))

    def all_rows(halves):
        rows = jnp.concatenate([halves[0, :half], halves[1, :half]], 0)
        return jnp.pad(rows, ((0, count - tokens), (0, 0))).astype(jnp.float32)

    def upright(rows):
        return jnp.pad(rows, ((0, context.shape[0] - rows.shape[0]), (0, 0))).T

    def beside(*values):
        return lax.optimization_barrier(values)

    rows, cot = all_rows(lats), all_rows(cots)
    low_one, pre_one, value_one, squares_one = project_self(
        places, everyone, rows, mod, vecs, heads_here
    )
    squares_one_other = pair_swap(squares_one)
    query_one, key_one, heads_one, part_one = attend_self(
        places, everyone, pre_one, value_one, squares_one, squares_one_other, vecs, cos_tab,
        sin_tab, heads_here, tokens,
    )
    part_one, context = beside(part_one, context)
    part_one_other = pair_swap(part_one)
    key_pre, value_two, text_squares = project_text(places, everyone, context, vecs, heads_here)
    left_context, left_one = upright(context), upright(low_one)
    part_one_other, key_pre, left_context, left_one = beside(
        part_one_other, key_pre, left_context, left_one
    )
    branch_one, after_one, low_two, pre_two, squares_two = project_cross(
        places, everyone, rows, part_one, part_one_other, mod, shared_params, vecs,
        text_squares, heads_here,
    )
    squares_two_other = pair_swap(squares_two)
    query_two, key_two, heads_two, part_two = attend_cross(
        places, everyone, pre_two, key_pre, value_two, squares_two, squares_two_other, vecs,
        heads_here,
    )
    part_two, cot, low_two = beside(part_two, cot, low_two)
    part_two_other = pair_swap(part_two)
    grad_three, d_act = hidden_back(places, everyone, mod, cot, heads_here, blocks_here)
    left_two, left_grad_three = upright(low_two), upright(grad_three)
    part_two_other, d_act, left_two, left_grad_three = beside(
        part_two_other, d_act, left_two, left_grad_three
    )
    after_two, low_three, hidden, d_hidden, d_up_bias, da_two = hidden_both(
        places, everyone, after_one, part_two, part_two_other, mod, shared_params, d_act, up_bias,
        heads_here, blocks_here,
    )
    da_two_other = pair_swap(da_two)
    y_three = hidden_out(places, everyone, hidden, heads_here)
    left_three = upright(low_three)
    da_two_other, y_three, left_three = beside(da_two_other, y_three, left_three)
    dx_two, grad_two, dq_two, dk_two, dv_two, sums_two = cross_back(
        places, everyone, cot, after_two, da_two, da_two_other, mod, query_two, key_two,
        value_two, pre_two, key_pre, vecs, heads_here,
    )
    query_grad_two, key_grad_two, vecs_two, da_three = cross_back_rows(
        places, everyone, pre_two, key_pre, dq_two, dk_two, dv_two, squares_two,
        squares_two_other, sums_two, pair_swap(sums_two), vecs, heads_here,
    )
    da_three_other = pair_swap(da_three)
    shared_grad = shared_sums(
        places, after_one, after_two, grad_two, grad_three, cot, da_two, da_three, y_three,
        shared_params,
    )
    left_grad_two = upright(grad_two)
    da_three_other, shared_grad, left_grad_two = beside(da_three_other, shared_grad, left_grad_two)
    dx_one, grad_one, d_one, dv_one, sums_one, rows_a = self_back(
        places, everyone, dx_two, after_one, da_three, da_three_other, mod, shared_params,
        branch_one, query_one, key_one, value_one, pre_one, vecs, cos_tab, sin_tab, heads_here,
        tokens,
    )
    query_grad_one, key_grad_one, vecs_one, da_one, rows_b = self_back_rows(
        places, everyone, rows, pre_one, d_one, dv_one, squares_one, squares_one_other, sums_one,
        pair_swap(sums_one), vecs, heads_here,
    )
    shared_grad = jnp.concatenate(
        [rows_a[0:1], shared_grad[1:5], rows_b, rows_a[1:2], shared_grad[8:]], 0
    )
    head_grad = jnp.concatenate(
        [vecs_one[:5].reshape(-1), vecs_two[:5].reshape(-1), d_up_bias.reshape(-1)]
    )
    tensor_rank = lax.axis_index("tensor")
    head_padded = jnp.where(jnp.arange(tensors)[:, None] == rank, head_grad[None, :], 0.0)
    vector = jnp.concatenate([head_padded.reshape(-1), shared_grad.reshape(-1)])
    vector = jnp.pad(vector, (0, -vector.shape[0] % 1024)).reshape(-1, 128)
    parts, vector, output, grad_input = reduce_slots(
        holder,
        kind_of_blocks(tile_count, heads_here, blocks_here),
        (left_one, upright(grad_one), left_two, left_context, left_grad_two, left_three, left_grad_three),
        (
            query_grad_one,
            key_grad_one,
            dv_one,
            heads_one,
            query_grad_two,
            key_grad_two,
            dv_two,
            heads_two,
            d_hidden,
            hidden,
        ),
        vector,
        (rows, after_two, dx_one, y_three, da_one),
        jnp.concatenate([mod[5:6], mod[1:2], shared_params[2:3], jnp.zeros((5, D), F32)], 0),
        slot_count,
    )
    output, grad_input = (
        jnp.where(lax.axis_index("tensor") == 0, v[:half], v[half:tokens])
        for v in (output, grad_input)
    )
    new_master, new_first, new_second = adam_slots(
        parts, master, first_moment, second_moment, slot_scale, filled
    )
    vector = vector.reshape(-1)
    head_total = vector[: head_padded.size].reshape(head_padded.shape)
    shared_total = vector[head_padded.size : head_padded.size + shared_grad.size]
    shared_total = shared_total.reshape(shared_grad.shape)
    mine_head = lax.dynamic_slice_in_dim(head_total, tensor_rank, 1, 0)
    new_head, new_head_first, new_head_second = adam_step(
        head_params, mine_head, head_first, head_second, VECTOR_RATE, 0.0
    )
    new_shared, new_shared_first, new_shared_second = adam_step(
        shared_params, shared_total, shared_first, shared_second, VECTOR_RATE, 0.0
    )
    return (
        output,
        grad_input,
        new_master,
        new_first,
        new_second,
        new_head,
        new_head_first,
        new_head_second,
        new_shared,
        new_shared_first,
        new_shared_second,
    )


def solution(mesh):
    return jax.shard_map(
        body,
        mesh=mesh,
        in_specs=(
            P(("dp", "tensor"), None),
            P("dp", None),
            P(("dp", "tensor"), None),
            P(None, "dp"),
            P("dp"),
            P(),
            P(),
            P("tensor", "dp", None, None),
            P("tensor", "dp", None, None),
            P("tensor", "dp", None, None),
            P("tensor", None),
            P("tensor", None),
            P("tensor", None),
            P(),
            P(),
            P(),
        ),
        out_specs=(
            P(("dp", "tensor"), None),
            P(("dp", "tensor"), None),
            P("tensor", "dp", None, None),
            P("tensor", "dp", None, None),
            P("tensor", "dp", None, None),
            P("tensor", None),
            P("tensor", None),
            P("tensor", None),
            P(),
            P(),
            P(),
        ),
        check_vma=False,
    )
```

profile of v0, /device:TPU:0, one launch (start us, length us, event | category | flops | bytes accessed | tf_op | source)
XLA Modules:
  0.0 759.2 jit_solution(2303349834142330815)
XLA Ops:
  0.7 0.9 convert_reduce_fusion
  3.8 1.0 pad.48.lat
  5.9 3.8 fusion.own
  9.8 240.8 %shard_map.248 = (bf16[16,9,1536,128]{3,2,1,0:T(8,128)(2,1)}, bf16[2,144,1536]{2,1,0:T(8,128)(2,1)S(1)}, bf16[2,144,1536]{2,1,0:T(8,128)(2,1)S(1)}, bf16[512,1536]{1,0:T(8,128)(2,1)S(1)}, f32[104,128]{1,0:T(8,128)S(1)}) custom-call(bf16[9,1536,128]{2,1,0:T(8,128)(2,1)S(1)} %fusion.own, bf16[144,1536]{1,0:T(8,128)(2,1)S(1)} %pad.48.lat, ...), custom_call_target="tpu_custom_call" | custom-call | tf_op jit(solution)/shard_map/pallas_call | solution.py:393
  250.6 1.1 copy-done.2
  253.6 1.4 fusion.6.rows_ref.refs_17_
  255.1 1.0 fusion.15
  256.7 8.5 %shard_map.249 = (bf16[272,1536]{1,0:T(8,128)(2,1)}, f32[2,272,768]{2,1,0:T(8,128)}, bf16[272,768]{1,0:T(8,128)(2,1)}, f32[272,128]{1,0:T(8,128)}) custom-call(s32[118]{0:T(128)S(1)} %get-tuple-element.196._.where, f32[272,1536]{1,0:T(8,128)} %fusion.6.rows_ref.refs_17_, f32[6,1536]{1,0:T(8,128)} %bitcast_add_fusion.mod_ref, f32[10,768]{1,0:T(8,128)} %reshape.175.vec_ref, ...), custom_call_target="tpu_custom_call" | custom-call | tf_op jit(solution)/shard_map/pallas_call | solution.py:1018
  268.2 3.0 collective-permute-done.other_ref.sqo_ref
  271.8 8.3 %shard_map.250 = (bf16[272,768]{1,0:T(8,128)(2,1)}, bf16[272,768]{1,0:T(8,128)(2,1)}, bf16[6,272,128]{2,1,0:T(8,128)(2,1)}, bf16[272,1536]{1,0:T(8,128)(2,1)}) custom-call(s32[118]{0:T(128)S(1)} %get-tuple-element.196._.where, f32[2,272,768]{2,1,0:T(8,128)} %get-tuple-element.94.pre_ref, bf16[272,768]{1,0:T(8,128)(2,1)} %get-tuple-element.95.value_ref.v_ref, ...), custom_call_target="tpu_custom_call" | custom-call | tf_op jit(solution)/shard_map/pallas_call | solution.py:1018
  280.8 1.6 copy.49
  282.4 1.3 pad_bitcast_fusion.5.refs_0_
  283.8 1.0 slice_bitcast_fusion.1
  284.7 8.0 %shard_map.251 = (f32[512,768]{1,0:T(8,128)}, bf16[512,768]{1,0:T(8,128)(2,1)}, f32[512,128]{1,0:T(8,128)}) custom-call(s32[118]{0:T(128)S(1)} %get-tuple-element.196._.where, bf16[512,1536]{1,0:T(8,128)(2,1)} %copy-done.2, f32[10,768]{1,0:T(8,128)} %reshape.175.vec_ref, bf16[144,1536,128]{2,1,0:T(8,128)(2,1)} %bitcast.63, bf16[144,1536,128]{2,1,0:T(8,128)(2,1)} %bitcast.64, ...), custom_call_target="tpu_custom_call" | custom-call | tf_op jit(solution)/shard_map/pallas_call | solution.py:1018
  292.7 1.8 copy.48
  294.5 5.8 collective-permute-done.1.other_ref
  300.3 0.9 copy-done.23
  301.2 6.1 shard_map.252
  307.3 0.8 collective-permute-start.2
  308.0 1.4 fusion.8.cot_ref
  309.4 3.1 collective-permute-done.2.other_ref.sqo_ref
  313.2 6.9 shard_map.253
  320.1 0.8 collective-permute-start.3
  320.8 0.7 slice_bitcast_fusion.4
  322.2 11.6 %shard_map.254 = (bf16[272,1536]{1,0:T(8,128)(2,1)}, bf16[272,4480]{1,0:T(8,128)(2,1)}) custom-call(s32[118]{0:T(128)S(1)} %get-tuple-element.196._.where, bf16[144,1536,128]{2,1,0:T(8,128)(2,1)} %bitcast.81, f32[6,1536]{1,0:T(8,128)} %bitcast_add_fusion.mod_ref, f32[272,1536]{1,0:T(8,128)} %fusion.8.cot_ref), custom_call_target="tpu_custom_call" | custom-call | tf_op jit(solution)/shard_map/pallas_call | solution.py:1018
  333.8 0.7 copy.50
  335.7 1.3 pad_bitcast_fusion.4.refs_2_
  337.0 1.4 pad_bitcast_fusion.3.refs_6_
  338.4 19.0 %shard_map.255 = (f32[272,1536]{1,0:T(8,128)}, bf16[272,1536]{1,0:T(8,128)(2,1)}, bf16[35,272,128]{2,1,0:T(8,128)(2,1)}, bf16[35,272,128]{2,1,0:T(8,128)(2,1)}, ...) custom-call(s32[118]{0:T(128)S(1)} %get-tuple-element.196._.where, bf16[144,1536,128]{2,1,0:T(8,128)(2,1)} %bitcast.82, ...), custom_call_target="tpu_custom_call" | custom-call | tf_op jit(solution)/shard_map/pallas_call | solution.py:1018
  357.4 1.3 collective-permute-start.4
  358.8 1.5 fusion.26
  360.2 11.8 %shard_map.256.y3.refs_20_ = bf16[272,1536]{1,0:T(8,128)(2,1)} custom-call(s32[118]{0:T(128)S(1)} %get-tuple-element.196._.where, bf16[144,1536,128]{2,1,0:T(8,128)(2,1)} %bitcast.83, bf16[35,272,128]{2,1,0:T(8,128)(2,1)} %get-tuple-element.123.hidden_ref.refs_16_), custom_call_target="tpu_custom_call" | custom-call | tf_op jit(solution)/shard_map/pallas_call | solution.py:1018
  372.1 0.9 copy.52
  373.0 1.4 pad_bitcast_fusion.2.refs_5_
  374.4 1.0 collective-permute-done.4.other_ref
  375.4 0.9 copy-done.22
  376.3 13.2 %shard_map.257 = (f32[272,1536]{1,0:T(8,128)}, bf16[272,1536]{1,0:T(8,128)(2,1)}, f32[272,768]{1,0:T(8,128)}, f32[512,768]{1,0:T(8,128)}, bf16[6,512,128]{2,1,0:T(8,128)(2,1)}, /*index=5*/f32[272,128]{1,0:T(8,128)}) custom-call(s32[118]{0:T(128)S(1)} %get-tuple-element.196._.where, f32[272,1536]{1,0:T(8,128)} %fusion.8.cot_ref, ...), custom_call_target="tpu_custom_call" | custom-call | tf_op jit(solution)/shard_map/pallas_call | solution.py:1018
  389.5 1.0 collective-permute-start.5
  390.5 0.8 slice.114
  391.4 1.5 gather_fusion
  393.1 1.7 collective-permute-done.5.sumo_ref
  395.4 6.4 shard_map.258
  401.9 1.0 collective-permute-start.6
  403.8 1.3 pad_bitcast_fusion.1.refs_4_
  405.1 7.1 shard_map.259
  412.2 5.5 collective-permute-done.6.other_ref
  417.7 0.8 slice.118
  418.6 14.5 %shard_map.260 = (f32[272,1536]{1,0:T(8,128)}, bf16[272,1536]{1,0:T(8,128)(2,1)}, f32[2,272,768]{2,1,0:T(8,128)}, bf16[6,272,128]{2,1,0:T(8,128)(2,1)}, f32[272,128]{1,0:T(8,128)}, /*index=5*/f32[2,1536]{1,0:T(2,128)}) custom-call(s32[118]{0:T(128)S(1)} %get-tuple-element.196._.where, f32[272,1536]{1,0:T(8,128)} %get-tuple-element.128.dx_in, ...), custom_call_target="tpu_custom_call" | custom-call | tf_op jit(solution)/shard_map/pallas_call | solution.py:1018
  433.2 1.7 copy.54
  434.9 0.9 collective-permute-start.7
  435.7 1.3 pad_bitcast_fusion.refs_1_
  437.1 2.9 collective-permute-done.7.sumo_ref
  440.7 9.9 %shard_map.261 = (bf16[6,272,128]{2,1,0:T(8,128)(2,1)}, bf16[6,272,128]{2,1,0:T(8,128)(2,1)}, f32[8,768]{1,0:T(8,128)}, bf16[272,1536]{1,0:T(8,128)(2,1)}, f32[2,1536]{1,0:T(2,128)}) custom-call(s32[118]{0:T(128)S(1)} %get-tuple-element.196._.where, f32[272,1536]{1,0:T(8,128)} %fusion.6.rows_ref.refs_17_, f32[2,272,768]{2,1,0:T(8,128)} %get-tuple-element.94.pre_ref, ...), custom_call_target="tpu_custom_call" | custom-call | tf_op jit(solution)/shard_map/pallas_call | solution.py:1018
  450.6 0.8 concatenate.30
  452.1 0.7 reshape.178
  453.1 0.9 fusion.9.refs_23_
  454.1 1.0 copy-done.11
  455.1 1.0 copy-done.12
  456.1 276.6 %shard_map.262 = (bf16[2,9,1536,128]{3,2,1,0:T(8,128)(2,1)}, f32[328,128]{1,0:T(8,128)S(1)}, bf16[272,1536]{1,0:T(8,128)(2,1)S(1)}, f32[272,1536]{1,0:T(8,128)},...) custom-call(s32[144]{0:T(256)S(1)} %gather_fusion, ...), custom_call_target="tpu_custom_call" | custom-call | tf_op jit(solution)/shard_map/pallas_call | solution.py:800
  732.7 0.9 slice_select_fusion.1
  733.6 2.5 slice_select_fusion
  736.2 0.7 multiply_subtract_fusion
  736.9 20.8 %shard_map.263 = (f32[1,9,1536,128]{3,2,1,0:T(8,128)}, f32[1,9,1536,128]{3,2,1,0:T(8,128)}, f32[1,9,1536,128]{3,2,1,0:T(8,128)}) custom-call(f32[9]{0:T(128)S(1)} %copy-done.15, s32[9]{0:T(128)S(1)} %compare_convert_fusion.fill_ref, bf16[2,9,1536,128]{3,2,1,0:T(8,128)(2,1)} %get-tuple-element.166.grads, f32[1,9,1536,128]{3,2,1,0:T(8,128)} %weight.1, ...), custom_call_target="tpu_custom_call" | custom-call | tf_op jit(solution)/shard_map/pallas_call | solution.py:915
  757.7 1.0 multiply_subtract_fusion.1
  (153 shorter events, 15.2 us)
Async XLA Ops:
  0.6 254.4 %copy-start = (f32[16,6,1536]{2,0,1:T(8,128)S(1)}, f32[16,6,1536]{2,0,1:T(8,128)}, u32[]{:S(2)}) copy-start(f32[16,6,1536]{2,0,1:T(8,128)} %param.23) | copy-start | bytes 1769476
  0.7 4.2 copy-start.29
  0.7 4.3 copy-start.44
  0.7 5.0 copy-start.30
  3.0 0.7 copy-start.46
  3.8 2.1 copy-start.14
  5.9 3.9 copy-start.6
  250.6 1.1 copy-start.2
  251.7 0.6 copy-start.13
  252.4 3.6 copy-start.18
  265.2 6.0 collective-permute-start
  271.2 0.7 copy-start.27
  280.2 20.1 %collective-permute-start.1 = (bf16[272,1536]{1,0:T(8,128)(2,1)}, bf16[272,1536]{1,0:T(8,128)(2,1)S(1)}, u32[]{:S(2)}, u32[]{:S(2)}) collective-permute-start(bf16[272,1536]{1,0:T(8,128)(2,1)} %get-tuple-element.99.part_ref), channel_id=1, source_target_pairs={{0,8},{2,10},{4,12},{6,14},{8,0},{10,2},{12,4},{14,6},{16,24},{18,... | collective-permute-start | bytes 2506760 | tf_op jit(solution)/shard_map/ppermute | solution.py:111
  284.7 8.0 %copy-start.3 = (bf16[512,1536]{1,0:T(8,128)(2,1)S(1)}, bf16[512,1536]{1,0:T(8,128)(2,1)}, u32[]{:S(2)}) copy-start(bf16[512,1536]{1,0:T(8,128)(2,1)} %copy-done.2) | copy-start | bytes 4718596
  300.3 0.9 copy-start.23
  301.2 6.9 copy-start.20
  301.2 6.9 copy-start.21
  307.3 5.3 collective-permute-start.2
  312.5 0.7 copy-start.28
  320.1 18.3 %collective-permute-start.3 = (bf16[272,1536]{1,0:T(8,128)(2,1)}, bf16[272,1536]{1,0:T(8,128)(2,1)}, u32[]{:S(2)}, u32[]{:S(2)}) collective-permute-start(bf16[272,1536]{1,0:T(8,128)(2,1)} %get-tuple-element.115.part_ref), channel_id=1, source_target_pairs={{0,8},{2,10},{4,12},{6,14},{8,0},{10,2},{12,4},{14,6},{16,24},{18,... | collective-permute-start | bytes 2506760 | tf_op jit(solution)/shard_map/ppermute | solution.py:111
  322.2 11.6 %copy-start.24 = (bf16[272,1536]{1,0:T(8,128)(2,1)S(1)}, bf16[272,1536]{1,0:T(8,128)(2,1)}, u32[]{:S(2)}) copy-start(bf16[272,1536]{1,0:T(8,128)(2,1)} %get-tuple-element.117) | copy-start | bytes 2506756
  333.8 1.2 copy-start.16
  338.4 20.4 %copy-start.45 = (s32[144]{0:T(256)S(1)}, s32[144]{0:T(256)}, u32[]{:S(2)}) copy-start(s32[144]{0:T(256)} %get-tuple-element.191) | copy-start | bytes 1732
  357.4 18.0 %collective-permute-start.4 = (bf16[272,1536]{1,0:T(8,128)(2,1)}, bf16[272,1536]{1,0:T(8,128)(2,1)S(1)}, u32[]{:S(2)}, u32[]{:S(2)}) collective-permute-start(bf16[272,1536]{1,0:T(8,128)(2,1)} %get-tuple-element.122.part_ref.da2), channel_id=1, source_target_pairs={{0,8},{2,10},{4,12},{6,14},{8,0},{10,2},{12,4},{14,6},{16,24},{18,... | collective-permute-start | bytes 2506760 | tf_op jit(solution)/shard_map/ppermute | solution.py:111
  360.2 11.8 %copy-start.25 = (bf16[272,1536]{1,0:T(8,128)(2,1)S(1)}, bf16[272,1536]{1,0:T(8,128)(2,1)}, u32[]{:S(2)}) copy-start(bf16[272,1536]{1,0:T(8,128)(2,1)} %get-tuple-element.124) | copy-start | bytes 2506756
  375.4 0.9 copy-start.22
  376.3 16.7 %copy-start.47 = (s32[144]{0:T(256)S(1)}, s32[144]{0:T(256)}, u32[]{:S(2)}) copy-start(s32[144]{0:T(256)} %copy-done.46) | copy-start | bytes 1732
  389.5 5.3 collective-permute-start.5
  394.8 0.6 copy-start.32
  395.4 7.5 copy-start.40
  395.4 7.5 copy-start.41
  395.4 7.5 copy-start.42
  395.4 7.6 %copy-start.17 = (bf16[272,1536]{1,0:T(8,128)(2,1)S(1)}, bf16[272,1536]{1,0:T(8,128)(2,1)}, u32[]{:S(2)}) copy-start(bf16[272,1536]{1,0:T(8,128)(2,1)} %get-tuple-element.134.dy2) | copy-start | bytes 2506756
  401.9 15.8 %collective-permute-start.6 = (bf16[272,1536]{1,0:T(8,128)(2,1)}, bf16[272,1536]{1,0:T(8,128)(2,1)S(1)}, u32[]{:S(2)}, u32[]{:S(2)}) collective-permute-start(bf16[272,1536]{1,0:T(8,128)(2,1)} %get-tuple-element.133.da3.part_ref), channel_id=1, source_target_pairs={{0,8},{2,10},{4,12},{6,14},{8,0},{10,2},{12,4},{14,6},{16,24},{18,... | collective-permute-start | bytes 2506760 | tf_op jit(solution)/shard_map/ppermute | solution.py:111
  405.1 7.1 copy-start.39
  417.7 1.0 copy-start.26
  433.1 1.7 copy-start.33
  433.2 2.6 copy-start.43
  434.9 5.1 collective-permute-start.7
  440.0 0.7 copy-start.34
  440.7 10.0 %slice-start = ((f32[11,1536]{1,0:T(8,128)}), f32[3,1536]{1,0:T(4,128)S(1)}, s32[]{:S(2)}) async-start(f32[11,1536]{1,0:T(8,128)} %shard_map.259), calls=%async_computation | async-start | bytes 49152 | tf_op jit(solution)/shard_map/slice | solution.py:1848
  440.7 13.3 %copy-start.5 = (bf16[6,272,128]{2,1,0:T(8,128)(2,1)S(1)}, bf16[6,272,128]{2,1,0:T(8,128)(2,1)}, u32[]{:S(2)}) copy-start(bf16[6,272,128]{2,1,0:T(8,128)(2,1)} %get-tuple-element.147.dv_ref.refs_9_) | copy-start | bytes 1253380
  440.7 13.3 %copy-start.7 = (bf16[6,512,128]{2,1,0:T(8,128)(2,1)S(1)}, bf16[6,512,128]{2,1,0:T(8,128)(2,1)}, u32[]{:S(2)}) copy-start(bf16[6,512,128]{2,1,0:T(8,128)(2,1)} %get-tuple-element.153.refs_12_) | copy-start | bytes 2359300
  440.7 13.3 %copy-start.8 = (bf16[6,272,128]{2,1,0:T(8,128)(2,1)S(1)}, bf16[6,272,128]{2,1,0:T(8,128)(2,1)}, u32[]{:S(2)}) copy-start(bf16[6,272,128]{2,1,0:T(8,128)(2,1)} %get-tuple-element.151.refs_10_) | copy-start | bytes 1253380
  440.7 13.3 %copy-start.9 = (bf16[6,272,128]{2,1,0:T(8,128)(2,1)S(1)}, bf16[6,272,128]{2,1,0:T(8,128)(2,1)}, u32[]{:S(2)}) copy-start(bf16[6,272,128]{2,1,0:T(8,128)(2,1)} %get-tuple-element.154.refs_14_) | copy-start | bytes 1253380
  440.7 13.3 %copy-start.10 = (bf16[6,272,128]{2,1,0:T(8,128)(2,1)S(1)}, bf16[6,272,128]{2,1,0:T(8,128)(2,1)}, u32[]{:S(2)}) copy-start(bf16[6,272,128]{2,1,0:T(8,128)(2,1)} %get-tuple-element.152.refs_11_) | copy-start | bytes 1253380
  450.6 3.4 copy-start.4
  454.0 1.0 copy-start.11
  455.0 1.0 copy-start.12
  733.6 2.6 copy-start.19
  733.6 2.6 copy-start.35
  733.6 2.6 copy-start.36
  733.6 3.3 copy-start.15
  736.9 20.8 %copy-start.31 = (f32[1,12160]{1,0:T(1,128)S(1)}, f32[1,12160]{1,0:T(1,128)}, u32[]{:S(2)}) copy-start(f32[1,12160]{1,0:T(1,128)} %param.27) | copy-start | bytes 145924
  736.9 20.8 %copy-start.37 = (f32[1,12160]{1,0:T(1,128)S(1)}, f32[1,12160]{1,0:T(1,128)}, u32[]{:S(2)}) copy-start(f32[1,12160]{1,0:T(1,128)} %param.28) | copy-start | bytes 145924
  736.9 20.8 %copy-start.38 = (f32[1,12160]{1,0:T(1,128)S(1)}, f32[1,12160]{1,0:T(1,128)}, u32[]{:S(2)}) copy-start(f32[1,12160]{1,0:T(1,128)} %param.29) | copy-start | bytes 145924
  736.9 21.8 %copy-start.1 = (f32[16,6,1536]{2,0,1:T(8,128)S(1)}, f32[16,6,1536]{2,0,1:T(8,128)}, u32[]{:S(2)}) copy-start(f32[16,6,1536]{2,0,1:T(8,128)} %param.23) | copy-start | bytes 1769476
where the time goes:
time: 769 us; the launch traced here: 759 us
  Pallas kernels  670 us (87%)
  local copies, waits for them, and re-layouts  39.7 us (5%)
  waiting for transfers between devices  23 us (3%)
  other arithmetic  16.8 us (2%)
    pallas_call x1, Pallas kernels, reduce_slots(): pl.pallas_call(reduce_kernel, out_shape=[jax.ShapeDtypeStruct((2, slot_co...  277 us
    pallas_call x1, Pallas kernels, gather_slots(): pl.pallas_call(gather_kernel, out_shape=[jax.ShapeDtypeStruct((16,) + sca...  241 us
    pallas_call x13, Pallas kernels, call(): pl.pallas_call(body, grid_spec=pltpu.PrefetchScalarGridSpec(num_scalar_pr...  131 us
    ppermute x8, waiting for transfers between devices, pair_swap(): return lax.ppermute(value, 'dp', [(i, i ^ 4) for i in range(16)])  23 us
    pallas_call x1, Pallas kernels, adam_slots(): pl.pallas_call(step, grid=(slot_count,), in_specs=[scalars, scalars, pl.B...  20.8 us
  transfers between devices with their start and end apart: 8, of which 7 were waited for; matrix products, arithmetic and copies ran while one was open for 3% of the time, Pallas kernels for 5%

commit v1 on v0

--- a/solution.py
+++ b/solution.py
@@ -421,9 +421,9 @@
     (
         *pieces, rows_in, after_in, dx_in, y_in, da_in, gains, vec_in,
         final, vec_out, result, result_grad, y_other, da_other, from_sib, from_x, from_y, corner_a, corner_b,
-        left, right, ring, corners, side_x, side_y, middle, stage, vec_box,
+        left, right, ring, corners, side_x, side_y, middle, stage, vec_box, end_wide, end_low,
         load_s, stage_s, sib_s, sib_r, x_s, x_r, y_s, y_r, ca_s, ca_r, cb_s, cb_r, f_s, f_r, v_s, v_r,
-        end_s, end_r,
+        end_s, end_r, end_load,
     ) = refs
     chip, core, z, y, x = place_of()
     rank = z % 2
@@ -443,9 +443,12 @@
 
     kinds = left.shape[0]
     depth = right.shape[1]
-    loads = [
-        pltpu.make_async_copy(pieces[i], left.at[i], load_s.at[i]) for i in range(kinds)
-    ]
+    loads = []
+    for i in range(kinds):
+        columns = pieces[i].shape[1]
+        loads.append(
+            pltpu.make_async_copy(pieces[i], left.at[i, :, pl.ds(0, columns)], load_s.at[i])
+        )
     first = 0
     blank = []
     for i, piece in enumerate(pieces[kinds:]):
@@ -470,6 +473,12 @@
 
         lax.fori_loop(0, number, clear, 0)
     right[first] = jnp.zeros((depth, lanes), right.dtype)
+    for i in range(kinds):
+        columns = pieces[i].shape[1]
+        if columns < depth:
+            left[i, :, pl.ds(columns, depth - columns)] = jnp.zeros(
+                (width, depth - columns), left.dtype
+            )
     vec_out[...] = vec_in[...]
     greet(chip, core, z, y, x)
     for load in loads:
@@ -555,12 +564,7 @@
     def stays(s):
         return jnp.logical_and(s >= turns - batches, rank == core)
 
-    def staged(source, place, i):
-        copy = pltpu.make_async_copy(source, place, stage_s.at[i])
-        copy.start()
-        return copy
-
-    def for_sibling(s):
+    def for_sibling(s, low, high):
         def one(q, carry):
             @pl.when(s >= 1)
             def _():
@@ -570,76 +574,90 @@
             sib_copy(q, s).start()
             return carry
 
-        lax.fori_loop(0, 4, one, 0)
+        lax.fori_loop(low, high, one, 0)
+
+    def fetched(q, s):
+        i = 2 * q + s % 2
+        return pltpu.make_async_copy(from_sib.at[turns * q + s], stage.at[i], stage_s.at[i])
+
+    def fetch(q, s):
+        sib_copy(q, s).wait_recv()
+        fetched(q, s).start()
+
+    def taken(q, s):
+        return stage.at[2 * q + s % 2]
 
     def corner(s):
-        sib_copy(0, s).wait_recv()
-        in_sib = staged(from_sib.at[s], stage.at[0], 0)
-
         @pl.when(s >= deep)
         def _():
             a_copy(s - deep).wait_send()
             b_copy(s - deep).wait_send()
 
-        in_sib.wait()
-        sums(0, s, mine, (stage.at[0],), corners.at[s % deep])
+        fetched(0, s).wait()
+        sums(0, s, mine, (taken(0, s),), corners.at[s % deep])
         a_copy(s).start()
         b_copy(s).start()
 
     def direct_sides(s):
-        sib_copy(1, s).wait_recv()
-        in_x = staged(from_sib.at[turns + s], stage.at[0], 0)
-        sib_copy(2, s).wait_recv()
-        in_y = staged(from_sib.at[2 * turns + s], stage.at[1], 1)
-
         @pl.when(s >= deep)
         def _():
             for n in range(2):
                 x_copy(s - deep, n).wait_send()
                 y_copy(s - deep, n).wait_send()
 
-        in_x.wait()
-        sums(1, s, mine, (sub(stage.at[0], 0),), sub(side_x.at[s % deep], 0))
+        fetched(1, s).wait()
+        sums(1, s, mine, (sub(taken(1, s), 0),), sub(side_x.at[s % deep], 0))
         x_copy(s, 0).start()
-        in_y.wait()
-        sums(2, s, mine + part, (sub(stage.at[1], part),), sub(side_y.at[s % deep], part))
+        fetched(2, s).wait()
+        sums(2, s, mine + part, (sub(taken(2, s), part),), sub(side_y.at[s % deep], part))
         y_copy(s, 0).start()
 
+    def relayed(s):
+        return (
+            pltpu.make_async_copy(corner_b.at[s], sub(stage.at[8], 0), stage_s.at[8]),
+            pltpu.make_async_copy(corner_a.at[s], sub(stage.at[8], part), stage_s.at[9]),
+        )
+
+    def relayed_in(s):
+        b_copy(s).wait_recv()
+        relayed(s)[0].start()
+        a_copy(s).wait_recv()
+        relayed(s)[1].start()
+
     def relayed_sides(s):
-        b_copy(s).wait_recv()
-        in_b = staged(corner_b.at[s], sub(stage.at[2], 0), 2)
-        a_copy(s).wait_recv()
-        in_a = staged(corner_a.at[s], sub(stage.at[2], part), 3)
-        in_b.wait()
+        relayed(s)[0].wait()
         sums(
-            1, s, mine + part, (sub(stage.at[0], part), sub(stage.at[2], 0)),
+            1, s, mine + part, (sub(taken(1, s), part), sub(stage.at[8], 0)),
             sub(side_x.at[s % deep], part),
         )
         x_copy(s, 1).start()
-        in_a.wait()
+        relayed(s)[1].wait()
         sums(
-            2, s, mine, (sub(stage.at[1], 0), sub(stage.at[2], part)), sub(side_y.at[s % deep], 0)
+            2, s, mine, (sub(taken(2, s), 0), sub(stage.at[8], part)), sub(side_y.at[s % deep], 0)
         )
         y_copy(s, 1).start()
 
+    def centre_terms(s):
+        return (
+            pltpu.make_async_copy(from_x.at[s], stage.at[9], stage_s.at[10]),
+            pltpu.make_async_copy(from_y.at[s], stage.at[10], stage_s.at[11]),
+        )
+
+    def centre_in(s):
+        for n, copies in enumerate((x_copy, y_copy)):
+            copies(s, 0).wait_recv()
+            copies(s, 1).wait_recv()
+            centre_terms(s)[n].start()
+
     def centre(s):
-        sib_copy(3, s).wait_recv()
-        in_sib = staged(from_sib.at[3 * turns + s], stage.at[3], 4)
-        x_copy(s, 0).wait_recv()
-        x_copy(s, 1).wait_recv()
-        in_x = staged(from_x.at[s], stage.at[4], 5)
-        y_copy(s, 0).wait_recv()
-        y_copy(s, 1).wait_recv()
-        in_y = staged(from_y.at[s], stage.at[5], 6)
-
         @pl.when(s >= deep)
         def _():
             f_copy(s - deep)[0].wait_send()
 
-        in_sib.wait()
-        in_x.wait()
-        in_y.wait()
-        sums(3, s, mine, (stage.at[3], stage.at[4], stage.at[5]), middle.at[s % deep])
+        fetched(3, s).wait()
+        for term in centre_terms(s):
+            term.wait()
+        sums(3, s, mine, (taken(3, s), stage.at[9], stage.at[10]), middle.at[s % deep])
         go, here = f_copy(s)
 
         @pl.when(stays(s))
@@ -655,28 +673,51 @@
     ends = [
         remote(y_in, y_other, end_s.at[0], end_r.at[0], pair_device),
         remote(da_in, da_other, end_s.at[1], end_r.at[1], pair_device),
-        remote(result, result, end_s.at[2], end_r.at[2], sibling),
-        remote(result_grad, result_grad, end_s.at[3], end_r.at[3], sibling),
+        remote(end_low.at[0], result, end_s.at[2], end_r.at[2], sibling),
+        remote(end_wide.at[0], result_grad, end_s.at[3], end_r.at[3], sibling),
     ]
+    end_loads = [
+        pltpu.make_async_copy(src, dst, end_load.at[i])
+        for i, (src, dst) in enumerate(
+            (
+                (rows_in, end_wide.at[0]), (after_in, end_wide.at[1]), (dx_in, end_wide.at[2]),
+                (y_in, end_low.at[0]), (da_in, end_low.at[1]),
+                (y_other, end_low.at[2]), (da_other, end_low.at[3]),
+            )
+        )
+    ]
+    end_stores = [
+        pltpu.make_async_copy(end_low.at[0], result, end_load.at[7]),
+        pltpu.make_async_copy(end_wide.at[0], result_grad, end_load.at[8]),
+    ]
 
     def finish_rows():
-        ends[0].wait_recv()
-        ends[1].wait_recv()
+        for n in range(2):
+            ends[n].wait_recv()
+            end_loads[5 + n].start()
+        for load in end_loads:
+            load.wait()
         tall = 16
-        spec = pl.BlockSpec((tall, width), lambda i: (i, 0))
-
-        def one(x_ref, x2_ref, dx_ref, y_ref, yo_ref, da_ref, dao_ref, out_ref, grad_ref):
-            y_all = y_ref[...].astype(F32) + yo_ref[...].astype(F32) + gains[2:3]
-            out_ref[...] = (x2_ref[...] + gains[0:1] * y_all).astype(out_ref.dtype)
-            da = da_ref[...].astype(F32) + dao_ref[...].astype(F32)
-            back, _ = normed_back(x_ref[...], da * (1.0 + gains[1:2]))
-            grad_ref[...] = dx_ref[...] + back
-
-        pltpu.emit_pipeline(
-            one, grid=(rows_in.shape[0] // tall,), in_specs=[spec] * 7, out_specs=[spec] * 2
-        )(rows_in, after_in, dx_in, y_in, y_other, da_in, da_other, result, result_grad)
+
+        def one(i, carry):
+            at = pl.ds(pl.multiple_of(i * tall, tall), tall)
+            y_all = end_low[0, at].astype(F32) + end_low[2, at].astype(F32) + gains[2:3]
+            end_low[0, at] = (end_wide[1, at] + gains[0:1] * y_all).astype(end_low.dtype)
+            da = end_low[1, at].astype(F32) + end_low[3, at].astype(F32)
+            back, _ = normed_back(end_wide[0, at], da * (1.0 + gains[1:2]))
+            end_wide[0, at] = end_wide[2, at] + back
+            return carry
+
+        lax.fori_loop(0, rows_in.shape[0] // tall, one, 0)
         ends[2].start()
         ends[3].start()
+        for store in end_stores:
+            store.start()
+
+    @pl.when(home)
+    def _():
+        for load in end_loads[:5]:
+            load.start()
 
     @pl.when(jnp.logical_not(home))
     def _():
@@ -693,24 +734,38 @@
             def _():
                 vec_copy(i).start()
 
+        @pl.when(step + 1 < turns)
+        def _():
+            for_sibling(step + 1, 0, 4)
+
         @pl.when(step < turns)
         def _():
-            corner(step)
-            direct_sides(step)
+            relayed_in(step)
+
+        @pl.when(step >= 1)
+        def _():
+            centre_in(step - 1)
 
         @pl.when(step + 1 < turns)
         def _():
-            for_sibling(step + 1)
+            for q in range(3):
+                fetch(q, step + 1)
+
+        @pl.when(step < turns)
+        def _():
+            relayed_sides(step)
 
         @pl.when(step >= 1)
         def _():
             centre(step - 1)
 
-        @pl.when(step < turns)
-        def _():
-            relayed_sides(step)
-
-        @pl.when(jnp.logical_and(step == turns - batches, home))
+        @pl.when(step + 1 < turns)
+        def _():
+            fetch(3, step + 1)
+            corner(step + 1)
+            direct_sides(step + 1)
+
+        @pl.when(jnp.logical_and(step == 3, home))
         def _():
             finish_rows()
 
@@ -723,7 +778,13 @@
 
         return carry
 
-    for_sibling(0)
+    for_sibling(0, 0, 2)
+    fetch(0, 0)
+    corner(0)
+    for_sibling(0, 2, 4)
+    for q in range(1, 4):
+        fetch(q, 0)
+    direct_sides(0)
     lax.fori_loop(0, turns + 1, turn, 0)
     for q in range(4):
         sib_copy(q, turns - 1).wait_send()
@@ -748,6 +809,8 @@
     def _():
         ends[2].wait_send()
         ends[3].wait_send()
+        for store in end_stores:
+            store.wait()
 
     @pl.when(jnp.logical_not(home))
     def _():
@@ -776,7 +839,7 @@
         back, _ = normed_back(x, da_all * (1.0 + gains[1]))
         return total[None], lax.psum(vector, ("dp", "tensor")), result, dx + back
     left = rows
-    width, depth = left[0].shape
+    width, depth = left[0].shape[0], max(r.shape[1] for r in rows)
     lanes = columns[0].shape[2]
     tiles = sum(c.shape[0] for c in columns)
     block = jnp.where(holder >= 0, holder, tiles)
@@ -812,19 +875,21 @@
         scratch_shapes=[
             pltpu.VMEM((len(left), width, depth), low),
             pltpu.VMEM((tiles + 1, depth, lanes), low),
-            slab(4), slab(deep), slab(deep), slab(deep), slab(deep), slab(6),
+            slab(4), slab(deep), slab(deep), slab(deep), slab(deep), slab(11),
             pltpu.VMEM((5,) + vector.shape, vector.dtype),
+            pltpu.VMEM((3,) + ends[0].shape, F32),
+            pltpu.VMEM((4,) + ends[0].shape, low),
         ]
         + [
             dma((n,))
-            for n in (len(left) + len(columns), 7)
+            for n in (len(left) + len(columns), 12)
             + (4 * turns,) * 2
             + (2 * turns,) * 4
             + (turns,) * 6
-            + (5, 5, 4, 4)
+            + (5, 5, 4, 4, 9)
         ],
         compiler_params=pltpu.CompilerParams(
-            collective_id=1, has_side_effects=True, vmem_limit_bytes=48 * MIB
+            collective_id=1, has_side_effects=True, vmem_limit_bytes=58 * MIB
         ),
     )(kind, block, *left, *columns, *ends, gains, vector)
     return outs[:4]
@@ -890,36 +955,73 @@
 def adam_slots(planes, master, moment_one, moment_two, slot_scale, filled):
     count, slot_count, width, lanes = planes.shape
 
-    def step(scale_ref, fill_ref, grads, weight, one, two, new_weight, new_one, new_two):
-        slot = pl.program_id(0)
-
-        @pl.when(fill_ref[slot] == 1)
-        def _():
-            total = grads[0, 0].astype(jnp.float32)
-            for n in range(1, count):
-                total = total + grads[n, 0].astype(jnp.float32)
-            results = adam_step(
-                weight[0, 0], total * scale_ref[slot], one[0, 0], two[0, 0], TILE_RATE, TILE_DECAY
-            )
-            for ref, value in zip((new_weight, new_one, new_two), results):
-                ref[0, 0] = value
-
-        @pl.when(fill_ref[slot] == 0)
-        def _():
-            new_weight[...] = weight[...]
-            new_one[...] = one[...]
-            new_two[...] = two[...]
-
-    deep = pl.BlockSpec((1, 1, width, lanes), lambda s: (0, s, 0, 0))
+    def step(scale_ref, fill_ref, grads, weight, one, two, new_weight, new_one, new_two, grad_box, boxes, reads, writes):
+        sources = (weight, one, two)
+        targets = (new_weight, new_one, new_two)
+
+        def load(slot):
+            return [
+                pltpu.make_async_copy(src.at[0, slot], boxes.at[n, slot], reads.at[n, slot])
+                for n, src in enumerate(sources)
+            ] + [
+                pltpu.make_async_copy(
+                    grads.at[n, slot], grad_box.at[n, slot], reads.at[3 + n, slot]
+                )
+                for n in range(count)
+            ]
+
+        def store(slot):
+            return [
+                pltpu.make_async_copy(boxes.at[n, slot], dst.at[0, slot], writes.at[n, slot])
+                for n, dst in enumerate(targets)
+            ]
+
+        def begin(slot, carry):
+            for copy in load(slot):
+                copy.start()
+            return carry
+
+        def work(slot, carry):
+            for copy in load(slot):
+                copy.wait()
+
+            @pl.when(fill_ref[slot] == 1)
+            def _():
+                total = grad_box[0, slot].astype(jnp.float32)
+                for n in range(1, count):
+                    total = total + grad_box[n, slot].astype(jnp.float32)
+                results = adam_step(
+                    boxes[0, slot], total * scale_ref[slot], boxes[1, slot], boxes[2, slot],
+                    TILE_RATE, TILE_DECAY,
+                )
+                for n, value in enumerate(results):
+                    boxes[n, slot] = value
+
+            for copy in store(slot):
+                copy.start()
+            return carry
+
+        def finish(slot, carry):
+            for copy in store(slot):
+                copy.wait()
+            return carry
+
+        for part in (begin, work, finish):
+            lax.fori_loop(0, slot_count, part, 0)
+
     scalars = pl.BlockSpec(memory_space=pltpu.SMEM)
     return pl.pallas_call(
         step,
-        grid=(slot_count,),
-        in_specs=[scalars, scalars, pl.BlockSpec((count, 1, width, lanes), lambda s: (0, s, 0, 0))]
-        + [deep] * 3,
-        out_specs=[deep] * 3,
-        out_shape=[jax.ShapeDtypeStruct(master.shape, jnp.float32)] * 3,
-        compiler_params=pltpu.CompilerParams(vmem_limit_bytes=32 * MIB),
+        in_specs=[scalars, scalars] + [ANY] * 4,
+        out_specs=[ANY] * 3,
+        out_shape=[pltpu.HBM(master.shape, jnp.float32)] * 3,
+        scratch_shapes=[
+            pltpu.VMEM((count, slot_count, width, lanes), planes.dtype),
+            pltpu.VMEM((3, slot_count, width, lanes), jnp.float32),
+            pltpu.SemaphoreType.DMA((3 + count, slot_count)),
+            pltpu.SemaphoreType.DMA((3, slot_count)),
+        ],
+        compiler_params=pltpu.CompilerParams(vmem_limit_bytes=40 * MIB),
     )(
         slot_scale,
         filled.astype(jnp.int32),
@@ -1775,7 +1877,7 @@
         return jnp.pad(rows, ((0, count - tokens), (0, 0))).astype(jnp.float32)
 
     def upright(rows):
-        return jnp.pad(rows, ((0, context.shape[0] - rows.shape[0]), (0, 0))).T
+        return jnp.pad(rows, ((0, -rows.shape[0] % HEAD), (0, 0))).T
 
     def beside(*values):
         return lax.optimization_barrier(values)

time: 769 us -> 763 us (level)
  the two profiles are of different devices: /device:TPU:0 before, /device:TPU:9 now
where the time goes in v1:
time: 763 us; the launch traced here: 755 us
  Pallas kernels  672 us (88%)
  local copies, waits for them, and re-layouts  38.1 us (5%)
  other arithmetic  18.3 us (2%)
  waiting for transfers between devices  15 us (2%)
    pallas_call x1, Pallas kernels, reduce_slots(): pl.pallas_call(reduce_kernel, out_shape=[jax.ShapeDtypeStruct((2, slot_co...  284 us
    pallas_call x1, Pallas kernels, gather_slots(): pl.pallas_call(gather_kernel, out_shape=[jax.ShapeDtypeStruct((16,) + sca...  239 us
    pallas_call x13, Pallas kernels, call(): pl.pallas_call(body, grid_spec=pltpu.PrefetchScalarGridSpec(num_scalar_pr...  131 us
    pallas_call x1, Pallas kernels, adam_slots(): pl.pallas_call(step, in_specs=[scalars, scalars] + [ANY] * 4, out_specs=[...  18.4 us
  transfers between devices with their start and end apart: 8, of which 7 were waited for; matrix products, arithmetic and copies ran while one was open for 3% of the time, Pallas kernels for 5%

profile of v1, /device:TPU:9, one launch (start us, length us, event | category | flops | bytes accessed | tf_op | source)
XLA Modules:
  0.0 754.5 jit_solution(9901841522344629155)
XLA Ops:
  0.7 0.9 convert_reduce_fusion
  3.8 1.0 pad.48.lat
  5.9 3.8 fusion.own
  9.8 238.6 %shard_map.248 = (bf16[16,9,1536,128]{3,2,1,0:T(8,128)(2,1)}, bf16[2,144,1536]{2,1,0:T(8,128)(2,1)S(1)}, bf16[2,144,1536]{2,1,0:T(8,128)(2,1)S(1)}, bf16[512,1536]{1,0:T(8,128)(2,1)S(1)}, f32[104,128]{1,0:T(8,128)S(1)}) custom-call(bf16[9,1536,128]{2,1,0:T(8,128)(2,1)S(1)} %fusion.own, bf16[144,1536]{1,0:T(8,128)(2,1)S(1)} %pad.48.lat, ...), custom_call_target="tpu_custom_call" | custom-call | tf_op jit(solution)/shard_map/pallas_call | solution.py:393
  248.4 1.1 copy-done.2
  251.5 1.4 fusion.6.rows_ref.refs_17_
  252.9 1.0 fusion.15
  254.5 8.5 %shard_map.249 = (bf16[272,1536]{1,0:T(8,128)(2,1)}, f32[2,272,768]{2,1,0:T(8,128)}, bf16[272,768]{1,0:T(8,128)(2,1)}, f32[272,128]{1,0:T(8,128)}) custom-call(s32[118]{0:T(128)S(1)} %get-tuple-element.196._.where, f32[272,1536]{1,0:T(8,128)} %fusion.6.rows_ref.refs_17_, f32[6,1536]{1,0:T(8,128)} %bitcast_add_fusion.mod_ref, f32[10,768]{1,0:T(8,128)} %reshape.175.vec_ref, ...), custom_call_target="tpu_custom_call" | custom-call | tf_op jit(solution)/shard_map/pallas_call | solution.py:1120
  263.1 1.3 collective-permute-start
  266.9 1.5 collective-permute-done.other_ref.sqo_ref
  269.1 8.3 %shard_map.250 = (bf16[272,768]{1,0:T(8,128)(2,1)}, bf16[272,768]{1,0:T(8,128)(2,1)}, bf16[6,272,128]{2,1,0:T(8,128)(2,1)}, bf16[272,1536]{1,0:T(8,128)(2,1)}) custom-call(s32[118]{0:T(128)S(1)} %get-tuple-element.196._.where, f32[2,272,768]{2,1,0:T(8,128)} %get-tuple-element.94.pre_ref, bf16[272,768]{1,0:T(8,128)(2,1)} %get-tuple-element.95.value_ref.v_ref, ...), custom_call_target="tpu_custom_call" | custom-call | tf_op jit(solution)/shard_map/pallas_call | solution.py:1120
  277.4 1.0 collective-permute-start.1
  278.5 1.6 copy.49
  280.1 1.2 pad_bitcast_fusion.5.refs_0_
  281.3 1.0 slice_bitcast_fusion.1
  282.3 7.9 %shard_map.251 = (f32[512,768]{1,0:T(8,128)}, bf16[512,768]{1,0:T(8,128)(2,1)}, f32[512,128]{1,0:T(8,128)}) custom-call(s32[118]{0:T(128)S(1)} %get-tuple-element.196._.where, bf16[512,1536]{1,0:T(8,128)(2,1)} %copy-done.2, f32[10,768]{1,0:T(8,128)} %reshape.175.vec_ref, bf16[144,1536,128]{2,1,0:T(8,128)(2,1)} %bitcast.63, bf16[144,1536,128]{2,1,0:T(8,128)(2,1)} %bitcast.64, ...), custom_call_target="tpu_custom_call" | custom-call | tf_op jit(solution)/shard_map/pallas_call | solution.py:1120
  290.2 1.7 copy.48
  291.9 4.9 collective-permute-done.1.other_ref
  296.8 0.9 copy-done.15
  297.7 6.2 shard_map.252
  303.9 0.7 collective-permute-start.2
  304.6 1.4 fusion.8.cot_ref
  306.0 2.0 collective-permute-done.2.other_ref.sqo_ref
  308.6 6.8 shard_map.253
  315.5 0.7 collective-permute-start.3
  316.2 0.7 slice_bitcast_fusion.4
  317.6 11.6 %shard_map.254 = (bf16[272,1536]{1,0:T(8,128)(2,1)}, bf16[272,4480]{1,0:T(8,128)(2,1)}) custom-call(s32[118]{0:T(128)S(1)} %get-tuple-element.196._.where, bf16[144,1536,128]{2,1,0:T(8,128)(2,1)} %bitcast.81, f32[6,1536]{1,0:T(8,128)} %bitcast_add_fusion.mod_ref, f32[272,1536]{1,0:T(8,128)} %fusion.8.cot_ref), custom_call_target="tpu_custom_call" | custom-call | tf_op jit(solution)/shard_map/pallas_call | solution.py:1120
  329.2 0.7 copy.50
  331.1 1.2 pad_bitcast_fusion.4.refs_2_
  332.2 1.2 pad_bitcast_fusion.3.refs_6_
  333.5 19.1 %shard_map.255 = (f32[272,1536]{1,0:T(8,128)}, bf16[272,1536]{1,0:T(8,128)(2,1)}, bf16[35,272,128]{2,1,0:T(8,128)(2,1)}, bf16[35,272,128]{2,1,0:T(8,128)(2,1)}, ...) custom-call(s32[118]{0:T(128)S(1)} %get-tuple-element.196._.where, bf16[144,1536,128]{2,1,0:T(8,128)(2,1)} %bitcast.82, ...), custom_call_target="tpu_custom_call" | custom-call | tf_op jit(solution)/shard_map/pallas_call | solution.py:1120
  352.5 0.8 collective-permute-start.4
  353.3 1.5 fusion.26
  354.8 11.8 %shard_map.256.y3.refs_20_ = bf16[272,1536]{1,0:T(8,128)(2,1)} custom-call(s32[118]{0:T(128)S(1)} %get-tuple-element.196._.where, bf16[144,1536,128]{2,1,0:T(8,128)(2,1)} %bitcast.83, bf16[35,272,128]{2,1,0:T(8,128)(2,1)} %get-tuple-element.123.hidden_ref.refs_16_), custom_call_target="tpu_custom_call" | custom-call | tf_op jit(solution)/shard_map/pallas_call | solution.py:1120
  366.6 0.9 copy.52
  367.5 1.1 pad_bitcast_fusion.2.refs_5_
  369.4 0.9 copy-done.14
  370.2 13.2 %shard_map.257 = (f32[272,1536]{1,0:T(8,128)}, bf16[272,1536]{1,0:T(8,128)(2,1)}, f32[272,768]{1,0:T(8,128)}, f32[512,768]{1,0:T(8,128)}, bf16[6,512,128]{2,1,0:T(8,128)(2,1)}, /*index=5*/f32[272,128]{1,0:T(8,128)}) custom-call(s32[118]{0:T(128)S(1)} %get-tuple-element.196._.where, f32[272,1536]{1,0:T(8,128)} %fusion.8.cot_ref, ...), custom_call_target="tpu_custom_call" | custom-call | tf_op jit(solution)/shard_map/pallas_call | solution.py:1120
  383.5 0.9 collective-permute-start.5
  384.4 3.2 collective-permute-done.5.sumo_ref
  388.2 6.4 shard_map.258
  394.7 0.9 collective-permute-start.6
  395.7 0.8 slice.114
  396.5 2.1 gather_fusion
  400.2 1.1 pad_bitcast_fusion.1.refs_4_
  401.3 7.2 shard_map.259
  408.5 1.0 collective-permute-done.6.other_ref
  409.5 0.8 slice.118
  410.3 14.5 %shard_map.260 = (f32[272,1536]{1,0:T(8,128)}, bf16[272,1536]{1,0:T(8,128)(2,1)}, f32[2,272,768]{2,1,0:T(8,128)}, bf16[6,272,128]{2,1,0:T(8,128)(2,1)}, f32[272,128]{1,0:T(8,128)}, /*index=5*/f32[2,1536]{1,0:T(2,128)}) custom-call(s32[118]{0:T(128)S(1)} %get-tuple-element.196._.where, f32[272,1536]{1,0:T(8,128)} %get-tuple-element.128.dx_in, ...), custom_call_target="tpu_custom_call" | custom-call | tf_op jit(solution)/shard_map/pallas_call | solution.py:1120
  424.9 1.7 copy.54
  426.6 1.1 collective-permute-start.7
  427.7 1.1 pad_bitcast_fusion.refs_1_
  428.8 1.7 collective-permute-done.7.sumo_ref
  431.2 9.8 %shard_map.261 = (bf16[6,272,128]{2,1,0:T(8,128)(2,1)}, bf16[6,272,128]{2,1,0:T(8,128)(2,1)}, f32[8,768]{1,0:T(8,128)}, bf16[272,1536]{1,0:T(8,128)(2,1)}, f32[2,1536]{1,0:T(2,128)}) custom-call(s32[118]{0:T(128)S(1)} %get-tuple-element.196._.where, f32[272,1536]{1,0:T(8,128)} %fusion.6.rows_ref.refs_17_, f32[2,272,768]{2,1,0:T(8,128)} %get-tuple-element.94.pre_ref, ...), custom_call_target="tpu_custom_call" | custom-call | tf_op jit(solution)/shard_map/pallas_call | solution.py:1120
  441.0 0.8 concatenate.30
  441.8 0.7 reshape.178
  443.5 284.1 %shard_map.262 = (bf16[2,9,1536,128]{3,2,1,0:T(8,128)(2,1)}, f32[328,128]{1,0:T(8,128)}, bf16[272,1536]{1,0:T(8,128)(2,1)}, f32[272,1536]{1,0:T(8,128)}, bf16[27...) custom-call(s32[144]{0:T(256)} %gather_fusion, ...), custom_call_target="tpu_custom_call" | custom-call | tf_op jit(solution)/shard_map/pallas_call | solution.py:863
  727.5 0.9 slice.125
  728.4 0.9 slice.126
  729.3 2.0 slice_select_fusion.1
  731.3 2.5 slice_select_fusion
  733.9 0.7 multiply_subtract_fusion
  734.7 18.4 %shard_map.263 = (f32[1,9,1536,128]{3,2,1,0:T(8,128)}, f32[1,9,1536,128]{3,2,1,0:T(8,128)}, f32[1,9,1536,128]{3,2,1,0:T(8,128)}) custom-call(f32[9]{0:T(128)S(1)} %copy-done.7, s32[9]{0:T(128)S(1)} %compare_convert_fusion.fill_ref, bf16[2,9,1536,128]{3,2,1,0:T(8,128)(2,1)} %get-tuple-element.166.grads, f32[1,9,1536,128]{3,2,1,0:T(8,128)} %weight.1, ...), custom_call_target="tpu_custom_call" | custom-call | tf_op jit(solution)/shard_map/pallas_call | solution.py:1013
  753.1 1.0 multiply_subtract_fusion.1
  (135 shorter events, 15.4 us)
Async XLA Ops:
  0.6 252.3 %copy-start = (f32[16,6,1536]{2,0,1:T(8,128)S(1)}, f32[16,6,1536]{2,0,1:T(8,128)}, u32[]{:S(2)}) copy-start(f32[16,6,1536]{2,0,1:T(8,128)} %param.23) | copy-start | bytes 1769476
  0.7 4.2 copy-start.20
  0.7 4.3 copy-start.35
  0.7 5.0 copy-start.21
  3.0 1.9 copy-start.37
  3.8 2.1 copy-start.6
  5.9 3.9 copy-start.4
  248.4 1.1 copy-start.2
  249.6 0.6 copy-start.5
  250.3 3.6 copy-start.10
  263.1 5.4 collective-permute-start
  268.4 0.7 copy-start.18
  277.4 19.4 %collective-permute-start.1 = (bf16[272,1536]{1,0:T(8,128)(2,1)}, bf16[272,1536]{1,0:T(8,128)(2,1)S(1)}, u32[]{:S(2)}, u32[]{:S(2)}) collective-permute-start(bf16[272,1536]{1,0:T(8,128)(2,1)} %get-tuple-element.99.part_ref), channel_id=1, source_target_pairs={{0,8},{2,10},{4,12},{6,14},{8,0},{10,2},{12,4},{14,6},{16,24},{18,... | collective-permute-start | bytes 2506760 | tf_op jit(solution)/shard_map/ppermute | solution.py:111
  282.3 7.9 %copy-start.3 = (bf16[512,1536]{1,0:T(8,128)(2,1)S(1)}, bf16[512,1536]{1,0:T(8,128)(2,1)}, u32[]{:S(2)}) copy-start(bf16[512,1536]{1,0:T(8,128)(2,1)} %copy-done.2) | copy-start | bytes 4718596
  296.8 0.9 copy-start.15
  297.7 6.9 copy-start.12
  297.7 6.9 copy-start.13
  303.9 4.1 collective-permute-start.2
  308.0 0.6 copy-start.19
  315.5 18.0 %collective-permute-start.3 = (bf16[272,1536]{1,0:T(8,128)(2,1)}, bf16[272,1536]{1,0:T(8,128)(2,1)}, u32[]{:S(2)}, u32[]{:S(2)}) collective-permute-start(bf16[272,1536]{1,0:T(8,128)(2,1)} %get-tuple-element.115.part_ref), channel_id=1, source_target_pairs={{0,8},{2,10},{4,12},{6,14},{8,0},{10,2},{12,4},{14,6},{16,24},{18,... | collective-permute-start | bytes 2506760 | tf_op jit(solution)/shard_map/ppermute | solution.py:111
  317.6 11.6 %copy-start.16 = (bf16[272,1536]{1,0:T(8,128)(2,1)S(1)}, bf16[272,1536]{1,0:T(8,128)(2,1)}, u32[]{:S(2)}) copy-start(bf16[272,1536]{1,0:T(8,128)(2,1)} %get-tuple-element.117) | copy-start | bytes 2506756
  329.2 1.2 copy-start.8
  352.5 16.8 %collective-permute-start.4 = (bf16[272,1536]{1,0:T(8,128)(2,1)}, bf16[272,1536]{1,0:T(8,128)(2,1)S(1)}, u32[]{:S(2)}, u32[]{:S(2)}) collective-permute-start(bf16[272,1536]{1,0:T(8,128)(2,1)} %get-tuple-element.122.part_ref.da2), channel_id=1, source_target_pairs={{0,8},{2,10},{4,12},{6,14},{8,0},{10,2},{12,4},{14,6},{16,24},{18,... | collective-permute-start | bytes 2506760 | tf_op jit(solution)/shard_map/ppermute | solution.py:111
  354.8 11.8 %copy-start.17 = (bf16[272,1536]{1,0:T(8,128)(2,1)S(1)}, bf16[272,1536]{1,0:T(8,128)(2,1)}, u32[]{:S(2)}) copy-start(bf16[272,1536]{1,0:T(8,128)(2,1)} %get-tuple-element.124) | copy-start | bytes 2506756
  369.4 0.9 copy-start.14
  370.2 14.1 %copy-start.36 = (s32[144]{0:T(256)S(1)}, s32[144]{0:T(256)}, u32[]{:S(2)}) copy-start(s32[144]{0:T(256)} %get-tuple-element.191) | copy-start | bytes 1732
  383.5 4.1 collective-permute-start.5
  387.6 0.6 copy-start.23
  388.2 7.4 copy-start.38
  388.2 10.5 %copy-start.31 = (f32[1,1536]{1,0:T(1,128)S(1)}, f32[1,1536]{1,0:T(1,128)}, u32[]{:S(2)}) copy-start(f32[1,1536]{1,0:T(1,128)} %get-tuple-element.183) | copy-start | bytes 18436
  388.2 10.5 %copy-start.32 = (f32[1,1536]{1,0:T(1,128)S(1)}, f32[1,1536]{1,0:T(1,128)}, u32[]{:S(2)}) copy-start(f32[1,1536]{1,0:T(1,128)} %get-tuple-element.184) | copy-start | bytes 18436
  388.2 11.2 %copy-start.33 = (f32[1,4480]{1,0:T(1,128)S(1)}, f32[1,4480]{1,0:T(1,128)}, u32[]{:S(2)}) copy-start(f32[1,4480]{1,0:T(1,128)} %get-tuple-element.160) | copy-start | bytes 53764
  394.7 4.8 copy-start.9
  394.7 14.9 %collective-permute-start.6 = (bf16[272,1536]{1,0:T(8,128)(2,1)}, bf16[272,1536]{1,0:T(8,128)(2,1)}, u32[]{:S(2)}, u32[]{:S(2)}) collective-permute-start(bf16[272,1536]{1,0:T(8,128)(2,1)} %get-tuple-element.133.da3.part_ref), channel_id=1, source_target_pairs={{0,8},{2,10},{4,12},{6,14},{8,0},{10,2},{12,4},{14,6},{16,24},{18,... | collective-permute-start | bytes 2506760 | tf_op jit(solution)/shard_map/ppermute | solution.py:111
  401.3 7.2 copy-start.30
  424.8 1.7 copy-start.24
  424.8 2.8 copy-start.34
  426.6 4.0 collective-permute-start.7
  430.5 0.7 copy-start.25
  431.2 9.8 %slice-start = ((f32[11,1536]{1,0:T(8,128)}), f32[3,1536]{1,0:T(4,128)S(1)}, s32[]{:S(2)}) async-start(f32[11,1536]{1,0:T(8,128)} %shard_map.259), calls=%async_computation | async-start | bytes 49152 | tf_op jit(solution)/shard_map/slice | solution.py:1950
  731.3 2.6 copy-start.11
  731.3 2.6 copy-start.26
  731.3 2.6 copy-start.27
  731.3 3.3 copy-start.7
  734.6 18.4 %copy-start.22 = (f32[1,12160]{1,0:T(1,128)S(1)}, f32[1,12160]{1,0:T(1,128)}, u32[]{:S(2)}) copy-start(f32[1,12160]{1,0:T(1,128)} %param.27) | copy-start | bytes 145924
  734.6 18.4 %copy-start.28 = (f32[1,12160]{1,0:T(1,128)S(1)}, f32[1,12160]{1,0:T(1,128)}, u32[]{:S(2)}) copy-start(f32[1,12160]{1,0:T(1,128)} %param.28) | copy-start | bytes 145924
  734.6 18.4 %copy-start.29 = (f32[1,12160]{1,0:T(1,128)S(1)}, f32[1,12160]{1,0:T(1,128)}, u32[]{:S(2)}) copy-start(f32[1,12160]{1,0:T(1,128)} %param.29) | copy-start | bytes 145924
  734.7 19.4 %copy-start.1 = (f32[16,6,1536]{2,0,1:T(8,128)S(1)}, f32[16,6,1536]{2,0,1:T(8,128)}, u32[]{:S(2)}) copy-start(f32[16,6,1536]{2,0,1:T(8,128)} %param.23) | copy-start | bytes 1769476

commit v2 on v1

--- a/solution.py
+++ b/solution.py
@@ -736,34 +736,37 @@
 
         @pl.when(step + 1 < turns)
         def _():
-            for_sibling(step + 1, 0, 4)
-
-        @pl.when(step < turns)
-        def _():
-            relayed_in(step)
-
-        @pl.when(step >= 1)
-        def _():
-            centre_in(step - 1)
-
-        @pl.when(step + 1 < turns)
-        def _():
-            for q in range(3):
-                fetch(q, step + 1)
-
-        @pl.when(step < turns)
-        def _():
-            relayed_sides(step)
-
-        @pl.when(step >= 1)
-        def _():
-            centre(step - 1)
-
-        @pl.when(step + 1 < turns)
-        def _():
-            fetch(3, step + 1)
             corner(step + 1)
             direct_sides(step + 1)
+
+        @pl.when(step + 2 < turns)
+        def _():
+            for_sibling(step + 2, 0, 4)
+
+        @pl.when(step < turns)
+        def _():
+            relayed_in(step)
+
+        @pl.when(step >= 1)
+        def _():
+            centre_in(step - 1)
+
+        @pl.when(step < turns)
+        def _():
+            relayed_sides(step)
+
+        @pl.when(step >= 1)
+        def _():
+            centre(step - 1)
+
+        @pl.when(step + 2 < turns)
+        def _():
+            for q in range(3):
+                fetch(q, step + 2)
+
+        @pl.when(step + 1 < turns)
+        def _():
+            fetch(3, step + 1)
 
         @pl.when(jnp.logical_and(step == 3, home))
         def _():
@@ -785,6 +788,9 @@
     for q in range(1, 4):
         fetch(q, 0)
     direct_sides(0)
+    for_sibling(1, 0, 4)
+    for q in range(3):
+        fetch(q, 1)
     lax.fori_loop(0, turns + 1, turn, 0)
     for q in range(4):
         sib_copy(q, turns - 1).wait_send()

time: 763 us -> 765 us (level)
  no operation moved by 1% of the time
where the time goes in v2:
time: 765 us; the launch traced here: 753 us
  Pallas kernels  671 us (88%)
  local copies, waits for them, and re-layouts  38.1 us (5%)
  other arithmetic  18.3 us (2%)
  waiting for transfers between devices  15 us (2%)
    pallas_call x1, Pallas kernels, reduce_slots(): pl.pallas_call(reduce_kernel, out_shape=[jax.ShapeDtypeStruct((2, slot_co...  283 us
    pallas_call x1, Pallas kernels, gather_slots(): pl.pallas_call(gather_kernel, out_shape=[jax.ShapeDtypeStruct((16,) + sca...  239 us
    pallas_call x13, Pallas kernels, call(): pl.pallas_call(body, grid_spec=pltpu.PrefetchScalarGridSpec(num_scalar_pr...  131 us
    pallas_call x1, Pallas kernels, adam_slots(): pl.pallas_call(step, in_specs=[scalars, scalars] + [ANY] * 4, out_specs=[...  18.4 us
  transfers between devices with their start and end apart: 8, of which 7 were waited for; matrix products, arithmetic and copies ran while one was open for 3% of the time, Pallas kernels for 5%

profile of v2, /device:TPU:9, one launch (start us, length us, event | category | flops | bytes accessed | tf_op | source)
XLA Modules:
  0.0 753.4 jit_solution(1606316026932125048)
XLA Ops:
  0.7 0.9 convert_reduce_fusion
  3.8 1.0 pad.48.lat
  5.9 3.8 fusion.own
  9.8 238.6 %shard_map.248 = (bf16[16,9,1536,128]{3,2,1,0:T(8,128)(2,1)}, bf16[2,144,1536]{2,1,0:T(8,128)(2,1)S(1)}, bf16[2,144,1536]{2,1,0:T(8,128)(2,1)S(1)}, bf16[512,1536]{1,0:T(8,128)(2,1)S(1)}, f32[104,128]{1,0:T(8,128)S(1)}) custom-call(bf16[9,1536,128]{2,1,0:T(8,128)(2,1)S(1)} %fusion.own, bf16[144,1536]{1,0:T(8,128)(2,1)S(1)} %pad.48.lat, ...), custom_call_target="tpu_custom_call" | custom-call | tf_op jit(solution)/shard_map/pallas_call | solution.py:393
  248.4 1.1 copy-done.2
  251.5 1.4 fusion.6.rows_ref.refs_17_
  252.9 1.0 fusion.15
  254.5 8.5 %shard_map.249 = (bf16[272,1536]{1,0:T(8,128)(2,1)}, f32[2,272,768]{2,1,0:T(8,128)}, bf16[272,768]{1,0:T(8,128)(2,1)}, f32[272,128]{1,0:T(8,128)}) custom-call(s32[118]{0:T(128)S(1)} %get-tuple-element.196._.where, f32[272,1536]{1,0:T(8,128)} %fusion.6.rows_ref.refs_17_, f32[6,1536]{1,0:T(8,128)} %bitcast_add_fusion.mod_ref, f32[10,768]{1,0:T(8,128)} %reshape.175.vec_ref, ...), custom_call_target="tpu_custom_call" | custom-call | tf_op jit(solution)/shard_map/pallas_call | solution.py:1126
  263.1 1.3 collective-permute-start
  266.9 1.5 collective-permute-done.other_ref.sqo_ref
  269.1 8.3 %shard_map.250 = (bf16[272,768]{1,0:T(8,128)(2,1)}, bf16[272,768]{1,0:T(8,128)(2,1)}, bf16[6,272,128]{2,1,0:T(8,128)(2,1)}, bf16[272,1536]{1,0:T(8,128)(2,1)}) custom-call(s32[118]{0:T(128)S(1)} %get-tuple-element.196._.where, f32[2,272,768]{2,1,0:T(8,128)} %get-tuple-element.94.pre_ref, bf16[272,768]{1,0:T(8,128)(2,1)} %get-tuple-element.95.value_ref.v_ref, ...), custom_call_target="tpu_custom_call" | custom-call | tf_op jit(solution)/shard_map/pallas_call | solution.py:1126
  277.4 1.0 collective-permute-start.1
  278.5 1.6 copy.49
  280.1 1.2 pad_bitcast_fusion.5.refs_0_
  281.3 1.0 slice_bitcast_fusion.1
  282.3 7.9 %shard_map.251 = (f32[512,768]{1,0:T(8,128)}, bf16[512,768]{1,0:T(8,128)(2,1)}, f32[512,128]{1,0:T(8,128)}) custom-call(s32[118]{0:T(128)S(1)} %get-tuple-element.196._.where, bf16[512,1536]{1,0:T(8,128)(2,1)} %copy-done.2, f32[10,768]{1,0:T(8,128)} %reshape.175.vec_ref, bf16[144,1536,128]{2,1,0:T(8,128)(2,1)} %bitcast.63, bf16[144,1536,128]{2,1,0:T(8,128)(2,1)} %bitcast.64, ...), custom_call_target="tpu_custom_call" | custom-call | tf_op jit(solution)/shard_map/pallas_call | solution.py:1126
  290.2 1.7 copy.48
  291.9 4.9 collective-permute-done.1.other_ref
  296.8 0.9 copy-done.15
  297.7 6.1 shard_map.252
  303.8 0.7 collective-permute-start.2
  304.6 1.4 fusion.8.cot_ref
  305.9 2.0 collective-permute-done.2.other_ref.sqo_ref
  308.6 6.8 shard_map.253
  315.4 0.7 collective-permute-start.3
  316.2 0.7 slice_bitcast_fusion.4
  317.5 11.6 %shard_map.254 = (bf16[272,1536]{1,0:T(8,128)(2,1)}, bf16[272,4480]{1,0:T(8,128)(2,1)}) custom-call(s32[118]{0:T(128)S(1)} %get-tuple-element.196._.where, bf16[144,1536,128]{2,1,0:T(8,128)(2,1)} %bitcast.81, f32[6,1536]{1,0:T(8,128)} %bitcast_add_fusion.mod_ref, f32[272,1536]{1,0:T(8,128)} %fusion.8.cot_ref), custom_call_target="tpu_custom_call" | custom-call | tf_op jit(solution)/shard_map/pallas_call | solution.py:1126
  329.1 0.7 copy.50
  331.0 1.2 pad_bitcast_fusion.4.refs_2_
  332.2 1.2 pad_bitcast_fusion.3.refs_6_
  333.4 19.1 %shard_map.255 = (f32[272,1536]{1,0:T(8,128)}, bf16[272,1536]{1,0:T(8,128)(2,1)}, bf16[35,272,128]{2,1,0:T(8,128)(2,1)}, bf16[35,272,128]{2,1,0:T(8,128)(2,1)}, ...) custom-call(s32[118]{0:T(128)S(1)} %get-tuple-element.196._.where, bf16[144,1536,128]{2,1,0:T(8,128)(2,1)} %bitcast.82, ...), custom_call_target="tpu_custom_call" | custom-call | tf_op jit(solution)/shard_map/pallas_call | solution.py:1126
  352.4 0.8 collective-permute-start.4
  353.2 1.5 fusion.26
  354.7 11.8 %shard_map.256.y3.refs_20_ = bf16[272,1536]{1,0:T(8,128)(2,1)} custom-call(s32[118]{0:T(128)S(1)} %get-tuple-element.196._.where, bf16[144,1536,128]{2,1,0:T(8,128)(2,1)} %bitcast.83, bf16[35,272,128]{2,1,0:T(8,128)(2,1)} %get-tuple-element.123.hidden_ref.refs_16_), custom_call_target="tpu_custom_call" | custom-call | tf_op jit(solution)/shard_map/pallas_call | solution.py:1126
  366.5 0.9 copy.52
  367.5 1.1 pad_bitcast_fusion.2.refs_5_
  369.3 0.9 copy-done.14
  370.2 13.1 %shard_map.257 = (f32[272,1536]{1,0:T(8,128)}, bf16[272,1536]{1,0:T(8,128)(2,1)}, f32[272,768]{1,0:T(8,128)}, f32[512,768]{1,0:T(8,128)}, bf16[6,512,128]{2,1,0:T(8,128)(2,1)}, /*index=5*/f32[272,128]{1,0:T(8,128)}) custom-call(s32[118]{0:T(128)S(1)} %get-tuple-element.196._.where, f32[272,1536]{1,0:T(8,128)} %fusion.8.cot_ref, ...), custom_call_target="tpu_custom_call" | custom-call | tf_op jit(solution)/shard_map/pallas_call | solution.py:1126
  383.3 0.9 collective-permute-start.5
  384.2 3.2 collective-permute-done.5.sumo_ref
  388.1 6.4 shard_map.258
  394.5 0.9 collective-permute-start.6
  395.5 0.8 slice.114
  396.3 2.1 gather_fusion
  400.0 1.1 pad_bitcast_fusion.1.refs_4_
  401.1 7.2 shard_map.259
  408.3 1.0 collective-permute-done.6.other_ref
  409.3 0.8 slice.118
  410.1 14.5 %shard_map.260 = (f32[272,1536]{1,0:T(8,128)}, bf16[272,1536]{1,0:T(8,128)(2,1)}, f32[2,272,768]{2,1,0:T(8,128)}, bf16[6,272,128]{2,1,0:T(8,128)(2,1)}, f32[272,128]{1,0:T(8,128)}, /*index=5*/f32[2,1536]{1,0:T(2,128)}) custom-call(s32[118]{0:T(128)S(1)} %get-tuple-element.196._.where, f32[272,1536]{1,0:T(8,128)} %get-tuple-element.128.dx_in, ...), custom_call_target="tpu_custom_call" | custom-call | tf_op jit(solution)/shard_map/pallas_call | solution.py:1126
  424.7 1.7 copy.54
  426.4 1.1 collective-permute-start.7
  427.5 1.1 pad_bitcast_fusion.refs_1_
  428.6 1.7 collective-permute-done.7.sumo_ref
  431.0 9.8 %shard_map.261 = (bf16[6,272,128]{2,1,0:T(8,128)(2,1)}, bf16[6,272,128]{2,1,0:T(8,128)(2,1)}, f32[8,768]{1,0:T(8,128)}, bf16[272,1536]{1,0:T(8,128)(2,1)}, f32[2,1536]{1,0:T(2,128)}) custom-call(s32[118]{0:T(128)S(1)} %get-tuple-element.196._.where, f32[272,1536]{1,0:T(8,128)} %fusion.6.rows_ref.refs_17_, f32[2,272,768]{2,1,0:T(8,128)} %get-tuple-element.94.pre_ref, ...), custom_call_target="tpu_custom_call" | custom-call | tf_op jit(solution)/shard_map/pallas_call | solution.py:1126
  440.8 0.8 concatenate.30
  441.6 0.7 reshape.178
  443.3 283.2 %shard_map.262 = (bf16[2,9,1536,128]{3,2,1,0:T(8,128)(2,1)}, f32[328,128]{1,0:T(8,128)}, bf16[272,1536]{1,0:T(8,128)(2,1)}, f32[272,1536]{1,0:T(8,128)}, bf16[27...) custom-call(s32[144]{0:T(256)} %gather_fusion, ...), custom_call_target="tpu_custom_call" | custom-call | tf_op jit(solution)/shard_map/pallas_call | solution.py:869
  726.4 0.9 slice.125
  727.3 0.9 slice.126
  728.2 2.0 slice_select_fusion.1
  730.2 2.5 slice_select_fusion
  732.8 0.7 multiply_subtract_fusion
  733.6 18.4 %shard_map.263 = (f32[1,9,1536,128]{3,2,1,0:T(8,128)}, f32[1,9,1536,128]{3,2,1,0:T(8,128)}, f32[1,9,1536,128]{3,2,1,0:T(8,128)}) custom-call(f32[9]{0:T(128)S(1)} %copy-done.7, s32[9]{0:T(128)S(1)} %compare_convert_fusion.fill_ref, bf16[2,9,1536,128]{3,2,1,0:T(8,128)(2,1)} %get-tuple-element.166.grads, f32[1,9,1536,128]{3,2,1,0:T(8,128)} %weight.1, ...), custom_call_target="tpu_custom_call" | custom-call | tf_op jit(solution)/shard_map/pallas_call | solution.py:1019
  752.0 1.0 multiply_subtract_fusion.1
  (135 shorter events, 15.4 us)
Async XLA Ops:
  0.6 252.3 %copy-start = (f32[16,6,1536]{2,0,1:T(8,128)S(1)}, f32[16,6,1536]{2,0,1:T(8,128)}, u32[]{:S(2)}) copy-start(f32[16,6,1536]{2,0,1:T(8,128)} %param.23) | copy-start | bytes 1769476
  0.7 4.2 copy-start.20
  0.7 4.3 copy-start.35
  0.7 5.0 copy-start.21
  3.0 1.9 copy-start.37
  3.8 2.1 copy-start.6
  5.9 3.9 copy-start.4
  248.4 1.1 copy-start.2
  249.6 0.6 copy-start.5
  250.3 3.6 copy-start.10
  263.1 5.4 collective-permute-start
  268.4 0.7 copy-start.18
  277.4 19.4 %collective-permute-start.1 = (bf16[272,1536]{1,0:T(8,128)(2,1)}, bf16[272,1536]{1,0:T(8,128)(2,1)S(1)}, u32[]{:S(2)}, u32[]{:S(2)}) collective-permute-start(bf16[272,1536]{1,0:T(8,128)(2,1)} %get-tuple-element.99.part_ref), channel_id=1, source_target_pairs={{0,8},{2,10},{4,12},{6,14},{8,0},{10,2},{12,4},{14,6},{16,24},{18,... | collective-permute-start | bytes 2506760 | tf_op jit(solution)/shard_map/ppermute | solution.py:111
  282.3 7.9 %copy-start.3 = (bf16[512,1536]{1,0:T(8,128)(2,1)S(1)}, bf16[512,1536]{1,0:T(8,128)(2,1)}, u32[]{:S(2)}) copy-start(bf16[512,1536]{1,0:T(8,128)(2,1)} %copy-done.2) | copy-start | bytes 4718596
  296.8 0.9 copy-start.15
  297.7 6.8 copy-start.12
  297.7 6.8 copy-start.13
  303.8 4.1 collective-permute-start.2
  307.9 0.6 copy-start.19
  315.4 18.0 %collective-permute-start.3 = (bf16[272,1536]{1,0:T(8,128)(2,1)}, bf16[272,1536]{1,0:T(8,128)(2,1)}, u32[]{:S(2)}, u32[]{:S(2)}) collective-permute-start(bf16[272,1536]{1,0:T(8,128)(2,1)} %get-tuple-element.115.part_ref), channel_id=1, source_target_pairs={{0,8},{2,10},{4,12},{6,14},{8,0},{10,2},{12,4},{14,6},{16,24},{18,... | collective-permute-start | bytes 2506760 | tf_op jit(solution)/shard_map/ppermute | solution.py:111
  317.5 11.6 %copy-start.16 = (bf16[272,1536]{1,0:T(8,128)(2,1)S(1)}, bf16[272,1536]{1,0:T(8,128)(2,1)}, u32[]{:S(2)}) copy-start(bf16[272,1536]{1,0:T(8,128)(2,1)} %get-tuple-element.117) | copy-start | bytes 2506756
  329.1 1.2 copy-start.8
  352.4 16.8 %collective-permute-start.4 = (bf16[272,1536]{1,0:T(8,128)(2,1)}, bf16[272,1536]{1,0:T(8,128)(2,1)S(1)}, u32[]{:S(2)}, u32[]{:S(2)}) collective-permute-start(bf16[272,1536]{1,0:T(8,128)(2,1)} %get-tuple-element.122.part_ref.da2), channel_id=1, source_target_pairs={{0,8},{2,10},{4,12},{6,14},{8,0},{10,2},{12,4},{14,6},{16,24},{18,... | collective-permute-start | bytes 2506760 | tf_op jit(solution)/shard_map/ppermute | solution.py:111
  354.7 11.8 %copy-start.17 = (bf16[272,1536]{1,0:T(8,128)(2,1)S(1)}, bf16[272,1536]{1,0:T(8,128)(2,1)}, u32[]{:S(2)}) copy-start(bf16[272,1536]{1,0:T(8,128)(2,1)} %get-tuple-element.124) | copy-start | bytes 2506756
  369.3 0.9 copy-start.14
  370.2 14.0 %copy-start.36 = (s32[144]{0:T(256)S(1)}, s32[144]{0:T(256)}, u32[]{:S(2)}) copy-start(s32[144]{0:T(256)} %get-tuple-element.191) | copy-start | bytes 1732
  383.3 4.1 collective-permute-start.5
  387.4 0.6 copy-start.23
  388.0 7.4 copy-start.38
  388.0 10.5 %copy-start.31 = (f32[1,1536]{1,0:T(1,128)S(1)}, f32[1,1536]{1,0:T(1,128)}, u32[]{:S(2)}) copy-start(f32[1,1536]{1,0:T(1,128)} %get-tuple-element.183) | copy-start | bytes 18436
  388.0 10.5 %copy-start.32 = (f32[1,1536]{1,0:T(1,128)S(1)}, f32[1,1536]{1,0:T(1,128)}, u32[]{:S(2)}) copy-start(f32[1,1536]{1,0:T(1,128)} %get-tuple-element.184) | copy-start | bytes 18436
  388.0 11.2 %copy-start.33 = (f32[1,4480]{1,0:T(1,128)S(1)}, f32[1,4480]{1,0:T(1,128)}, u32[]{:S(2)}) copy-start(f32[1,4480]{1,0:T(1,128)} %get-tuple-element.160) | copy-start | bytes 53764
  394.5 4.8 copy-start.9
  394.5 14.9 %collective-permute-start.6 = (bf16[272,1536]{1,0:T(8,128)(2,1)}, bf16[272,1536]{1,0:T(8,128)(2,1)}, u32[]{:S(2)}, u32[]{:S(2)}) collective-permute-start(bf16[272,1536]{1,0:T(8,128)(2,1)} %get-tuple-element.133.da3.part_ref), channel_id=1, source_target_pairs={{0,8},{2,10},{4,12},{6,14},{8,0},{10,2},{12,4},{14,6},{16,24},{18,... | collective-permute-start | bytes 2506760 | tf_op jit(solution)/shard_map/ppermute | solution.py:111
  401.1 7.2 copy-start.30
  424.7 1.7 copy-start.24
  424.7 2.8 copy-start.34
  426.4 4.0 collective-permute-start.7
  430.3 0.7 copy-start.25
  431.0 9.8 %slice-start = ((f32[11,1536]{1,0:T(8,128)}), f32[3,1536]{1,0:T(4,128)S(1)}, s32[]{:S(2)}) async-start(f32[11,1536]{1,0:T(8,128)} %shard_map.259), calls=%async_computation | async-start | bytes 49152 | tf_op jit(solution)/shard_map/slice | solution.py:1956
  730.2 2.6 copy-start.11
  730.2 2.6 copy-start.26
  730.2 2.6 copy-start.27
  730.2 3.3 copy-start.7
  733.6 18.4 %copy-start.22 = (f32[1,12160]{1,0:T(1,128)S(1)}, f32[1,12160]{1,0:T(1,128)}, u32[]{:S(2)}) copy-start(f32[1,12160]{1,0:T(1,128)} %param.27) | copy-start | bytes 145924
  733.6 18.4 %copy-start.28 = (f32[1,12160]{1,0:T(1,128)S(1)}, f32[1,12160]{1,0:T(1,128)}, u32[]{:S(2)}) copy-start(f32[1,12160]{1,0:T(1,128)} %param.28) | copy-start | bytes 145924
  733.6 18.4 %copy-start.29 = (f32[1,12160]{1,0:T(1,128)S(1)}, f32[1,12160]{1,0:T(1,128)}, u32[]{:S(2)}) copy-start(f32[1,12160]{1,0:T(1,128)} %param.29) | copy-start | bytes 145924
  733.6 19.4 %copy-start.1 = (f32[16,6,1536]{2,0,1:T(8,128)S(1)}, f32[16,6,1536]{2,0,1:T(8,128)}, u32[]{:S(2)}) copy-start(f32[16,6,1536]{2,0,1:T(8,128)} %param.23) | copy-start | bytes 1769476

commit v3 on v2

--- a/solution.py
+++ b/solution.py
@@ -714,11 +714,6 @@
         for store in end_stores:
             store.start()
 
-    @pl.when(home)
-    def _():
-        for load in end_loads[:5]:
-            load.start()
-
     @pl.when(jnp.logical_not(home))
     def _():
         ends[0].start()
@@ -730,7 +725,7 @@
     def turn(step, carry):
         for i in range(5):
 
-            @pl.when(step == i)
+            @pl.when(step == 2 * i)
             def _():
                 vec_copy(i).start()
 
@@ -768,13 +763,18 @@
         def _():
             fetch(3, step + 1)
 
+        @pl.when(jnp.logical_and(step == 1, home))
+        def _():
+            for load in end_loads[:5]:
+                load.start()
+
         @pl.when(jnp.logical_and(step == 3, home))
         def _():
             finish_rows()
 
         for i in range(5):
 
-            @pl.when(step == i)
+            @pl.when(step == 2 * i + 1)
             def _():
                 vec_copy(i).wait()
                 vec_out[...] = vec_out[...] + vec_box[i]

time: 765 us -> 744 us (0.973)
  Pallas kernels: 671 us -> 653 us
    pallas_call x1, Pallas kernels: 283 us -> 266 us  [reduce_slots(): pl.pallas_call(reduce_kernel, out_shape=[jax.ShapeDtypeStruct((2, slot_co...]
where the time goes in v3:
time: 744 us; the launch traced here: 735 us
  Pallas kernels  653 us (88%)
  local copies, waits for them, and re-layouts  38.1 us (5%)
  other arithmetic  18.3 us (2%)
  waiting for transfers between devices  15 us (2%)
  starting transfers between devices  7.5 us (1%)
    pallas_call x1, Pallas kernels, reduce_slots(): pl.pallas_call(reduce_kernel, out_shape=[jax.ShapeDtypeStruct((2, slot_co...  266 us
    pallas_call x1, Pallas kernels, gather_slots(): pl.pallas_call(gather_kernel, out_shape=[jax.ShapeDtypeStruct((16,) + sca...  239 us
    pallas_call x13, Pallas kernels, call(): pl.pallas_call(body, grid_spec=pltpu.PrefetchScalarGridSpec(num_scalar_pr...  131 us
    pallas_call x1, Pallas kernels, adam_slots(): pl.pallas_call(step, in_specs=[scalars, scalars] + [ANY] * 4, out_specs=[...  17.1 us
    ppermute x8, waiting for transfers between devices, pair_swap(): return lax.ppermute(value, 'dp', [(i, i ^ 4) for i in range(16)])  15 us
  transfers between devices with their start and end apart: 8, of which 7 were waited for; matrix products, arithmetic and copies ran while one was open for 3% of the time, Pallas kernels for 5%

profile of v3, /device:TPU:9, one launch (start us, length us, event | category | flops | bytes accessed | tf_op | source)
XLA Modules:
  0.0 735.1 jit_solution(8792814643728111043)
XLA Ops:
  0.7 0.9 convert_reduce_fusion
  3.8 1.0 pad.48.lat
  5.9 3.8 fusion.own
  9.8 238.6 %shard_map.248 = (bf16[16,9,1536,128]{3,2,1,0:T(8,128)(2,1)}, bf16[2,144,1536]{2,1,0:T(8,128)(2,1)S(1)}, bf16[2,144,1536]{2,1,0:T(8,128)(2,1)S(1)}, bf16[512,1536]{1,0:T(8,128)(2,1)S(1)}, f32[104,128]{1,0:T(8,128)S(1)}) custom-call(bf16[9,1536,128]{2,1,0:T(8,128)(2,1)S(1)} %fusion.own, bf16[144,1536]{1,0:T(8,128)(2,1)S(1)} %pad.48.lat, ...), custom_call_target="tpu_custom_call" | custom-call | tf_op jit(solution)/shard_map/pallas_call | solution.py:393
  248.4 1.1 copy-done.2
  251.5 1.4 fusion.6.rows_ref.refs_17_
  252.9 1.0 fusion.15
  254.5 8.5 %shard_map.249 = (bf16[272,1536]{1,0:T(8,128)(2,1)}, f32[2,272,768]{2,1,0:T(8,128)}, bf16[272,768]{1,0:T(8,128)(2,1)}, f32[272,128]{1,0:T(8,128)}) custom-call(s32[118]{0:T(128)S(1)} %get-tuple-element.196._.where, f32[272,1536]{1,0:T(8,128)} %fusion.6.rows_ref.refs_17_, f32[6,1536]{1,0:T(8,128)} %bitcast_add_fusion.mod_ref, f32[10,768]{1,0:T(8,128)} %reshape.175.vec_ref, ...), custom_call_target="tpu_custom_call" | custom-call | tf_op jit(solution)/shard_map/pallas_call | solution.py:1126
  263.1 1.3 collective-permute-start
  266.9 1.5 collective-permute-done.other_ref.sqo_ref
  269.1 8.3 %shard_map.250 = (bf16[272,768]{1,0:T(8,128)(2,1)}, bf16[272,768]{1,0:T(8,128)(2,1)}, bf16[6,272,128]{2,1,0:T(8,128)(2,1)}, bf16[272,1536]{1,0:T(8,128)(2,1)}) custom-call(s32[118]{0:T(128)S(1)} %get-tuple-element.196._.where, f32[2,272,768]{2,1,0:T(8,128)} %get-tuple-element.94.pre_ref, bf16[272,768]{1,0:T(8,128)(2,1)} %get-tuple-element.95.value_ref.v_ref, ...), custom_call_target="tpu_custom_call" | custom-call | tf_op jit(solution)/shard_map/pallas_call | solution.py:1126
  277.4 1.0 collective-permute-start.1
  278.5 1.6 copy.49
  280.1 1.2 pad_bitcast_fusion.5.refs_0_
  281.3 1.0 slice_bitcast_fusion.1
  282.3 7.9 %shard_map.251 = (f32[512,768]{1,0:T(8,128)}, bf16[512,768]{1,0:T(8,128)(2,1)}, f32[512,128]{1,0:T(8,128)}) custom-call(s32[118]{0:T(128)S(1)} %get-tuple-element.196._.where, bf16[512,1536]{1,0:T(8,128)(2,1)} %copy-done.2, f32[10,768]{1,0:T(8,128)} %reshape.175.vec_ref, bf16[144,1536,128]{2,1,0:T(8,128)(2,1)} %bitcast.63, bf16[144,1536,128]{2,1,0:T(8,128)(2,1)} %bitcast.64, ...), custom_call_target="tpu_custom_call" | custom-call | tf_op jit(solution)/shard_map/pallas_call | solution.py:1126
  290.1 1.7 copy.48
  291.9 4.9 collective-permute-done.1.other_ref
  296.8 0.9 copy-done.15
  297.7 6.1 shard_map.252
  303.8 0.7 collective-permute-start.2
  304.6 1.4 fusion.8.cot_ref
  305.9 2.0 collective-permute-done.2.other_ref.sqo_ref
  308.6 6.8 shard_map.253
  315.4 0.7 collective-permute-start.3
  316.2 0.7 slice_bitcast_fusion.4
  317.5 11.6 %shard_map.254 = (bf16[272,1536]{1,0:T(8,128)(2,1)}, bf16[272,4480]{1,0:T(8,128)(2,1)}) custom-call(s32[118]{0:T(128)S(1)} %get-tuple-element.196._.where, bf16[144,1536,128]{2,1,0:T(8,128)(2,1)} %bitcast.81, f32[6,1536]{1,0:T(8,128)} %bitcast_add_fusion.mod_ref, f32[272,1536]{1,0:T(8,128)} %fusion.8.cot_ref), custom_call_target="tpu_custom_call" | custom-call | tf_op jit(solution)/shard_map/pallas_call | solution.py:1126
  329.1 0.7 copy.50
  331.0 1.2 pad_bitcast_fusion.4.refs_2_
  332.2 1.2 pad_bitcast_fusion.3.refs_6_
  333.4 19.1 %shard_map.255 = (f32[272,1536]{1,0:T(8,128)}, bf16[272,1536]{1,0:T(8,128)(2,1)}, bf16[35,272,128]{2,1,0:T(8,128)(2,1)}, bf16[35,272,128]{2,1,0:T(8,128)(2,1)}, ...) custom-call(s32[118]{0:T(128)S(1)} %get-tuple-element.196._.where, bf16[144,1536,128]{2,1,0:T(8,128)(2,1)} %bitcast.82, ...), custom_call_target="tpu_custom_call" | custom-call | tf_op jit(solution)/shard_map/pallas_call | solution.py:1126
  352.4 0.8 collective-permute-start.4
  353.2 1.5 fusion.26
  354.7 11.8 %shard_map.256.y3.refs_20_ = bf16[272,1536]{1,0:T(8,128)(2,1)} custom-call(s32[118]{0:T(128)S(1)} %get-tuple-element.196._.where, bf16[144,1536,128]{2,1,0:T(8,128)(2,1)} %bitcast.83, bf16[35,272,128]{2,1,0:T(8,128)(2,1)} %get-tuple-element.123.hidden_ref.refs_16_), custom_call_target="tpu_custom_call" | custom-call | tf_op jit(solution)/shard_map/pallas_call | solution.py:1126
  366.5 0.9 copy.52
  367.5 1.1 pad_bitcast_fusion.2.refs_5_
  369.3 0.9 copy-done.14
  370.2 13.1 %shard_map.257 = (f32[272,1536]{1,0:T(8,128)}, bf16[272,1536]{1,0:T(8,128)(2,1)}, f32[272,768]{1,0:T(8,128)}, f32[512,768]{1,0:T(8,128)}, bf16[6,512,128]{2,1,0:T(8,128)(2,1)}, /*index=5*/f32[272,128]{1,0:T(8,128)}) custom-call(s32[118]{0:T(128)S(1)} %get-tuple-element.196._.where, f32[272,1536]{1,0:T(8,128)} %fusion.8.cot_ref, ...), custom_call_target="tpu_custom_call" | custom-call | tf_op jit(solution)/shard_map/pallas_call | solution.py:1126
  383.3 0.9 collective-permute-start.5
  384.2 3.2 collective-permute-done.5.sumo_ref
  388.1 6.4 shard_map.258
  394.5 0.9 collective-permute-start.6
  395.5 0.8 slice.114
  396.3 2.1 gather_fusion
  400.0 1.1 pad_bitcast_fusion.1.refs_4_
  401.1 7.2 shard_map.259
  408.3 1.0 collective-permute-done.6.other_ref
  409.3 0.8 slice.118
  410.1 14.5 %shard_map.260 = (f32[272,1536]{1,0:T(8,128)}, bf16[272,1536]{1,0:T(8,128)(2,1)}, f32[2,272,768]{2,1,0:T(8,128)}, bf16[6,272,128]{2,1,0:T(8,128)(2,1)}, f32[272,128]{1,0:T(8,128)}, /*index=5*/f32[2,1536]{1,0:T(2,128)}) custom-call(s32[118]{0:T(128)S(1)} %get-tuple-element.196._.where, f32[272,1536]{1,0:T(8,128)} %get-tuple-element.128.dx_in, ...), custom_call_target="tpu_custom_call" | custom-call | tf_op jit(solution)/shard_map/pallas_call | solution.py:1126
  424.7 1.7 copy.54
  426.4 1.1 collective-permute-start.7
  427.5 1.1 pad_bitcast_fusion.refs_1_
  428.6 1.7 collective-permute-done.7.sumo_ref
  431.0 9.9 %shard_map.261 = (bf16[6,272,128]{2,1,0:T(8,128)(2,1)}, bf16[6,272,128]{2,1,0:T(8,128)(2,1)}, f32[8,768]{1,0:T(8,128)}, bf16[272,1536]{1,0:T(8,128)(2,1)}, f32[2,1536]{1,0:T(2,128)}) custom-call(s32[118]{0:T(128)S(1)} %get-tuple-element.196._.where, f32[272,1536]{1,0:T(8,128)} %fusion.6.rows_ref.refs_17_, f32[2,272,768]{2,1,0:T(8,128)} %get-tuple-element.94.pre_ref, ...), custom_call_target="tpu_custom_call" | custom-call | tf_op jit(solution)/shard_map/pallas_call | solution.py:1126
  440.9 0.8 concatenate.30
  441.7 0.7 reshape.178
  443.3 266.0 %shard_map.262 = (bf16[2,9,1536,128]{3,2,1,0:T(8,128)(2,1)}, f32[328,128]{1,0:T(8,128)}, bf16[272,1536]{1,0:T(8,128)(2,1)}, f32[272,1536]{1,0:T(8,128)}, bf16[27...) custom-call(s32[144]{0:T(256)} %gather_fusion, ...), custom_call_target="tpu_custom_call" | custom-call | tf_op jit(solution)/shard_map/pallas_call | solution.py:869
  709.3 0.9 slice.125
  710.2 0.9 slice.126
  711.1 2.0 slice_select_fusion.1
  713.1 2.5 slice_select_fusion
  715.7 0.7 multiply_subtract_fusion
  716.5 17.1 %shard_map.263 = (f32[1,9,1536,128]{3,2,1,0:T(8,128)}, f32[1,9,1536,128]{3,2,1,0:T(8,128)}, f32[1,9,1536,128]{3,2,1,0:T(8,128)}) custom-call(f32[9]{0:T(128)S(1)} %copy-done.7, s32[9]{0:T(128)S(1)} %compare_convert_fusion.fill_ref, bf16[2,9,1536,128]{3,2,1,0:T(8,128)(2,1)} %get-tuple-element.166.grads, f32[1,9,1536,128]{3,2,1,0:T(8,128)} %weight.1, ...), custom_call_target="tpu_custom_call" | custom-call | tf_op jit(solution)/shard_map/pallas_call | solution.py:1019
  733.6 1.0 multiply_subtract_fusion.1
  (135 shorter events, 15.4 us)
Async XLA Ops:
  0.6 252.3 %copy-start = (f32[16,6,1536]{2,0,1:T(8,128)S(1)}, f32[16,6,1536]{2,0,1:T(8,128)}, u32[]{:S(2)}) copy-start(f32[16,6,1536]{2,0,1:T(8,128)} %param.23) | copy-start | bytes 1769476
  0.7 4.2 copy-start.20
  0.7 4.3 copy-start.35
  0.7 5.0 copy-start.21
  3.0 1.9 copy-start.37
  3.8 2.1 copy-start.6
  5.9 3.9 copy-start.4
  248.4 1.1 copy-start.2
  249.6 0.6 copy-start.5
  250.3 3.6 copy-start.10
  263.1 5.4 collective-permute-start
  268.4 0.7 copy-start.18
  277.4 19.4 %collective-permute-start.1 = (bf16[272,1536]{1,0:T(8,128)(2,1)}, bf16[272,1536]{1,0:T(8,128)(2,1)S(1)}, u32[]{:S(2)}, u32[]{:S(2)}) collective-permute-start(bf16[272,1536]{1,0:T(8,128)(2,1)} %get-tuple-element.99.part_ref), channel_id=1, source_target_pairs={{0,8},{2,10},{4,12},{6,14},{8,0},{10,2},{12,4},{14,6},{16,24},{18,... | collective-permute-start | bytes 2506760 | tf_op jit(solution)/shard_map/ppermute | solution.py:111
  282.3 7.9 %copy-start.3 = (bf16[512,1536]{1,0:T(8,128)(2,1)S(1)}, bf16[512,1536]{1,0:T(8,128)(2,1)}, u32[]{:S(2)}) copy-start(bf16[512,1536]{1,0:T(8,128)(2,1)} %copy-done.2) | copy-start | bytes 4718596
  296.8 0.9 copy-start.15
  297.7 6.8 copy-start.12
  297.7 6.8 copy-start.13
  303.8 4.1 collective-permute-start.2
  307.9 0.6 copy-start.19
  315.4 18.0 %collective-permute-start.3 = (bf16[272,1536]{1,0:T(8,128)(2,1)}, bf16[272,1536]{1,0:T(8,128)(2,1)}, u32[]{:S(2)}, u32[]{:S(2)}) collective-permute-start(bf16[272,1536]{1,0:T(8,128)(2,1)} %get-tuple-element.115.part_ref), channel_id=1, source_target_pairs={{0,8},{2,10},{4,12},{6,14},{8,0},{10,2},{12,4},{14,6},{16,24},{18,... | collective-permute-start | bytes 2506760 | tf_op jit(solution)/shard_map/ppermute | solution.py:111
  317.5 11.6 %copy-start.16 = (bf16[272,1536]{1,0:T(8,128)(2,1)S(1)}, bf16[272,1536]{1,0:T(8,128)(2,1)}, u32[]{:S(2)}) copy-start(bf16[272,1536]{1,0:T(8,128)(2,1)} %get-tuple-element.117) | copy-start | bytes 2506756
  329.1 1.2 copy-start.8
  352.4 16.8 %collective-permute-start.4 = (bf16[272,1536]{1,0:T(8,128)(2,1)}, bf16[272,1536]{1,0:T(8,128)(2,1)S(1)}, u32[]{:S(2)}, u32[]{:S(2)}) collective-permute-start(bf16[272,1536]{1,0:T(8,128)(2,1)} %get-tuple-element.122.part_ref.da2), channel_id=1, source_target_pairs={{0,8},{2,10},{4,12},{6,14},{8,0},{10,2},{12,4},{14,6},{16,24},{18,... | collective-permute-start | bytes 2506760 | tf_op jit(solution)/shard_map/ppermute | solution.py:111
  354.7 11.8 %copy-start.17 = (bf16[272,1536]{1,0:T(8,128)(2,1)S(1)}, bf16[272,1536]{1,0:T(8,128)(2,1)}, u32[]{:S(2)}) copy-start(bf16[272,1536]{1,0:T(8,128)(2,1)} %get-tuple-element.124) | copy-start | bytes 2506756
  369.3 0.9 copy-start.14
  370.2 14.0 %copy-start.36 = (s32[144]{0:T(256)S(1)}, s32[144]{0:T(256)}, u32[]{:S(2)}) copy-start(s32[144]{0:T(256)} %get-tuple-element.191) | copy-start | bytes 1732
  383.3 4.1 collective-permute-start.5
  387.4 0.6 copy-start.23
  388.0 7.4 %copy-start.38 = (s32[144]{0:T(256)S(1)}, s32[144]{0:T(256)}, u32[]{:S(2)}) copy-start(s32[144]{0:T(256)} %copy-done.37) | copy-start | bytes 1732
  388.0 10.5 %copy-start.31 = (f32[1,1536]{1,0:T(1,128)S(1)}, f32[1,1536]{1,0:T(1,128)}, u32[]{:S(2)}) copy-start(f32[1,1536]{1,0:T(1,128)} %get-tuple-element.183) | copy-start | bytes 18436
  388.0 10.5 %copy-start.32 = (f32[1,1536]{1,0:T(1,128)S(1)}, f32[1,1536]{1,0:T(1,128)}, u32[]{:S(2)}) copy-start(f32[1,1536]{1,0:T(1,128)} %get-tuple-element.184) | copy-start | bytes 18436
  388.1 11.2 %copy-start.33 = (f32[1,4480]{1,0:T(1,128)S(1)}, f32[1,4480]{1,0:T(1,128)}, u32[]{:S(2)}) copy-start(f32[1,4480]{1,0:T(1,128)} %get-tuple-element.160) | copy-start | bytes 53764
  394.5 4.8 copy-start.9
  394.5 14.8 %collective-permute-start.6 = (bf16[272,1536]{1,0:T(8,128)(2,1)}, bf16[272,1536]{1,0:T(8,128)(2,1)}, u32[]{:S(2)}, u32[]{:S(2)}) collective-permute-start(bf16[272,1536]{1,0:T(8,128)(2,1)} %get-tuple-element.133.da3.part_ref), channel_id=1, source_target_pairs={{0,8},{2,10},{4,12},{6,14},{8,0},{10,2},{12,4},{14,6},{16,24},{18,... | collective-permute-start | bytes 2506760 | tf_op jit(solution)/shard_map/ppermute | solution.py:111
  401.1 7.2 copy-start.30
  424.6 1.7 copy-start.24
  424.6 2.8 copy-start.34
  426.4 4.0 collective-permute-start.7
  430.3 0.7 copy-start.25
  431.0 9.9 %slice-start = ((f32[11,1536]{1,0:T(8,128)}), f32[3,1536]{1,0:T(4,128)S(1)}, s32[]{:S(2)}) async-start(f32[11,1536]{1,0:T(8,128)} %shard_map.259), calls=%async_computation | async-start | bytes 49152 | tf_op jit(solution)/shard_map/slice | solution.py:1956
  713.1 2.6 copy-start.11
  713.1 2.6 copy-start.26
  713.1 2.6 copy-start.27
  713.1 3.3 copy-start.7
  716.5 17.2 %copy-start.22 = (f32[1,12160]{1,0:T(1,128)S(1)}, f32[1,12160]{1,0:T(1,128)}, u32[]{:S(2)}) copy-start(f32[1,12160]{1,0:T(1,128)} %param.27) | copy-start | bytes 145924
  716.5 17.2 %copy-start.28 = (f32[1,12160]{1,0:T(1,128)S(1)}, f32[1,12160]{1,0:T(1,128)}, u32[]{:S(2)}) copy-start(f32[1,12160]{1,0:T(1,128)} %param.28) | copy-start | bytes 145924
  716.5 17.2 %copy-start.29 = (f32[1,12160]{1,0:T(1,128)S(1)}, f32[1,12160]{1,0:T(1,128)}, u32[]{:S(2)}) copy-start(f32[1,12160]{1,0:T(1,128)} %param.29) | copy-start | bytes 145924
  716.5 18.2 %copy-start.1 = (f32[16,6,1536]{2,0,1:T(8,128)S(1)}, f32[16,6,1536]{2,0,1:T(8,128)}, u32[]{:S(2)}) copy-start(f32[16,6,1536]{2,0,1:T(8,128)} %param.23) | copy-start | bytes 1769476

commit v4 on v3

--- a/solution.py
+++ b/solution.py
@@ -393,11 +393,11 @@
     everyone, *rest = pl.pallas_call(
         gather_kernel,
         out_shape=[
-            jax.ShapeDtypeStruct((16,) + scaled.shape, scaled.dtype),
-            jax.ShapeDtypeStruct((2,) + lat.shape, lat.dtype),
-            jax.ShapeDtypeStruct((2,) + cot.shape, cot.dtype),
-            jax.ShapeDtypeStruct(text.shape, text.dtype),
-            jax.ShapeDtypeStruct(small.shape, small.dtype),
+            pltpu.HBM((16,) + scaled.shape, scaled.dtype),
+            pltpu.HBM((2,) + lat.shape, lat.dtype),
+            pltpu.HBM((2,) + cot.shape, cot.dtype),
+            pltpu.HBM(text.shape, text.dtype),
+            pltpu.HBM(small.shape, small.dtype),
         ],
         in_specs=[ANY] * 5,
         out_specs=[ANY] * 5,
@@ -405,7 +405,7 @@
         compiler_params=pltpu.CompilerParams(
             collective_id=0, has_side_effects=True, vmem_limit_bytes=4 * MIB
         ),
-    )(scaled, lat, cot, text, small)
+    )(scaled, lat, cot, pltpu.with_memory_space_constraint(text, pltpu.HBM), small)
     return everyone.reshape((-1,) + scaled.shape[1:]), *rest
 
 
@@ -861,7 +861,7 @@
     deep = 3
 
     def room(count, tall):
-        return jax.ShapeDtypeStruct((count, batch, tall, lanes), low)
+        return pltpu.HBM((count, batch, tall, lanes), low)
 
     def slab(count):
         return pltpu.VMEM((count, batch, half, lanes), low)
@@ -869,10 +869,10 @@
     outs = pl.pallas_call(
         reduce_kernel,
         out_shape=[
-            jax.ShapeDtypeStruct((2, slot_count, width, lanes), low),
+            pltpu.HBM((2, slot_count, width, lanes), low),
             jax.ShapeDtypeStruct(vector.shape, vector.dtype),
-            jax.ShapeDtypeStruct(ends[0].shape, low), jax.ShapeDtypeStruct(ends[0].shape, F32),
-            jax.ShapeDtypeStruct(ends[0].shape, low), jax.ShapeDtypeStruct(ends[0].shape, low),
+            pltpu.HBM(ends[0].shape, low), pltpu.HBM(ends[0].shape, F32),
+            pltpu.HBM(ends[0].shape, low), pltpu.HBM(ends[0].shape, low),
             room(4 * turns, half), room(turns, half), room(turns, half),
             room(turns, half // 2), room(turns, half // 2),
         ],
@@ -897,7 +897,13 @@
         compiler_params=pltpu.CompilerParams(
             collective_id=1, has_side_effects=True, vmem_limit_bytes=58 * MIB
         ),
-    )(kind, block, *left, *columns, *ends, gains, vector)
+    )(
+        kind,
+        block,
+        *[pltpu.with_memory_space_constraint(v, pltpu.HBM) for v in (*left, *columns, *ends)],
+        gains,
+        vector,
+    )
     return outs[:4]
 
 
@@ -1377,7 +1383,7 @@
     i = pl.program_id(0)
 
     def fetch(step, act):
-        slot = step % 2
+        slot = step % 3
         for j in range(group):
             copy = pltpu.make_async_copy(
                 everyone.at[where[first + step * group + j]],
@@ -1389,17 +1395,19 @@
     @pl.when(i == 0)
     def _():
         fetch(0, True)
-
-    @pl.when(i + 1 < steps)
+        if steps > 1:
+            fetch(1, True)
+
+    @pl.when(i + 2 < steps)
     def _():
-        fetch(i + 1, True)
+        fetch(i + 2, True)
 
     fetch(i, False)
-    return held[i % 2]
+    return held[i % 3]
 
 
 def lanes_scratch(group):
-    return [pltpu.VMEM((2, D, group * HEAD), BF16), pltpu.SemaphoreType.DMA((2, group))]
+    return [pltpu.VMEM((3, D, group * HEAD), BF16), pltpu.SemaphoreType.DMA((3, group))]
 
 
 def hidden_back(places, everyone, mod, cot, heads, blocks):
@@ -1843,10 +1851,11 @@
     width_here = D // tensors
     places, holder = owner_layout(owners, slot_count, devices)
     scales = tile_scales(tile_count, heads_here, blocks_here)
-    my_slots = lax.dynamic_slice_in_dim(holder, lax.axis_index("dp") * slot_count, slot_count)
     rank = pair_rank()
-    filled = my_slots >= 0
-    slot_scale = jnp.where(filled, scales[jnp.maximum(my_slots, 0)], 0.0)
+    my_slots = lax.axis_index("dp") * slot_count + jnp.arange(slot_count, dtype=jnp.int32)
+    holds = places[None, :] == my_slots[:, None]
+    slot_scale = jnp.sum(jnp.where(holds, scales[None, :], 0.0), axis=1)
+    filled = jnp.any(holds, axis=1)
     scaled = (master[0] * slot_scale[:, None, None]).astype(jnp.bfloat16)
     half = latents.shape[0]
     tokens = 2 * half

time: 744 us -> 742 us (level)
  transfers between devices with their start and end apart: 8 -> 8, of which waited for: 7 -> 5; matrix products, arithmetic and copies ran while one was open for 3% -> 4% of each run, Pallas kernels for 5% -> 5%
where the time goes in v4:
time: 742 us; the launch traced here: 734 us
  Pallas kernels  650 us (88%)
  local copies, waits for them, and re-layouts  41.7 us (6%)
  other arithmetic  17.7 us (2%)
  waiting for transfers between devices  12.9 us (2%)
  starting transfers between devices  7.92 us (1%)
    pallas_call x1, Pallas kernels, reduce_slots(): pl.pallas_call(reduce_kernel, out_shape=[pltpu.HBM((2, slot_count, width,...  265 us
    pallas_call x1, Pallas kernels, gather_slots(): pl.pallas_call(gather_kernel, out_shape=[pltpu.HBM((16,) + scaled.shape,...  239 us
    pallas_call x13, Pallas kernels, call(): pl.pallas_call(body, grid_spec=pltpu.PrefetchScalarGridSpec(num_scalar_pr...  129 us
    pallas_call x1, Pallas kernels, adam_slots(): pl.pallas_call(step, in_specs=[scalars, scalars] + [ANY] * 4, out_specs=[...  17.8 us
  transfers between devices with their start and end apart: 8, of which 5 were waited for; matrix products, arithmetic and copies ran while one was open for 4% of the time, Pallas kernels for 5%

profile of v4, /device:TPU:9, one launch (start us, length us, event | category | flops | bytes accessed | tf_op | source)
XLA Modules:
  0.0 733.9 jit_solution(4540573338754287852)
XLA Ops:
  0.7 0.9 convert_reduce_fusion
  1.6 1.2 iota_add_fusion.1
  2.8 1.0 pad.48.lat
  3.8 1.0 pad.49.cot
  6.0 3.7 fusion.own
  9.8 238.6 %shard_map.248 = (bf16[16,9,1536,128]{3,2,1,0:T(8,128)(2,1)}, bf16[2,144,1536]{2,1,0:T(8,128)(2,1)}, bf16[2,144,1536]{2,1,0:T(8,128)(2,1)}, bf16[512,1536]{1,0:T(8,128)(2,1)}, f32[104,128]{1,0:T(8,128)}) custom-call(bf16[9,1536,128]{2,1,0:T(8,128)(2,1)S(1)} %fusion.own, bf16[144,1536]{1,0:T(8,128)(2,1)S(1)} %pad.48.lat, bf16[144,1536]{1,0:T(8,128)(2,1)S(1)} %pad.49.cot, ...), custom_call_target="tpu_custom_call" | custom-call | tf_op jit(solution)/shard_map/pallas_call | solution.py:393
  248.4 0.8 slice.105
  249.9 1.2 slice_bitcast_fusion.3
  252.3 1.4 fusion.6.rows_ref.refs_17_
  253.7 1.0 fusion.16
  255.3 8.6 %shard_map.249 = (bf16[272,1536]{1,0:T(8,128)(2,1)}, f32[2,272,768]{2,1,0:T(8,128)}, bf16[272,768]{1,0:T(8,128)(2,1)}, f32[272,128]{1,0:T(8,128)}) custom-call(s32[118]{0:T(128)S(1)} %get-tuple-element.195._.where, f32[272,1536]{1,0:T(8,128)} %fusion.6.rows_ref.refs_17_, f32[6,1536]{1,0:T(8,128)} %bitcast_add_fusion.mod_ref, f32[10,768]{1,0:T(8,128)} %reshape.198.vec_ref, ...), custom_call_target="tpu_custom_call" | custom-call | tf_op jit(solution)/shard_map/pallas_call | solution.py:1132
  263.9 1.2 collective-permute-start
  267.7 1.5 collective-permute-done.other_ref.sqo_ref
  269.9 8.3 %shard_map.250 = (bf16[272,768]{1,0:T(8,128)(2,1)}, bf16[272,768]{1,0:T(8,128)(2,1)}, bf16[6,272,128]{2,1,0:T(8,128)(2,1)}, bf16[272,1536]{1,0:T(8,128)(2,1)}) custom-call(s32[118]{0:T(128)S(1)} %get-tuple-element.195._.where, f32[2,272,768]{2,1,0:T(8,128)} %get-tuple-element.94.pre_ref, bf16[272,768]{1,0:T(8,128)(2,1)} %get-tuple-element.95.value_ref.v_ref, ...), custom_call_target="tpu_custom_call" | custom-call | tf_op jit(solution)/shard_map/pallas_call | solution.py:1132
  278.2 1.0 collective-permute-start.1
  280.0 1.2 pad_bitcast_fusion.5.refs_0_
  281.4 0.9 slice_bitcast_fusion.1
  282.4 8.0 %shard_map.251 = (f32[512,768]{1,0:T(8,128)}, bf16[512,768]{1,0:T(8,128)(2,1)}, f32[512,128]{1,0:T(8,128)}) custom-call(s32[118]{0:T(128)S(1)} %get-tuple-element.195._.where, bf16[512,1536]{1,0:T(8,128)(2,1)} %get-tuple-element.100.text_ref, f32[10,768]{1,0:T(8,128)} %reshape.198.vec_ref, bf16[144,1536,128]{2,1,0:T(8,128)(2,1)} %bitcast.63, ...), custom_call_target="tpu_custom_call" | custom-call | tf_op jit(solution)/shard_map/pallas_call | solution.py:1132
  290.4 1.7 copy.48
  292.1 5.6 collective-permute-done.1.other_ref
  297.8 6.1 shard_map.252
  304.6 1.4 fusion.8.cot_ref
  305.9 2.0 collective-permute-done.2.other_ref.sqo_ref
  308.6 6.9 shard_map.253
  317.7 10.2 %shard_map.254 = (bf16[272,1536]{1,0:T(8,128)(2,1)}, bf16[272,4480]{1,0:T(8,128)(2,1)}) custom-call(s32[118]{0:T(128)S(1)} %get-tuple-element.195._.where, bf16[144,1536,128]{2,1,0:T(8,128)(2,1)} %bitcast.81, f32[6,1536]{1,0:T(8,128)} %bitcast_add_fusion.mod_ref, f32[272,1536]{1,0:T(8,128)} %fusion.8.cot_ref), custom_call_target="tpu_custom_call" | custom-call | tf_op jit(solution)/shard_map/pallas_call | solution.py:1132
  327.8 1.6 copy.51
  329.5 1.6 copy.50
  331.1 1.2 pad_bitcast_fusion.3.refs_6_
  332.3 1.2 pad_bitcast_fusion.4.refs_2_
  333.5 0.9 copy-done.11
  334.4 19.1 %shard_map.255 = (f32[272,1536]{1,0:T(8,128)}, bf16[272,1536]{1,0:T(8,128)(2,1)}, bf16[35,272,128]{2,1,0:T(8,128)(2,1)}, bf16[35,272,128]{2,1,0:T(8,128)(2,1)}, ...) custom-call(s32[118]{0:T(128)S(1)} %get-tuple-element.195._.where, bf16[144,1536,128]{2,1,0:T(8,128)(2,1)} %bitcast.82, ...), custom_call_target="tpu_custom_call" | custom-call | tf_op jit(solution)/shard_map/pallas_call | solution.py:1132
  353.5 0.8 collective-permute-start.4
  354.9 1.5 fusion.27
  356.4 1.6 copy.52
  358.1 11.0 %shard_map.256.y3.refs_20_ = bf16[272,1536]{1,0:T(8,128)(2,1)} custom-call(s32[118]{0:T(128)S(1)} %get-tuple-element.195._.where, bf16[144,1536,128]{2,1,0:T(8,128)(2,1)} %bitcast.83, bf16[35,272,128]{2,1,0:T(8,128)(2,1)} %get-tuple-element.123.hidden_ref.refs_16_), custom_call_target="tpu_custom_call" | custom-call | tf_op jit(solution)/shard_map/pallas_call | solution.py:1132
  369.1 1.2 pad_bitcast_fusion.2.refs_5_
  370.3 0.9 copy-done.10
  371.2 13.1 %shard_map.257 = (f32[272,1536]{1,0:T(8,128)}, bf16[272,1536]{1,0:T(8,128)(2,1)}, f32[272,768]{1,0:T(8,128)}, f32[512,768]{1,0:T(8,128)}, bf16[6,512,128]{2,1,0:T(8,128)(2,1)}, /*index=5*/f32[272,128]{1,0:T(8,128)}) custom-call(s32[118]{0:T(128)S(1)} %get-tuple-element.195._.where, f32[272,1536]{1,0:T(8,128)} %fusion.8.cot_ref, ...), custom_call_target="tpu_custom_call" | custom-call | tf_op jit(solution)/shard_map/pallas_call | solution.py:1132
  384.3 1.0 collective-permute-start.5
  385.5 2.9 collective-permute-done.5.sumo_ref
  389.1 6.4 shard_map.258
  395.5 1.1 collective-permute-start.6
  396.6 0.8 slice.114
  397.5 2.1 gather_fusion
  401.1 1.2 pad_bitcast_fusion.1.refs_4_
  402.3 7.1 shard_map.259
  409.4 0.8 collective-permute-done.6.other_ref
  410.2 0.8 slice.118
  411.1 14.6 %shard_map.260 = (f32[272,1536]{1,0:T(8,128)}, bf16[272,1536]{1,0:T(8,128)(2,1)}, f32[2,272,768]{2,1,0:T(8,128)}, bf16[6,272,128]{2,1,0:T(8,128)(2,1)}, f32[272,128]{1,0:T(8,128)}, /*index=5*/f32[2,1536]{1,0:T(2,128)}) custom-call(s32[118]{0:T(128)S(1)} %get-tuple-element.195._.where, f32[272,1536]{1,0:T(8,128)} %get-tuple-element.128.dx_in, ...), custom_call_target="tpu_custom_call" | custom-call | tf_op jit(solution)/shard_map/pallas_call | solution.py:1132
  425.7 1.4 collective-permute-start.7
  427.1 0.8 fusion.28
  427.9 1.6 copy.54
  429.5 1.1 pad_bitcast_fusion.refs_1_
  431.3 9.8 %shard_map.261 = (bf16[6,272,128]{2,1,0:T(8,128)(2,1)}, bf16[6,272,128]{2,1,0:T(8,128)(2,1)}, f32[8,768]{1,0:T(8,128)}, bf16[272,1536]{1,0:T(8,128)(2,1)}, f32[2,1536]{1,0:T(2,128)}) custom-call(s32[118]{0:T(128)S(1)} %get-tuple-element.195._.where, f32[272,1536]{1,0:T(8,128)} %fusion.6.rows_ref.refs_17_, f32[2,272,768]{2,1,0:T(8,128)} %get-tuple-element.94.pre_ref, ...), custom_call_target="tpu_custom_call" | custom-call | tf_op jit(solution)/shard_map/pallas_call | solution.py:1132
  441.1 0.7 reshape.201
  442.1 0.8 concatenate.30
  443.6 264.9 %shard_map.262 = (bf16[2,9,1536,128]{3,2,1,0:T(8,128)(2,1)}, f32[328,128]{1,0:T(8,128)}, bf16[272,1536]{1,0:T(8,128)(2,1)}, f32[272,1536]{1,0:T(8,128)}, bf16[27...) custom-call(s32[144]{0:T(256)} %gather_fusion, ...), custom_call_target="tpu_custom_call" | custom-call | tf_op jit(solution)/shard_map/pallas_call | solution.py:869
  708.5 1.0 slice.126
  709.4 0.9 slice.125
  710.4 2.5 slice_select_fusion
  712.9 0.9 slice_select_fusion.1
  713.8 0.7 multiply_subtract_fusion
  714.6 17.8 %shard_map.263 = (f32[1,9,1536,128]{3,2,1,0:T(8,128)}, f32[1,9,1536,128]{3,2,1,0:T(8,128)}, f32[1,9,1536,128]{3,2,1,0:T(8,128)}) custom-call(f32[9]{0:T(128)S(1)} %copy-done.3, s32[9]{0:T(128)S(1)} %convert_element_type.56.fill_ref, bf16[2,9,1536,128]{3,2,1,0:T(8,128)(2,1)} %get-tuple-element.166.grads, f32[1,9,1536,128]{3,2,1,0:T(8,128)} %weight.1, ...), custom_call_target="tpu_custom_call" | custom-call | tf_op jit(solution)/shard_map/pallas_call | solution.py:1025
  732.5 1.0 multiply_subtract_fusion.1
  (124 shorter events, 15.6 us)
Async XLA Ops:
  0.6 253.1 %copy-start = (f32[16,6,1536]{2,0,1:T(8,128)S(1)}, f32[16,6,1536]{2,0,1:T(8,128)}, u32[]{:S(2)}) copy-start(f32[16,6,1536]{2,0,1:T(8,128)} %param.23) | copy-start | bytes 1769476
  0.7 4.2 copy-start.30
  0.7 5.0 copy-start.18
  2.8 7.0 copy-start.32
  6.0 3.8 copy-start.2
  251.1 3.6 copy-start.6
  263.9 5.4 collective-permute-start
  269.3 0.6 copy-start.16
  269.9 9.3 %copy-start.13 = (bf16[272,1536]{1,0:T(8,128)(2,1)S(1)}, bf16[272,1536]{1,0:T(8,128)(2,1)}, u32[]{:S(2)}) copy-start(bf16[272,1536]{1,0:T(8,128)(2,1)} %get-tuple-element.102) | copy-start | bytes 2506756
  278.2 19.5 %collective-permute-start.1 = (bf16[272,1536]{1,0:T(8,128)(2,1)}, bf16[272,1536]{1,0:T(8,128)(2,1)}, u32[]{:S(2)}, u32[]{:S(2)}) collective-permute-start(bf16[272,1536]{1,0:T(8,128)(2,1)} %get-tuple-element.99.part_ref), channel_id=1, source_target_pairs={{0,8},{2,10},{4,12},{6,14},{8,0},{10,2},{12,4},{14,6},{16,24},{18,... | collective-permute-start | bytes 2506760 | tf_op jit(solution)/shard_map/ppermute | solution.py:111
  280.0 1.5 copy-start.15
  282.4 8.0 %copy-start.4 = (bf16[512,1536]{1,0:T(8,128)(2,1)S(1)}, bf16[512,1536]{1,0:T(8,128)(2,1)}, u32[]{:S(2)}) copy-start(bf16[512,1536]{1,0:T(8,128)(2,1)} %get-tuple-element.100.text_ref) | copy-start | bytes 4718596
  297.8 6.8 copy-start.8
  297.8 6.8 copy-start.9
  303.8 4.1 collective-permute-start.2
  308.0 0.7 copy-start.17
  308.6 8.9 %copy-start.31 = (s32[118]{0:T(128)S(1)}, s32[118]{0:T(128)}, u32[]{:S(2)}) copy-start(s32[118]{0:T(128)} %get-tuple-element.194) | copy-start | bytes 1420
  315.5 18.0 %collective-permute-start.3 = (bf16[272,1536]{1,0:T(8,128)(2,1)}, bf16[272,1536]{1,0:T(8,128)(2,1)S(1)}, u32[]{:S(2)}, u32[]{:S(2)}) collective-permute-start(bf16[272,1536]{1,0:T(8,128)(2,1)} %get-tuple-element.115.part_ref), channel_id=1, source_target_pairs={{0,8},{2,10},{4,12},{6,14},{8,0},{10,2},{12,4},{14,6},{16,24},{18,... | collective-permute-start | bytes 2506760 | tf_op jit(solution)/shard_map/ppermute | solution.py:111
  333.5 0.9 copy-start.11
  353.5 16.8 %collective-permute-start.4 = (bf16[272,1536]{1,0:T(8,128)(2,1)}, bf16[272,1536]{1,0:T(8,128)(2,1)S(1)}, u32[]{:S(2)}, u32[]{:S(2)}) collective-permute-start(bf16[272,1536]{1,0:T(8,128)(2,1)} %get-tuple-element.122.part_ref.da2), channel_id=1, source_target_pairs={{0,8},{2,10},{4,12},{6,14},{8,0},{10,2},{12,4},{14,6},{16,24},{18,... | collective-permute-start | bytes 2506760 | tf_op jit(solution)/shard_map/ppermute | solution.py:111
  370.3 0.9 copy-start.10
  371.2 14.1 %copy-start.33 = (s32[9]{0:T(128)S(1)}, s32[9]{0:T(128)}, u32[]{:S(2)}) copy-start(s32[9]{0:T(128)} %copy-done.32) | copy-start | bytes 112
  384.3 4.1 collective-permute-start.5
  388.4 0.6 copy-start.20
  389.1 10.6 %copy-start.27 = (f32[1,1536]{1,0:T(1,128)S(1)}, f32[1,1536]{1,0:T(1,128)}, u32[]{:S(2)}) copy-start(f32[1,1536]{1,0:T(1,128)} %get-tuple-element.183) | copy-start | bytes 18436
  389.1 10.6 %copy-start.28 = (f32[1,1536]{1,0:T(1,128)S(1)}, f32[1,1536]{1,0:T(1,128)}, u32[]{:S(2)}) copy-start(f32[1,1536]{1,0:T(1,128)} %get-tuple-element.184) | copy-start | bytes 18436
  389.1 11.3 %copy-start.29 = (f32[1,4480]{1,0:T(1,128)S(1)}, f32[1,4480]{1,0:T(1,128)}, u32[]{:S(2)}) copy-start(f32[1,4480]{1,0:T(1,128)} %get-tuple-element.160) | copy-start | bytes 53764
  395.5 4.9 copy-start.5
  395.5 14.7 %collective-permute-start.6 = (bf16[272,1536]{1,0:T(8,128)(2,1)}, bf16[272,1536]{1,0:T(8,128)(2,1)S(1)}, u32[]{:S(2)}, u32[]{:S(2)}) collective-permute-start(bf16[272,1536]{1,0:T(8,128)(2,1)} %get-tuple-element.133.da3.part_ref), channel_id=1, source_target_pairs={{0,8},{2,10},{4,12},{6,14},{8,0},{10,2},{12,4},{14,6},{16,24},{18,... | collective-permute-start | bytes 2506760 | tf_op jit(solution)/shard_map/ppermute | solution.py:111
  402.3 7.1 copy-start.26
  410.2 0.9 copy-start.14
  425.7 4.9 collective-permute-start.7
  430.7 0.7 copy-start.21
  431.3 10.8 %slice-start = ((f32[11,1536]{1,0:T(8,128)}), f32[3,1536]{1,0:T(4,128)S(1)}, s32[]{:S(2)}) async-start(f32[11,1536]{1,0:T(8,128)} %shard_map.259), calls=%async_computation | async-start | bytes 49152 | tf_op jit(solution)/shard_map/slice | solution.py:1965
  708.5 4.4 copy-start.12
  710.4 3.4 copy-start.7
  710.4 3.4 copy-start.22
  710.4 3.4 copy-start.23
  712.9 1.7 copy-start.3
  714.6 17.9 %copy-start.19 = (f32[1,12160]{1,0:T(1,128)S(1)}, f32[1,12160]{1,0:T(1,128)}, u32[]{:S(2)}) copy-start(f32[1,12160]{1,0:T(1,128)} %param.27) | copy-start | bytes 145924
  714.6 17.9 %copy-start.24 = (f32[1,12160]{1,0:T(1,128)S(1)}, f32[1,12160]{1,0:T(1,128)}, u32[]{:S(2)}) copy-start(f32[1,12160]{1,0:T(1,128)} %param.28) | copy-start | bytes 145924
  714.6 17.9 %copy-start.25 = (f32[1,12160]{1,0:T(1,128)S(1)}, f32[1,12160]{1,0:T(1,128)}, u32[]{:S(2)}) copy-start(f32[1,12160]{1,0:T(1,128)} %param.29) | copy-start | bytes 145924
  714.6 18.9 %copy-start.1 = (f32[16,6,1536]{2,0,1:T(8,128)S(1)}, f32[16,6,1536]{2,0,1:T(8,128)}, u32[]{:S(2)}) copy-start(f32[16,6,1536]{2,0,1:T(8,128)} %param.23) | copy-start | bytes 1769476

commit v5 on v4

--- a/solution.py
+++ b/solution.py
@@ -144,16 +144,17 @@
         for flip in (0, 1):
             if k or flip:
                 friends.append((column_of(z, y, x, k), core if flip == 0 else 1 - core))
-    friends.append((column_of(z, y, 1 - x, 0), core))
-    friends.append((column_of(z, 1 - y, x, 0), core))
+    for side in (core, 1 - core):
+        friends.append((column_of(z, y, 1 - x, 0), side))
+        friends.append((column_of(z, 1 - y, x, 0), side))
     for friend in friends:
         pl.semaphore_signal(barrier, inc=1, device_id=friend, device_id_type=MESH)
     pl.semaphore_wait(barrier, len(friends))
 
 
 def gather_kernel(
-    own, lat, cot, text, small, out, lats, cots, texts, smalls, clip_s, clip_r,
-    near_s, col_r, x_s, x_r, y_s, y_r, sib_s, sib_r,
+    own, lat, cot, text, small, out, lats, cots, texts, smalls, relay_a, relay_b, clip_s, clip_r,
+    out_s, out_r, over_s, over_r, near_s, col_r, x_s, x_r, y_s, y_r, sib_s, sib_r,
 ):
     chip, core, z, y, x = place_of()
     rank = z % 2
@@ -166,6 +167,17 @@
     batch = max(n for n in (1, 2, 3) if own.shape[0] % n == 0)
     batches = own.shape[0] // batch
     turns = 4 * batches
+    mine, other = core * half, (1 - core) * half
+    sibling = (chip, 1 - core)
+    tail = pl.ds((batches - 1) * batch, batch)
+
+    def outward(n, h):
+        rows = pl.ds(h * half + n * part, part)
+        return pltpu.make_async_remote_copy(
+            src_ref=own.at[tail, rows, :], dst_ref=(relay_a, relay_b)[n].at[core],
+            send_sem=out_s.at[2 * n + h], recv_sem=out_r.at[2 * n + core],
+            device_id=((at_x, at_y)[n], h), device_id_type=MESH,
+        )
 
     def case(s):
         late = jnp.maximum(s - batches, 0)
@@ -193,6 +205,9 @@
         )
         return go, pltpu.make_async_copy(src, dst, recv)
 
+    for n in range(2):
+        for h in range(2):
+            outward(n, h).start()
     for g in range(batches):
         for j in range(2):
             for h in range(2):
@@ -267,96 +282,166 @@
         for h in range(2):
             hand_out(h, n, False)
 
-    mine, other = core * half, (1 - core) * half
-    sibling = (chip, 1 - core)
-
-    def to_x(s, n):
+
+    def spans(n, wide):
+        part_a, part_b = (mine, part), (mine + part, part)
+        if wide:
+            return part_b, part_a
+        return (part_a, part_b) if n else ((mine, half), (mine, half))
+
+    def over_x(s, n, wide, coming=0):
         k, g = case(s)
         i = turns * n + s
-        unit = toggled(z, y, x, n, 0, k)
-        return remote(unit, g, mine, part if n else half, x_s.at[i], x_r.at[i], (at_x, core))
-
-    def from_x(s, n):
+        first, count = spans(n, wide)[0]
+        unit = toggled(z, y, x, n, coming, k)
+        return remote(unit, g, first, count, x_s.at[i], x_r.at[i], (at_x, core))
+
+    def over_y(s, n, wide, coming=0):
         k, g = case(s)
         i = turns * n + s
-        unit = toggled(z, y, x, n, 1, k)
-        return remote(unit, g, mine, part if n else half, x_s.at[i], x_r.at[i], (at_x, core))
-
-    def to_y(s, n):
+        first, count = spans(n, wide)[1]
+        unit = toggled(z, y, x, coming, n, k)
+        return remote(unit, g, first, count, y_s.at[i], y_r.at[i], (at_y, core))
+
+    def to_sib(s, column, piece, away=False):
         k, g = case(s)
-        i = turns * n + s
-        unit = toggled(z, y, x, 0, n, k)
-        first, count = (mine + part, part) if n else (mine, half)
-        return remote(unit, g, first, count, y_s.at[i], y_r.at[i], (at_y, core))
-
-    def from_y(s, n):
-        k, g = case(s)
-        i = turns * n + s
-        unit = toggled(z, y, x, 1, n, k)
-        first, count = (mine + part, part) if n else (mine, half)
-        return remote(unit, g, first, count, y_s.at[i], y_r.at[i], (at_y, core))
-
-    def to_sib(s, n, away=False):
-        k, g = case(s)
-        i = turns * n + s
-        unit = toggled(z, y, x, int(n in (2, 3, 4)), int(n in (1, 3, 4)), k)
-        first = (other if away else mine) + (part if n == 4 else 0)
-        return remote(
-            unit, g, first, part if n >= 3 else half, sib_s.at[i], sib_r.at[i], sibling
-        )
-
-    def column_in(s):
+        i = turns * ({(0, 2): 0, (1, 2): 1, (2, 2): 2}.get((column, piece), 2 * column + piece - 1)) + s
+        unit = toggled(z, y, x, column // 2, column % 2, k)
+        first = (other if away else mine) + (part if piece == 1 else 0)
+        count = half if piece == 2 else part
+        return remote(unit, g, first, count, sib_s.at[i], sib_r.at[i], sibling)
+
+    def column_in(s, wide):
         k, g = case(s)
         unit = toggled(z, y, x, 0, 0, k)
         piece = out.at[
             unit, pl.ds(g * batch, batch), pl.ds(pl.multiple_of(mine, 16), half), :
         ]
         pltpu.make_async_copy(piece, piece, col_r.at[unit // 4 * batches + g]).wait()
-        to_x(s, 0).start()
-        to_y(s, 0).start()
-        to_sib(s, 0).start()
-
-    def side_in(s):
-        from_x(s, 0).wait_recv()
-        to_y(s, 1).start()
-        to_sib(s, 1).start()
-        from_y(s, 0).wait_recv()
-        to_x(s, 1).start()
-        to_sib(s, 2).start()
-
-    def corner_in(s):
-        from_x(s, 1).wait_recv()
-        to_sib(s, 3).start()
-        from_y(s, 1).wait_recv()
-        to_sib(s, 4).start()
+        over_x(s, 0, wide).start()
+        over_y(s, 0, wide).start()
+        to_sib(s, 0, 2).start()
+        if wide:
+            for n, (spot, first) in enumerate(((toggled(z, y, x, 0, 1, k), mine), (toggled(z, y, x, 1, 0, k), mine + part))):
+                piece = out.at[
+                    spot, pl.ds(g * batch, batch), pl.ds(pl.multiple_of(first, 16), part), :
+                ]
+                pltpu.make_async_copy(piece, piece, over_r.at[4 * n + spot // 4]).wait()
+            over_y(s, 1, wide).start()
+            to_sib(s, 1, 0).start()
+            over_x(s, 1, wide).start()
+            to_sib(s, 2, 1).start()
+
+    def side_in(s, wide):
+        over_x(s, 0, wide, 1).wait_recv()
+        if wide:
+            to_sib(s, 1, 1).start()
+        else:
+            over_y(s, 1, wide).start()
+            to_sib(s, 1, 2).start()
+        over_y(s, 0, wide, 1).wait_recv()
+        if wide:
+            to_sib(s, 2, 0).start()
+        else:
+            over_x(s, 1, wide).start()
+            to_sib(s, 2, 2).start()
+
+    def corner_in(s, wide):
+        over_x(s, 1, wide, 1).wait_recv()
+        to_sib(s, 3, 1 if wide else 0).start()
+        over_y(s, 1, wide, 1).wait_recv()
+        to_sib(s, 3, 0 if wide else 1).start()
+
+    def either(s, act):
+        _, g = case(s)
+        wide = g == batches - 1
+
+        @pl.when(wide)
+        def _():
+            act(s, True)
+
+        @pl.when(jnp.logical_not(wide))
+        def _():
+            act(s, False)
+
+    def onward(n, t, j):
+        origin = (at_x, at_y)[n]
+        src = (relay_a, relay_b)[n].at[t]
+        rows = pl.ds(pl.multiple_of(mine + n * part, 16), part)
+        dst = out.at[origin, tail, rows, :]
+        high = (z // 2 + j) % 2
+        recv = over_r.at[4 * n + z]
+        go = pltpu.make_async_remote_copy(
+            src_ref=src, dst_ref=dst, send_sem=over_s.at[4 * n + 2 * t + j], recv_sem=recv,
+            device_id=((2 * high + t) * 4 + 2 * y + x, core), device_id_type=MESH,
+        )
+        return go, pltpu.make_async_copy(src, dst, recv)
+
+    def pass_on(n):
+        for t in range(2):
+            piece = (relay_a, relay_b)[n].at[t]
+            pltpu.make_async_copy(piece, piece, out_r.at[2 * n + t]).wait()
+            for j in range(2):
+                go, here = onward(n, t, j)
+                if j == 1:
+                    go.start()
+                    continue
+
+                @pl.when(rank == t)
+                def _():
+                    here.start()
+
+                @pl.when(rank != t)
+                def _():
+                    go.start()
 
     def turn(step, carry):
         @pl.when(step < turns)
         def _():
-            column_in(step)
+            either(step, column_in)
 
         @pl.when(jnp.logical_and(step >= 1, step < turns + 1))
         def _():
-            side_in(step - 1)
+            either(step - 1, side_in)
 
         @pl.when(step >= 2)
         def _():
-            corner_in(step - 2)
+            either(step - 2, corner_in)
+
+        @pl.when(step == 0)
+        def _():
+            pass_on(0)
+            pass_on(1)
 
         return carry
 
     lax.fori_loop(0, turns + 2, turn, 0)
 
+    def close(s, wide):
+        for n in range(2):
+            over_x(s, n, wide).wait_send()
+            over_y(s, n, wide).wait_send()
+        pieces = [(0, 2), (3, 0), (3, 1)]
+        pieces += [(1, 0), (1, 1), (2, 0), (2, 1)] if wide else [(1, 2), (2, 2)]
+        for column, piece in pieces:
+            to_sib(s, column, piece).wait_send()
+            to_sib(s, column, piece, True).wait_recv()
+
     def settle(s, carry):
-        for n in range(2):
-            to_x(s, n).wait_send()
-            to_y(s, n).wait_send()
-        for n in range(5):
-            to_sib(s, n).wait_send()
-            to_sib(s, n, True).wait_recv()
+        either(s, close)
         return carry
 
     lax.fori_loop(0, turns, settle, 0)
+    for n in range(2):
+        for h in range(2):
+            outward(n, h).wait_send()
+        for t in range(2):
+            onward(n, t, 1)[0].wait_send()
+
+            @pl.when(rank != t)
+            def _():
+                onward(n, t, 0)[0].wait_send()
+
     for g in range(batches):
         for j in range(2):
             for h in range(2):
@@ -389,7 +474,9 @@
         return everyone, lats, cots, text, small
     dma = pltpu.SemaphoreType.DMA
     turns = 4 * scaled.shape[0] // max(n for n in (1, 2, 3) if scaled.shape[0] % n == 0)
-    counts = (7, 7, turns, turns) + (2 * turns,) * 4 + (5 * turns,) * 2
+    counts = (7, 7, 4, 4, 8, 8, turns, turns) + (2 * turns,) * 4 + (7 * turns,) * 2
+    batch = 4 * scaled.shape[0] // turns
+    relay = pltpu.HBM((2, batch, scaled.shape[1] // 4, scaled.shape[2]), scaled.dtype)
     everyone, *rest = pl.pallas_call(
         gather_kernel,
         out_shape=[
@@ -398,15 +485,17 @@
             pltpu.HBM((2,) + cot.shape, cot.dtype),
             pltpu.HBM(text.shape, text.dtype),
             pltpu.HBM(small.shape, small.dtype),
+            relay,
+            relay,
         ],
         in_specs=[ANY] * 5,
-        out_specs=[ANY] * 5,
+        out_specs=[ANY] * 7,
         scratch_shapes=[dma((n,)) for n in counts],
         compiler_params=pltpu.CompilerParams(
             collective_id=0, has_side_effects=True, vmem_limit_bytes=4 * MIB
         ),
     )(scaled, lat, cot, pltpu.with_memory_space_constraint(text, pltpu.HBM), small)
-    return everyone.reshape((-1,) + scaled.shape[1:]), *rest
+    return everyone.reshape((-1,) + scaled.shape[1:]), *rest[:4]
 
 
 def toggled(z, y, x, flip_y, flip_x, k):
@@ -1993,7 +2082,7 @@
         slot_count,
     )
     output, grad_input = (
-        jnp.where(lax.axis_index("tensor") == 0, v[:half], v[half:tokens])
+        lax.dynamic_slice_in_dim(v, lax.axis_index("tensor") * half, half, 0)
         for v in (output, grad_input)
     )
     new_master, new_first, new_second = adam_slots(

time: 742 us -> 737 us (level)
  Pallas kernels: 650 us -> 642 us
    pallas_call x1, Pallas kernels: 239 us -> 226 us  [gather_slots(): pl.pallas_call(gather_kernel, out_shape=[pltpu.HBM((16,) + scaled.shape,...]
  transfers between devices with their start and end apart: 8 -> 8, of which waited for: 5 -> 6; matrix products, arithmetic and copies ran while one was open for 4% -> 4% of each run, Pallas kernels for 5% -> 5%
where the time goes in v5:
time: 737 us; the launch traced here: 726 us
  Pallas kernels  642 us (87%)
  local copies, waits for them, and re-layouts  44.7 us (6%)
  other arithmetic  14.3 us (2%)
  waiting for transfers between devices  14.2 us (2%)
  starting transfers between devices  7.78 us (1%)
    pallas_call x1, Pallas kernels, reduce_slots(): pl.pallas_call(reduce_kernel, out_shape=[pltpu.HBM((2, slot_count, width,...  269 us
    pallas_call x1, Pallas kernels, gather_slots(): pl.pallas_call(gather_kernel, out_shape=[pltpu.HBM((16,) + scaled.shape,...  226 us
    pallas_call x13, Pallas kernels, call(): pl.pallas_call(body, grid_spec=pltpu.PrefetchScalarGridSpec(num_scalar_pr...  129 us
    pallas_call x1, Pallas kernels, adam_slots(): pl.pallas_call(step, in_specs=[scalars, scalars] + [ANY] * 4, out_specs=[...  17.1 us
  transfers between devices with their start and end apart: 8, of which 6 were waited for; matrix products, arithmetic and copies ran while one was open for 4% of the time, Pallas kernels for 5%

profile of v5, /device:TPU:9, one launch (start us, length us, event | category | flops | bytes accessed | tf_op | source)
XLA Modules:
  0.0 725.8 jit_solution(5021048372379368782)
XLA Ops:
  0.7 0.9 convert_reduce_fusion
  1.6 1.2 iota_add_fusion.1
  2.8 1.0 pad.48.lat
  3.8 1.0 pad.49.cot
  6.0 3.7 fusion.own
  9.8 226.4 %shard_map.248 = (bf16[16,9,1536,128]{3,2,1,0:T(8,128)(2,1)}, bf16[2,144,1536]{2,1,0:T(8,128)(2,1)}, bf16[2,144,1536]{2,1,0:T(8,128)(2,1)}, bf16[512,1536]{1,0:T...) custom-call(bf16[9,1536,128]{2,1,0:T(8,128)(2,1)S(1)} %fusion.own, ...), custom_call_target="tpu_custom_call" | custom-call | tf_op jit(solution)/shard_map/pallas_call | solution.py:480
  236.2 0.8 slice.93
  237.7 1.2 slice_bitcast_fusion.3
  240.1 1.4 fusion.6.rows_ref.refs_17_
  241.5 1.0 fusion.16
  243.1 8.6 %shard_map.249 = (bf16[272,1536]{1,0:T(8,128)(2,1)}, f32[2,272,768]{2,1,0:T(8,128)}, bf16[272,768]{1,0:T(8,128)(2,1)}, f32[272,128]{1,0:T(8,128)}) custom-call(s32[118]{0:T(128)S(1)} %get-tuple-element.195._.where, f32[272,1536]{1,0:T(8,128)} %fusion.6.rows_ref.refs_17_, f32[6,1536]{1,0:T(8,128)} %bitcast_add_fusion.mod_ref, f32[10,768]{1,0:T(8,128)} %reshape.198.vec_ref, ...), custom_call_target="tpu_custom_call" | custom-call | tf_op jit(solution)/shard_map/pallas_call | solution.py:1221
  251.7 1.8 collective-permute-start
  256.1 1.3 collective-permute-done.other_ref.sqo_ref
  258.1 8.3 %shard_map.250 = (bf16[272,768]{1,0:T(8,128)(2,1)}, bf16[272,768]{1,0:T(8,128)(2,1)}, bf16[6,272,128]{2,1,0:T(8,128)(2,1)}, bf16[272,1536]{1,0:T(8,128)(2,1)}) custom-call(s32[118]{0:T(128)S(1)} %get-tuple-element.195._.where, f32[2,272,768]{2,1,0:T(8,128)} %get-tuple-element.94.pre_ref, bf16[272,768]{1,0:T(8,128)(2,1)} %get-tuple-element.95.value_ref.v_ref, ...), custom_call_target="tpu_custom_call" | custom-call | tf_op jit(solution)/shard_map/pallas_call | solution.py:1221
  266.4 1.5 collective-permute-start.1
  268.6 1.2 pad_bitcast_fusion.5.refs_0_
  270.0 0.9 slice_bitcast_fusion.1
  271.0 7.9 %shard_map.251 = (f32[512,768]{1,0:T(8,128)}, bf16[512,768]{1,0:T(8,128)(2,1)}, f32[512,128]{1,0:T(8,128)}) custom-call(s32[118]{0:T(128)S(1)} %get-tuple-element.195._.where, bf16[512,1536]{1,0:T(8,128)(2,1)} %get-tuple-element.100.text_ref, f32[10,768]{1,0:T(8,128)} %reshape.198.vec_ref, bf16[144,1536,128]{2,1,0:T(8,128)(2,1)} %bitcast.63, ...), custom_call_target="tpu_custom_call" | custom-call | tf_op jit(solution)/shard_map/pallas_call | solution.py:1221
  278.9 1.7 copy.48
  280.6 5.4 collective-permute-done.1.other_ref
  286.0 6.1 shard_map.252
  292.1 1.3 collective-permute-start.2
  293.4 1.4 fusion.8.cot_ref
  294.8 1.4 collective-permute-done.2.other_ref.sqo_ref
  296.9 6.9 shard_map.253
  303.8 1.3 collective-permute-start.3
  306.5 10.2 %shard_map.254 = (bf16[272,1536]{1,0:T(8,128)(2,1)}, bf16[272,4480]{1,0:T(8,128)(2,1)}) custom-call(s32[118]{0:T(128)S(1)} %get-tuple-element.195._.where, bf16[144,1536,128]{2,1,0:T(8,128)(2,1)} %bitcast.81, f32[6,1536]{1,0:T(8,128)} %bitcast_add_fusion.mod_ref, f32[272,1536]{1,0:T(8,128)} %fusion.8.cot_ref), custom_call_target="tpu_custom_call" | custom-call | tf_op jit(solution)/shard_map/pallas_call | solution.py:1221
  316.7 1.6 copy.51
  318.4 1.6 copy.50
  320.0 1.2 pad_bitcast_fusion.3.refs_6_
  321.2 1.2 pad_bitcast_fusion.4.refs_2_
  322.4 0.9 copy-done.11
  323.2 19.1 %shard_map.255 = (f32[272,1536]{1,0:T(8,128)}, bf16[272,1536]{1,0:T(8,128)(2,1)}, bf16[35,272,128]{2,1,0:T(8,128)(2,1)}, bf16[35,272,128]{2,1,0:T(8,128)(2,1)}, ...) custom-call(s32[118]{0:T(128)S(1)} %get-tuple-element.195._.where, bf16[144,1536,128]{2,1,0:T(8,128)(2,1)} %bitcast.82, ...), custom_call_target="tpu_custom_call" | custom-call | tf_op jit(solution)/shard_map/pallas_call | solution.py:1221
  343.2 1.5 fusion.27
  344.7 1.6 copy.52
  346.3 11.0 %shard_map.256.y3.refs_20_ = bf16[272,1536]{1,0:T(8,128)(2,1)} custom-call(s32[118]{0:T(128)S(1)} %get-tuple-element.195._.where, bf16[144,1536,128]{2,1,0:T(8,128)(2,1)} %bitcast.83, bf16[35,272,128]{2,1,0:T(8,128)(2,1)} %get-tuple-element.123.hidden_ref.refs_16_), custom_call_target="tpu_custom_call" | custom-call | tf_op jit(solution)/shard_map/pallas_call | solution.py:1221
  357.4 1.2 pad_bitcast_fusion.2.refs_5_
  358.6 0.9 collective-permute-done.4.other_ref
  359.5 0.9 copy-done.10
  360.4 13.1 %shard_map.257 = (f32[272,1536]{1,0:T(8,128)}, bf16[272,1536]{1,0:T(8,128)(2,1)}, f32[272,768]{1,0:T(8,128)}, f32[512,768]{1,0:T(8,128)}, bf16[6,512,128]{2,1,0:T(8,128)(2,1)}, /*index=5*/f32[272,128]{1,0:T(8,128)}) custom-call(s32[118]{0:T(128)S(1)} %get-tuple-element.195._.where, f32[272,1536]{1,0:T(8,128)} %fusion.8.cot_ref, ...), custom_call_target="tpu_custom_call" | custom-call | tf_op jit(solution)/shard_map/pallas_call | solution.py:1221
  374.0 3.5 collective-permute-done.5.sumo_ref
  378.2 6.4 shard_map.258
  385.1 0.8 slice.102
  386.1 2.1 gather_fusion
  389.7 1.2 pad_bitcast_fusion.1.refs_4_
  390.8 7.1 shard_map.259
  398.0 1.6 collective-permute-done.6.other_ref
  399.6 0.8 slice.106
  400.5 14.6 %shard_map.260 = (f32[272,1536]{1,0:T(8,128)}, bf16[272,1536]{1,0:T(8,128)(2,1)}, f32[2,272,768]{2,1,0:T(8,128)}, bf16[6,272,128]{2,1,0:T(8,128)(2,1)}, f32[272,128]{1,0:T(8,128)}, /*index=5*/f32[2,1536]{1,0:T(2,128)}) custom-call(s32[118]{0:T(128)S(1)} %get-tuple-element.195._.where, f32[272,1536]{1,0:T(8,128)} %get-tuple-element.128.dx_in, ...), custom_call_target="tpu_custom_call" | custom-call | tf_op jit(solution)/shard_map/pallas_call | solution.py:1221
  415.1 0.8 collective-permute-start.7
  415.9 0.8 fusion.28
  416.7 1.6 copy.54
  418.3 1.1 pad_bitcast_fusion.refs_1_
  420.1 9.8 %shard_map.261 = (bf16[6,272,128]{2,1,0:T(8,128)(2,1)}, bf16[6,272,128]{2,1,0:T(8,128)(2,1)}, f32[8,768]{1,0:T(8,128)}, bf16[272,1536]{1,0:T(8,128)(2,1)}, f32[2,1536]{1,0:T(2,128)}) custom-call(s32[118]{0:T(128)S(1)} %get-tuple-element.195._.where, f32[272,1536]{1,0:T(8,128)} %fusion.6.rows_ref.refs_17_, f32[2,272,768]{2,1,0:T(8,128)} %get-tuple-element.94.pre_ref, ...), custom_call_target="tpu_custom_call" | custom-call | tf_op jit(solution)/shard_map/pallas_call | solution.py:1221
  429.9 0.7 reshape.201
  430.9 0.8 concatenate.30
  432.4 269.0 %shard_map.262 = (bf16[2,9,1536,128]{3,2,1,0:T(8,128)(2,1)}, f32[328,128]{1,0:T(8,128)}, bf16[272,1536]{1,0:T(8,128)(2,1)}, f32[272,1536]{1,0:T(8,128)}, bf16[27...) custom-call(s32[144]{0:T(256)} %gather_fusion, ...), custom_call_target="tpu_custom_call" | custom-call | tf_op jit(solution)/shard_map/pallas_call | solution.py:958
  701.4 1.0 slice.110
  702.4 0.9 slice.109
  703.3 2.2 constant_dynamic-slice_fusion
  705.5 0.9 constant_dynamic-slice_fusion.1
  706.4 0.7 multiply_subtract_fusion
  707.2 17.1 %shard_map.263 = (f32[1,9,1536,128]{3,2,1,0:T(8,128)}, f32[1,9,1536,128]{3,2,1,0:T(8,128)}, f32[1,9,1536,128]{3,2,1,0:T(8,128)}) custom-call(f32[9]{0:T(128)S(1)} %copy-done.3, s32[9]{0:T(128)S(1)} %convert_element_type.56.fill_ref, bf16[2,9,1536,128]{3,2,1,0:T(8,128)(2,1)} %get-tuple-element.166.grads, f32[1,9,1536,128]{3,2,1,0:T(8,128)} %weight.1, ...), custom_call_target="tpu_custom_call" | custom-call | tf_op jit(solution)/shard_map/pallas_call | solution.py:1114
  724.4 1.0 multiply_subtract_fusion.1
  (124 shorter events, 15.3 us)
Async XLA Ops:
  0.6 240.9 %copy-start = (f32[16,6,1536]{2,0,1:T(8,128)S(1)}, f32[16,6,1536]{2,0,1:T(8,128)}, u32[]{:S(2)}) copy-start(f32[16,6,1536]{2,0,1:T(8,128)} %param.23) | copy-start | bytes 1769476
  0.7 4.2 copy-start.30
  0.7 5.0 copy-start.18
  2.8 7.0 copy-start.32
  6.0 3.8 copy-start.2
  238.9 3.6 copy-start.6
  251.7 5.8 collective-permute-start
  257.5 0.6 copy-start.15
  258.1 9.8 %copy-start.12 = (bf16[272,1536]{1,0:T(8,128)(2,1)S(1)}, bf16[272,1536]{1,0:T(8,128)(2,1)}, u32[]{:S(2)}) copy-start(bf16[272,1536]{1,0:T(8,128)(2,1)} %get-tuple-element.102) | copy-start | bytes 2506756
  266.4 19.6 %collective-permute-start.1 = (bf16[272,1536]{1,0:T(8,128)(2,1)}, bf16[272,1536]{1,0:T(8,128)(2,1)}, u32[]{:S(2)}, u32[]{:S(2)}) collective-permute-start(bf16[272,1536]{1,0:T(8,128)(2,1)} %get-tuple-element.99.part_ref), channel_id=1, source_target_pairs={{0,8},{2,10},{4,12},{6,14},{8,0},{10,2},{12,4},{14,6},{16,24},{18,... | collective-permute-start | bytes 2506760 | tf_op jit(solution)/shard_map/ppermute | solution.py:111
  268.6 1.5 copy-start.14
  271.0 7.9 %copy-start.4 = (bf16[512,1536]{1,0:T(8,128)(2,1)S(1)}, bf16[512,1536]{1,0:T(8,128)(2,1)}, u32[]{:S(2)}) copy-start(bf16[512,1536]{1,0:T(8,128)(2,1)} %get-tuple-element.100.text_ref) | copy-start | bytes 4718596
  286.0 7.4 %copy-start.8 = (bf16[130,1536]{1,0:T(8,128)(2,1)S(1)}, bf16[130,1536]{1,0:T(8,128)(2,1)}, u32[]{:S(2)}) copy-start(bf16[130,1536]{1,0:T(8,128)(2,1)} %get-tuple-element.177) | copy-start | bytes 1198084
  286.0 7.4 %copy-start.9 = (bf16[130,1536]{1,0:T(8,128)(2,1)S(1)}, bf16[130,1536]{1,0:T(8,128)(2,1)}, u32[]{:S(2)}) copy-start(bf16[130,1536]{1,0:T(8,128)(2,1)} %get-tuple-element.178) | copy-start | bytes 1198084
  292.1 4.1 collective-permute-start.2
  296.2 0.7 copy-start.16
  296.9 9.5 %copy-start.31 = (s32[118]{0:T(128)S(1)}, s32[118]{0:T(128)}, u32[]{:S(2)}) copy-start(s32[118]{0:T(128)} %get-tuple-element.194) | copy-start | bytes 1420
  303.8 18.6 %collective-permute-start.3 = (bf16[272,1536]{1,0:T(8,128)(2,1)}, bf16[272,1536]{1,0:T(8,128)(2,1)S(1)}, u32[]{:S(2)}, u32[]{:S(2)}) collective-permute-start(bf16[272,1536]{1,0:T(8,128)(2,1)} %get-tuple-element.115.part_ref), channel_id=1, source_target_pairs={{0,8},{2,10},{4,12},{6,14},{8,0},{10,2},{12,4},{14,6},{16,24},{18,... | collective-permute-start | bytes 2506760 | tf_op jit(solution)/shard_map/ppermute | solution.py:111
  322.4 0.9 copy-start.11
  342.4 17.1 %collective-permute-start.4 = (bf16[272,1536]{1,0:T(8,128)(2,1)}, bf16[272,1536]{1,0:T(8,128)(2,1)S(1)}, u32[]{:S(2)}, u32[]{:S(2)}) collective-permute-start(bf16[272,1536]{1,0:T(8,128)(2,1)} %get-tuple-element.122.part_ref.da2), channel_id=1, source_target_pairs={{0,8},{2,10},{4,12},{6,14},{8,0},{10,2},{12,4},{14,6},{16,24},{18,... | collective-permute-start | bytes 2506760 | tf_op jit(solution)/shard_map/ppermute | solution.py:111
  359.5 0.9 copy-start.10
  360.4 13.5 %copy-start.33 = (s32[9]{0:T(128)S(1)}, s32[9]{0:T(128)}, u32[]{:S(2)}) copy-start(s32[9]{0:T(128)} %copy-done.32) | copy-start | bytes 112
  373.4 4.1 collective-permute-start.5
  377.5 0.6 copy-start.20
  378.2 10.0 %copy-start.27 = (f32[1,1536]{1,0:T(1,128)S(1)}, f32[1,1536]{1,0:T(1,128)}, u32[]{:S(2)}) copy-start(f32[1,1536]{1,0:T(1,128)} %get-tuple-element.183) | copy-start | bytes 18436
  378.2 10.0 %copy-start.28 = (f32[1,1536]{1,0:T(1,128)S(1)}, f32[1,1536]{1,0:T(1,128)}, u32[]{:S(2)}) copy-start(f32[1,1536]{1,0:T(1,128)} %get-tuple-element.184) | copy-start | bytes 18436
  378.2 10.7 %copy-start.29 = (f32[1,4480]{1,0:T(1,128)S(1)}, f32[1,4480]{1,0:T(1,128)}, u32[]{:S(2)}) copy-start(f32[1,4480]{1,0:T(1,128)} %get-tuple-element.160) | copy-start | bytes 53764
  384.6 4.4 copy-start.5
  384.6 15.0 %collective-permute-start.6 = (bf16[272,1536]{1,0:T(8,128)(2,1)}, bf16[272,1536]{1,0:T(8,128)(2,1)S(1)}, u32[]{:S(2)}, u32[]{:S(2)}) collective-permute-start(bf16[272,1536]{1,0:T(8,128)(2,1)} %get-tuple-element.133.da3.part_ref), channel_id=1, source_target_pairs={{0,8},{2,10},{4,12},{6,14},{8,0},{10,2},{12,4},{14,6},{16,24},{18,... | collective-permute-start | bytes 2506760 | tf_op jit(solution)/shard_map/ppermute | solution.py:111
  390.8 7.1 copy-start.26
  399.6 0.9 copy-start.13
  415.1 4.4 collective-permute-start.7
  419.5 0.7 copy-start.21
  420.1 10.8 %slice-start = ((f32[11,1536]{1,0:T(8,128)}), f32[3,1536]{1,0:T(4,128)S(1)}, s32[]{:S(2)}) async-start(f32[11,1536]{1,0:T(8,128)} %shard_map.259), calls=%async_computation | async-start | bytes 49152 | tf_op jit(solution)/shard_map/slice | solution.py:2054
  701.4 4.1 copy-start.17
  701.4 5.0 copy-start.7
  701.4 5.0 copy-start.22
  701.4 5.0 copy-start.23
  703.3 3.9 copy-start.3
  707.2 17.2 %copy-start.19 = (f32[1,12160]{1,0:T(1,128)S(1)}, f32[1,12160]{1,0:T(1,128)}, u32[]{:S(2)}) copy-start(f32[1,12160]{1,0:T(1,128)} %param.27) | copy-start | bytes 145924
  707.2 17.2 %copy-start.24 = (f32[1,12160]{1,0:T(1,128)S(1)}, f32[1,12160]{1,0:T(1,128)}, u32[]{:S(2)}) copy-start(f32[1,12160]{1,0:T(1,128)} %param.28) | copy-start | bytes 145924
  707.2 17.2 %copy-start.25 = (f32[1,12160]{1,0:T(1,128)S(1)}, f32[1,12160]{1,0:T(1,128)}, u32[]{:S(2)}) copy-start(f32[1,12160]{1,0:T(1,128)} %param.29) | copy-start | bytes 145924
  707.2 18.2 %copy-start.1 = (f32[16,6,1536]{2,0,1:T(8,128)S(1)}, f32[16,6,1536]{2,0,1:T(8,128)}, u32[]{:S(2)}) copy-start(f32[16,6,1536]{2,0,1:T(8,128)} %param.23) | copy-start | bytes 1769476

commit v6 on v5

--- a/solution.py
+++ b/solution.py
@@ -818,14 +818,14 @@
             def _():
                 vec_copy(i).start()
 
+        @pl.when(step + 2 < turns)
+        def _():
+            for_sibling(step + 2, 0, 4)
+
         @pl.when(step + 1 < turns)
         def _():
             corner(step + 1)
             direct_sides(step + 1)
-
-        @pl.when(step + 2 < turns)
-        def _():
-            for_sibling(step + 2, 0, 4)
 
         @pl.when(step < turns)
         def _():

time: 737 us -> 746 us (1.012)
    pallas_call x1, Pallas kernels: 269 us -> 277 us  [reduce_slots(): pl.pallas_call(reduce_kernel, out_shape=[pltpu.HBM((2, slot_count, width,...]
where the time goes in v6:
time: 746 us; the launch traced here: 733 us
  Pallas kernels  649 us (87%)
  local copies, waits for them, and re-layouts  44.7 us (6%)
  other arithmetic  14.3 us (2%)
  waiting for transfers between devices  14 us (2%)
  starting transfers between devices  7.78 us (1%)
    pallas_call x1, Pallas kernels, reduce_slots(): pl.pallas_call(reduce_kernel, out_shape=[pltpu.HBM((2, slot_count, width,...  277 us
    pallas_call x1, Pallas kernels, gather_slots(): pl.pallas_call(gather_kernel, out_shape=[pltpu.HBM((16,) + scaled.shape,...  226 us
    pallas_call x13, Pallas kernels, call(): pl.pallas_call(body, grid_spec=pltpu.PrefetchScalarGridSpec(num_scalar_pr...  129 us
    pallas_call x1, Pallas kernels, adam_slots(): pl.pallas_call(step, in_specs=[scalars, scalars] + [ANY] * 4, out_specs=[...  17.1 us
  transfers between devices with their start and end apart: 8, of which 6 were waited for; matrix products, arithmetic and copies ran while one was open for 4% of the time, Pallas kernels for 5%

profile of v6, /device:TPU:9, one launch (start us, length us, event | category | flops | bytes accessed | tf_op | source)
XLA Modules:
  0.0 733.4 jit_solution(13075770976014997998)
XLA Ops:
  0.7 0.9 convert_reduce_fusion
  1.6 1.2 iota_add_fusion.1
  2.8 1.0 pad.48.lat
  3.8 1.0 pad.49.cot
  6.0 3.7 fusion.own
  9.8 226.4 %shard_map.248 = (bf16[16,9,1536,128]{3,2,1,0:T(8,128)(2,1)}, bf16[2,144,1536]{2,1,0:T(8,128)(2,1)}, bf16[2,144,1536]{2,1,0:T(8,128)(2,1)}, bf16[512,1536]{1,0:T...) custom-call(bf16[9,1536,128]{2,1,0:T(8,128)(2,1)S(1)} %fusion.own, ...), custom_call_target="tpu_custom_call" | custom-call | tf_op jit(solution)/shard_map/pallas_call | solution.py:480
  236.2 0.8 slice.93
  237.7 1.2 slice_bitcast_fusion.3
  240.1 1.4 fusion.6.rows_ref.refs_17_
  241.5 1.0 fusion.16
  243.1 8.6 %shard_map.249 = (bf16[272,1536]{1,0:T(8,128)(2,1)}, f32[2,272,768]{2,1,0:T(8,128)}, bf16[272,768]{1,0:T(8,128)(2,1)}, f32[272,128]{1,0:T(8,128)}) custom-call(s32[118]{0:T(128)S(1)} %get-tuple-element.195._.where, f32[272,1536]{1,0:T(8,128)} %fusion.6.rows_ref.refs_17_, f32[6,1536]{1,0:T(8,128)} %bitcast_add_fusion.mod_ref, f32[10,768]{1,0:T(8,128)} %reshape.198.vec_ref, ...), custom_call_target="tpu_custom_call" | custom-call | tf_op jit(solution)/shard_map/pallas_call | solution.py:1221
  251.7 1.8 collective-permute-start
  256.1 1.3 collective-permute-done.other_ref.sqo_ref
  258.1 8.3 %shard_map.250 = (bf16[272,768]{1,0:T(8,128)(2,1)}, bf16[272,768]{1,0:T(8,128)(2,1)}, bf16[6,272,128]{2,1,0:T(8,128)(2,1)}, bf16[272,1536]{1,0:T(8,128)(2,1)}) custom-call(s32[118]{0:T(128)S(1)} %get-tuple-element.195._.where, f32[2,272,768]{2,1,0:T(8,128)} %get-tuple-element.94.pre_ref, bf16[272,768]{1,0:T(8,128)(2,1)} %get-tuple-element.95.value_ref.v_ref, ...), custom_call_target="tpu_custom_call" | custom-call | tf_op jit(solution)/shard_map/pallas_call | solution.py:1221
  266.4 1.5 collective-permute-start.1
  268.6 1.2 pad_bitcast_fusion.5.refs_0_
  270.0 0.9 slice_bitcast_fusion.1
  271.0 8.0 %shard_map.251 = (f32[512,768]{1,0:T(8,128)}, bf16[512,768]{1,0:T(8,128)(2,1)}, f32[512,128]{1,0:T(8,128)}) custom-call(s32[118]{0:T(128)S(1)} %get-tuple-element.195._.where, bf16[512,1536]{1,0:T(8,128)(2,1)} %get-tuple-element.100.text_ref, f32[10,768]{1,0:T(8,128)} %reshape.198.vec_ref, bf16[144,1536,128]{2,1,0:T(8,128)(2,1)} %bitcast.63, ...), custom_call_target="tpu_custom_call" | custom-call | tf_op jit(solution)/shard_map/pallas_call | solution.py:1221
  279.0 1.7 copy.48
  280.7 5.3 collective-permute-done.1.other_ref
  286.0 6.1 shard_map.252
  292.1 1.3 collective-permute-start.2
  293.4 1.4 fusion.8.cot_ref
  294.8 1.4 collective-permute-done.2.other_ref.sqo_ref
  296.9 6.9 shard_map.253
  303.8 1.3 collective-permute-start.3
  306.5 10.2 %shard_map.254 = (bf16[272,1536]{1,0:T(8,128)(2,1)}, bf16[272,4480]{1,0:T(8,128)(2,1)}) custom-call(s32[118]{0:T(128)S(1)} %get-tuple-element.195._.where, bf16[144,1536,128]{2,1,0:T(8,128)(2,1)} %bitcast.81, f32[6,1536]{1,0:T(8,128)} %bitcast_add_fusion.mod_ref, f32[272,1536]{1,0:T(8,128)} %fusion.8.cot_ref), custom_call_target="tpu_custom_call" | custom-call | tf_op jit(solution)/shard_map/pallas_call | solution.py:1221
  316.7 1.6 copy.51
  318.4 1.6 copy.50
  320.0 1.2 pad_bitcast_fusion.3.refs_6_
  321.2 1.2 pad_bitcast_fusion.4.refs_2_
  322.4 0.9 copy-done.11
  323.2 19.1 %shard_map.255 = (f32[272,1536]{1,0:T(8,128)}, bf16[272,1536]{1,0:T(8,128)(2,1)}, bf16[35,272,128]{2,1,0:T(8,128)(2,1)}, bf16[35,272,128]{2,1,0:T(8,128)(2,1)}, ...) custom-call(s32[118]{0:T(128)S(1)} %get-tuple-element.195._.where, bf16[144,1536,128]{2,1,0:T(8,128)(2,1)} %bitcast.82, ...), custom_call_target="tpu_custom_call" | custom-call | tf_op jit(solution)/shard_map/pallas_call | solution.py:1221
  343.2 1.5 fusion.27
  344.7 1.6 copy.52
  346.3 11.0 %shard_map.256.y3.refs_20_ = bf16[272,1536]{1,0:T(8,128)(2,1)} custom-call(s32[118]{0:T(128)S(1)} %get-tuple-element.195._.where, bf16[144,1536,128]{2,1,0:T(8,128)(2,1)} %bitcast.83, bf16[35,272,128]{2,1,0:T(8,128)(2,1)} %get-tuple-element.123.hidden_ref.refs_16_), custom_call_target="tpu_custom_call" | custom-call | tf_op jit(solution)/shard_map/pallas_call | solution.py:1221
  357.4 1.2 pad_bitcast_fusion.2.refs_5_
  358.6 0.9 collective-permute-done.4.other_ref
  359.5 0.9 copy-done.10
  360.4 13.1 %shard_map.257 = (f32[272,1536]{1,0:T(8,128)}, bf16[272,1536]{1,0:T(8,128)(2,1)}, f32[272,768]{1,0:T(8,128)}, f32[512,768]{1,0:T(8,128)}, bf16[6,512,128]{2,1,0:T(8,128)(2,1)}, /*index=5*/f32[272,128]{1,0:T(8,128)}) custom-call(s32[118]{0:T(128)S(1)} %get-tuple-element.195._.where, f32[272,1536]{1,0:T(8,128)} %fusion.8.cot_ref, ...), custom_call_target="tpu_custom_call" | custom-call | tf_op jit(solution)/shard_map/pallas_call | solution.py:1221
  374.0 3.5 collective-permute-done.5.sumo_ref
  378.2 6.4 shard_map.258
  385.1 0.8 slice.102
  386.1 2.1 gather_fusion
  389.7 1.2 pad_bitcast_fusion.1.refs_4_
  390.8 7.1 shard_map.259
  398.0 1.6 collective-permute-done.6.other_ref
  399.6 0.8 slice.106
  400.5 14.6 %shard_map.260 = (f32[272,1536]{1,0:T(8,128)}, bf16[272,1536]{1,0:T(8,128)(2,1)}, f32[2,272,768]{2,1,0:T(8,128)}, bf16[6,272,128]{2,1,0:T(8,128)(2,1)}, f32[272,128]{1,0:T(8,128)}, /*index=5*/f32[2,1536]{1,0:T(2,128)}) custom-call(s32[118]{0:T(128)S(1)} %get-tuple-element.195._.where, f32[272,1536]{1,0:T(8,128)} %get-tuple-element.128.dx_in, ...), custom_call_target="tpu_custom_call" | custom-call | tf_op jit(solution)/shard_map/pallas_call | solution.py:1221
  415.1 0.8 collective-permute-start.7
  415.9 0.8 fusion.28
  416.7 1.6 copy.54
  418.3 1.1 pad_bitcast_fusion.refs_1_
  420.1 9.8 %shard_map.261 = (bf16[6,272,128]{2,1,0:T(8,128)(2,1)}, bf16[6,272,128]{2,1,0:T(8,128)(2,1)}, f32[8,768]{1,0:T(8,128)}, bf16[272,1536]{1,0:T(8,128)(2,1)}, f32[2,1536]{1,0:T(2,128)}) custom-call(s32[118]{0:T(128)S(1)} %get-tuple-element.195._.where, f32[272,1536]{1,0:T(8,128)} %fusion.6.rows_ref.refs_17_, f32[2,272,768]{2,1,0:T(8,128)} %get-tuple-element.94.pre_ref, ...), custom_call_target="tpu_custom_call" | custom-call | tf_op jit(solution)/shard_map/pallas_call | solution.py:1221
  429.9 0.7 reshape.201
  430.9 0.8 concatenate.30
  432.4 276.6 %shard_map.262 = (bf16[2,9,1536,128]{3,2,1,0:T(8,128)(2,1)}, f32[328,128]{1,0:T(8,128)}, bf16[272,1536]{1,0:T(8,128)(2,1)}, f32[272,1536]{1,0:T(8,128)}, bf16[27...) custom-call(s32[144]{0:T(256)} %gather_fusion, ...), custom_call_target="tpu_custom_call" | custom-call | tf_op jit(solution)/shard_map/pallas_call | solution.py:958
  709.0 1.0 slice.110
  710.0 0.9 slice.109
  710.9 2.2 constant_dynamic-slice_fusion
  713.1 0.9 constant_dynamic-slice_fusion.1
  714.0 0.7 multiply_subtract_fusion
  714.8 17.1 %shard_map.263 = (f32[1,9,1536,128]{3,2,1,0:T(8,128)}, f32[1,9,1536,128]{3,2,1,0:T(8,128)}, f32[1,9,1536,128]{3,2,1,0:T(8,128)}) custom-call(f32[9]{0:T(128)S(1)} %copy-done.3, s32[9]{0:T(128)S(1)} %convert_element_type.56.fill_ref, bf16[2,9,1536,128]{3,2,1,0:T(8,128)(2,1)} %get-tuple-element.166.grads, f32[1,9,1536,128]{3,2,1,0:T(8,128)} %weight.1, ...), custom_call_target="tpu_custom_call" | custom-call | tf_op jit(solution)/shard_map/pallas_call | solution.py:1114
  732.0 1.0 multiply_subtract_fusion.1
  (124 shorter events, 15.3 us)
Async XLA Ops:
  0.6 240.9 %copy-start = (f32[16,6,1536]{2,0,1:T(8,128)S(1)}, f32[16,6,1536]{2,0,1:T(8,128)}, u32[]{:S(2)}) copy-start(f32[16,6,1536]{2,0,1:T(8,128)} %param.23) | copy-start | bytes 1769476
  0.7 4.2 copy-start.30
  0.7 5.0 copy-start.18
  2.8 7.0 copy-start.32
  6.0 3.8 copy-start.2
  238.9 3.6 copy-start.6
  251.7 5.8 collective-permute-start
  257.5 0.6 copy-start.15
  258.1 9.8 %copy-start.12 = (bf16[272,1536]{1,0:T(8,128)(2,1)S(1)}, bf16[272,1536]{1,0:T(8,128)(2,1)}, u32[]{:S(2)}) copy-start(bf16[272,1536]{1,0:T(8,128)(2,1)} %get-tuple-element.102) | copy-start | bytes 2506756
  266.4 19.6 %collective-permute-start.1 = (bf16[272,1536]{1,0:T(8,128)(2,1)}, bf16[272,1536]{1,0:T(8,128)(2,1)}, u32[]{:S(2)}, u32[]{:S(2)}) collective-permute-start(bf16[272,1536]{1,0:T(8,128)(2,1)} %get-tuple-element.99.part_ref), channel_id=1, source_target_pairs={{0,8},{2,10},{4,12},{6,14},{8,0},{10,2},{12,4},{14,6},{16,24},{18,... | collective-permute-start | bytes 2506760 | tf_op jit(solution)/shard_map/ppermute | solution.py:111
  268.6 1.5 copy-start.14
  271.0 8.0 %copy-start.4 = (bf16[512,1536]{1,0:T(8,128)(2,1)S(1)}, bf16[512,1536]{1,0:T(8,128)(2,1)}, u32[]{:S(2)}) copy-start(bf16[512,1536]{1,0:T(8,128)(2,1)} %get-tuple-element.100.text_ref) | copy-start | bytes 4718596
  286.0 7.4 %copy-start.8 = (bf16[130,1536]{1,0:T(8,128)(2,1)S(1)}, bf16[130,1536]{1,0:T(8,128)(2,1)}, u32[]{:S(2)}) copy-start(bf16[130,1536]{1,0:T(8,128)(2,1)} %get-tuple-element.177) | copy-start | bytes 1198084
  286.0 7.4 %copy-start.9 = (bf16[130,1536]{1,0:T(8,128)(2,1)S(1)}, bf16[130,1536]{1,0:T(8,128)(2,1)}, u32[]{:S(2)}) copy-start(bf16[130,1536]{1,0:T(8,128)(2,1)} %get-tuple-element.178) | copy-start | bytes 1198084
  292.1 4.1 collective-permute-start.2
  296.2 0.7 copy-start.16
  296.9 9.5 %copy-start.31 = (s32[118]{0:T(128)S(1)}, s32[118]{0:T(128)}, u32[]{:S(2)}) copy-start(s32[118]{0:T(128)} %get-tuple-element.194) | copy-start | bytes 1420
  303.8 18.6 %collective-permute-start.3 = (bf16[272,1536]{1,0:T(8,128)(2,1)}, bf16[272,1536]{1,0:T(8,128)(2,1)S(1)}, u32[]{:S(2)}, u32[]{:S(2)}) collective-permute-start(bf16[272,1536]{1,0:T(8,128)(2,1)} %get-tuple-element.115.part_ref), channel_id=1, source_target_pairs={{0,8},{2,10},{4,12},{6,14},{8,0},{10,2},{12,4},{14,6},{16,24},{18,... | collective-permute-start | bytes 2506760 | tf_op jit(solution)/shard_map/ppermute | solution.py:111
  322.4 0.9 copy-start.11
  342.4 17.1 %collective-permute-start.4 = (bf16[272,1536]{1,0:T(8,128)(2,1)}, bf16[272,1536]{1,0:T(8,128)(2,1)S(1)}, u32[]{:S(2)}, u32[]{:S(2)}) collective-permute-start(bf16[272,1536]{1,0:T(8,128)(2,1)} %get-tuple-element.122.part_ref.da2), channel_id=1, source_target_pairs={{0,8},{2,10},{4,12},{6,14},{8,0},{10,2},{12,4},{14,6},{16,24},{18,... | collective-permute-start | bytes 2506760 | tf_op jit(solution)/shard_map/ppermute | solution.py:111
  359.5 0.9 copy-start.10
  360.4 13.5 %copy-start.33 = (s32[9]{0:T(128)S(1)}, s32[9]{0:T(128)}, u32[]{:S(2)}) copy-start(s32[9]{0:T(128)} %copy-done.32) | copy-start | bytes 112
  373.4 4.1 collective-permute-start.5
  377.5 0.6 copy-start.20
  378.2 10.0 %copy-start.27 = (f32[1,1536]{1,0:T(1,128)S(1)}, f32[1,1536]{1,0:T(1,128)}, u32[]{:S(2)}) copy-start(f32[1,1536]{1,0:T(1,128)} %get-tuple-element.183) | copy-start | bytes 18436
  378.2 10.0 %copy-start.28 = (f32[1,1536]{1,0:T(1,128)S(1)}, f32[1,1536]{1,0:T(1,128)}, u32[]{:S(2)}) copy-start(f32[1,1536]{1,0:T(1,128)} %get-tuple-element.184) | copy-start | bytes 18436
  378.2 10.7 %copy-start.29 = (f32[1,4480]{1,0:T(1,128)S(1)}, f32[1,4480]{1,0:T(1,128)}, u32[]{:S(2)}) copy-start(f32[1,4480]{1,0:T(1,128)} %get-tuple-element.160) | copy-start | bytes 53764
  384.6 4.4 copy-start.5
  384.6 15.0 %collective-permute-start.6 = (bf16[272,1536]{1,0:T(8,128)(2,1)}, bf16[272,1536]{1,0:T(8,128)(2,1)S(1)}, u32[]{:S(2)}, u32[]{:S(2)}) collective-permute-start(bf16[272,1536]{1,0:T(8,128)(2,1)} %get-tuple-element.133.da3.part_ref), channel_id=1, source_target_pairs={{0,8},{2,10},{4,12},{6,14},{8,0},{10,2},{12,4},{14,6},{16,24},{18,... | collective-permute-start | bytes 2506760 | tf_op jit(solution)/shard_map/ppermute | solution.py:111
  390.8 7.1 copy-start.26
  399.6 0.9 copy-start.13
  415.1 4.4 collective-permute-start.7
  419.5 0.7 copy-start.21
  420.1 10.8 %slice-start = ((f32[11,1536]{1,0:T(8,128)}), f32[3,1536]{1,0:T(4,128)S(1)}, s32[]{:S(2)}) async-start(f32[11,1536]{1,0:T(8,128)} %shard_map.259), calls=%async_computation | async-start | bytes 49152 | tf_op jit(solution)/shard_map/slice | solution.py:2054
  709.0 4.1 copy-start.17
  709.0 5.0 copy-start.7
  709.0 5.0 copy-start.22
  709.0 5.0 copy-start.23
  710.9 3.9 copy-start.3
  714.8 17.2 %copy-start.19 = (f32[1,12160]{1,0:T(1,128)S(1)}, f32[1,12160]{1,0:T(1,128)}, u32[]{:S(2)}) copy-start(f32[1,12160]{1,0:T(1,128)} %param.27) | copy-start | bytes 145924
  714.8 17.2 %copy-start.24 = (f32[1,12160]{1,0:T(1,128)S(1)}, f32[1,12160]{1,0:T(1,128)}, u32[]{:S(2)}) copy-start(f32[1,12160]{1,0:T(1,128)} %param.28) | copy-start | bytes 145924
  714.8 17.2 %copy-start.25 = (f32[1,12160]{1,0:T(1,128)S(1)}, f32[1,12160]{1,0:T(1,128)}, u32[]{:S(2)}) copy-start(f32[1,12160]{1,0:T(1,128)} %param.29) | copy-start | bytes 145924
  714.8 18.2 %copy-start.1 = (f32[16,6,1536]{2,0,1:T(8,128)S(1)}, f32[16,6,1536]{2,0,1:T(8,128)}, u32[]{:S(2)}) copy-start(f32[16,6,1536]{2,0,1:T(8,128)} %param.23) | copy-start | bytes 1769476
